TPU v7x, 32 devices: a whole 2x2x4 slice. The times are simulated.
32 devices in a mesh: dp: 8 (over y, x, core), seq: 4 (over z).
Axes of the slice: x: 2, y: 2, z: 4, core: 2. Of those that a mesh axis runs over, the one named last changes fastest.
Arguments:
- tokens: bfloat16 [16384, 1024], P(('dp', 'seq')), may hold values from -6 to 6
- patches: bfloat16 [8192, 1024], P(('dp', 'seq')), may hold values from -6 to 6
- cameras: bfloat16 [32, 16], P('dp'), may hold values from -4 to 4
- tri_items: int32 [16384], P('dp'), may hold values from 0 to 3, as said below
- patch_items: int32 [8192], P('dp'), may hold values from 0 to 3, as said below
- mod_weight: bfloat16 [2048, 16], P(('dp', 'seq')), may hold values from -0.75 to 0.75
- qkv_weight: bfloat16 [1024, 3072], P(('dp', 'seq')), may hold values from -0.1875 to 0.1875
- self_out_weight: bfloat16 [1024, 1024], P(('dp', 'seq')), may hold values from -3 to 3
- norm2_gain: bfloat16 [1024], P(('dp', 'seq')), may hold values from 0.5 to 1.5
- norm2_bias: bfloat16 [1024], P(('dp', 'seq')), may hold values from -3 to 3
- cross_q_weight: bfloat16 [1024, 1024], P(('dp', 'seq')), may hold values from -0.1875 to 0.1875
- cross_kv_weight: bfloat16 [1024, 2048], P(('dp', 'seq')), may hold values from -0.1875 to 0.1875
- cross_out_weight: bfloat16 [1024, 1024], P(('dp', 'seq')), may hold values from -3 to 3
- norm3_gain: bfloat16 [1024], P(('dp', 'seq')), may hold values from 0.5 to 1.5
- norm3_bias: bfloat16 [1024], P(('dp', 'seq')), may hold values from -3 to 3
- mlp_in_weight: bfloat16 [1024, 4096], P(('dp', 'seq')), may hold values from -0.1875 to 0.1875
- mlp_in_bias: bfloat16 [4096], P(('dp', 'seq')), may hold values from -3 to 3
- mlp_out_weight: bfloat16 [4096, 1024], P(('dp', 'seq')), may hold values from -0.09375 to 0.09375
- mlp_out_bias: bfloat16 [1024], P(('dp', 'seq')), may hold values from -3 to 3
- cotangent: bfloat16 [16384, 1024], P(('dp', 'seq')), may hold values from -6 to 6
Outputs:
- block_out: bfloat16 [16384, 1024], P(('dp', 'seq'))
- input_grad: float32 [16384, 1024], P(('dp', 'seq'))
- patch_grad: float32 [8192, 1024], P(('dp', 'seq'))
- mod_weight_grad: float32 [2048, 16], P(('dp', 'seq'))
- qkv_weight_grad: float32 [1024, 3072], P(('dp', 'seq'))
- self_out_weight_grad: float32 [1024, 1024], P(('dp', 'seq'))
- norm2_gain_grad: float32 [1024], P(('dp', 'seq'))
- norm2_bias_grad: float32 [1024], P(('dp', 'seq'))
- cross_q_weight_grad: float32 [1024, 1024], P(('dp', 'seq'))
- cross_kv_weight_grad: float32 [1024, 2048], P(('dp', 'seq'))
- cross_out_weight_grad: float32 [1024, 1024], P(('dp', 'seq'))
- norm3_gain_grad: float32 [1024], P(('dp', 'seq'))
- norm3_bias_grad: float32 [1024], P(('dp', 'seq'))
- mlp_in_weight_grad: float32 [1024, 4096], P(('dp', 'seq'))
- mlp_in_bias_grad: float32 [4096], P(('dp', 'seq'))
- mlp_out_weight_grad: float32 [4096, 1024], P(('dp', 'seq'))
- mlp_out_bias_grad: float32 [1024], P(('dp', 'seq'))
Inputs may be any that keep to these rules, and one draw needn't show every extreme that they name: `tri_items`: within each group item numbers never fall along the rows, every item has tokens, and one item of each group, drawn from the seed, runs from the group's first 512 rows into its last 512 rows. `patch_items`: within each group item numbers never fall along the rows and every item has patches.
All inputs are finite; a program needn't handle non-finite values.
Results may differ from a plain program's by a relative error of at most 0.017.
Values may be sent and summed in bfloat16 or wider, within the bound.
No kernel may reach another device: no remote copies, remote signals or barrier semaphores. Data moves between devices by JAX's collectives and lax.ppermute only.
A program may use at most 320 MiB of HBM per device.

v0:
```python
import math

import jax
import jax.numpy as jnp
from jax import lax
from jax.sharding import PartitionSpec as P

HEADS = 16


def product(left_side, right_side):
    return jnp.dot(left_side, right_side, preferred_element_type=jnp.float32)


def product_t(left_side, right_side):
    return lax.dot_general(
        left_side, right_side, (((1,), (1,)), ((), ())), preferred_element_type=jnp.float32
    )


def contract_rows(left_side, right_side):
    return lax.dot_general(
        left_side, right_side, (((0,), (0,)), ((), ())), preferred_element_type=jnp.float32
    )


def normed(values):
    centre = values - jnp.mean(values, axis=-1, keepdims=True)
    spread = jnp.mean(centre * centre, axis=-1, keepdims=True)
    return centre * lax.rsqrt(spread + 1e-05)


def modulated(values, shift_vec, scale_vec):
    return normed(values) * (1.0 + scale_vec) + shift_vec


def affine_norm(values, gain_vec, bias_vec):
    return normed(values) * gain_vec + bias_vec


def gelu_exact(hidden_in):
    return jax.nn.gelu(hidden_in, approximate=False)


def split_heads(tensor):
    head_dim = tensor.shape[1] // HEADS
    return tensor.reshape(tensor.shape[0], HEADS, head_dim).transpose(1, 0, 2)


def merge_heads(tensor):
    return tensor.transpose(1, 0, 2).reshape(tensor.shape[1], tensor.shape[0] * tensor.shape[2])


def attend_forward(queries, key_rows, values, allowed):
    score_scale = 1.0 / math.sqrt(queries.shape[1] // HEADS)

    def attend_per_head(unused, pieces):
        head_q, head_k, head_v = pieces
        scores = jnp.where(allowed, product_t(head_q, head_k) * score_scale, -1e30)
        row_max = jnp.max(scores, axis=1, keepdims=True)
        exponent = jnp.exp(scores - row_max)
        row_total = jnp.sum(exponent, axis=1, keepdims=True)
        probs_low = (exponent / row_total).astype(jnp.bfloat16)
        return (unused, (product(probs_low, head_v), row_max + jnp.log(row_total)))

    unused, (outputs, log_total) = lax.scan(
        attend_per_head,
        jnp.zeros((), jnp.float32),
        (split_heads(queries), split_heads(key_rows), split_heads(values)),
    )
    return (merge_heads(outputs), log_total)


def attention_reverse_pass(queries, key_rows, values, allowed, log_total, grad_out):
    score_scale = 1.0 / math.sqrt(queries.shape[1] // HEADS)

    def attention_per_head(unused, pieces):
        head_q, head_k, head_v, head_lse, head_grad = pieces
        scores = jnp.where(allowed, product_t(head_q, head_k) * score_scale, -1e30)
        probs_full = jnp.exp(scores - head_lse)
        grad_prob = product_t(head_grad, head_v)
        row_delta = jnp.sum(probs_full * grad_prob, axis=1, keepdims=True)
        grad_score = (probs_full * (grad_prob - row_delta)).astype(jnp.bfloat16)
        grad_query = product(grad_score, head_k) * score_scale
        grad_key = contract_rows(grad_score, head_q) * score_scale
        grad_value = contract_rows(probs_full.astype(jnp.bfloat16), head_grad)
        return (unused, (grad_query, grad_key, grad_value, row_delta))

    unused, (grad_queries, grad_keys, grad_values, deltas) = lax.scan(
        attention_per_head,
        jnp.zeros((), jnp.float32),
        (
            split_heads(queries),
            split_heads(key_rows),
            split_heads(values),
            log_total,
            split_heads(grad_out),
        ),
    )
    return (merge_heads(grad_queries), merge_heads(grad_keys), merge_heads(grad_values), deltas)


def shards(
    tokens,
    patches,
    cameras,
    tri_items,
    patch_items,
    mod_weight,
    qkv_weight,
    self_out_weight,
    norm2_gain,
    norm2_bias,
    cross_q_weight,
    cross_kv_weight,
    cross_out_weight,
    norm3_gain,
    norm3_bias,
    mlp_in_weight,
    mlp_in_bias,
    mlp_out_weight,
    mlp_out_bias,
    cotangent,
):
    gathered = (
        lax.all_gather(mod_weight, ("dp", "seq"), axis=0, tiled=True),
        lax.all_gather(qkv_weight, ("dp", "seq"), axis=0, tiled=True),
        lax.all_gather(self_out_weight, ("dp", "seq"), axis=0, tiled=True),
        lax.all_gather(norm2_gain, ("dp", "seq"), axis=0, tiled=True),
        lax.all_gather(norm2_bias, ("dp", "seq"), axis=0, tiled=True),
        lax.all_gather(cross_q_weight, ("dp", "seq"), axis=0, tiled=True),
        lax.all_gather(cross_kv_weight, ("dp", "seq"), axis=0, tiled=True),
        lax.all_gather(cross_out_weight, ("dp", "seq"), axis=0, tiled=True),
        lax.all_gather(norm3_gain, ("dp", "seq"), axis=0, tiled=True),
        lax.all_gather(norm3_bias, ("dp", "seq"), axis=0, tiled=True),
        lax.all_gather(mlp_in_weight, ("dp", "seq"), axis=0, tiled=True),
        lax.all_gather(mlp_in_bias, ("dp", "seq"), axis=0, tiled=True),
        lax.all_gather(mlp_out_weight, ("dp", "seq"), axis=0, tiled=True),
        lax.all_gather(mlp_out_bias, ("dp", "seq"), axis=0, tiled=True),
    )
    (
        mod_full,
        qkv_full,
        self_out_full,
        gain_two,
        bias_two,
        cross_q_full,
        cross_kv_full,
        cross_out_full,
        gain_three,
        bias_three,
        in_full,
        in_bias_full,
        out_full,
        out_bias_full,
    ) = gathered
    row_count = tokens.shape[0]
    width = tokens.shape[1]
    my_items = lax.dynamic_slice_in_dim(tri_items, lax.axis_index("seq") * row_count, row_count)
    item_range = jnp.arange(cameras.shape[0], dtype=jnp.int32)
    onehot = (my_items[:, None] == item_range[None, :]).astype(jnp.float32)
    cam_float = cameras.astype(jnp.float32)
    mod_items = product_t(cameras, mod_full)
    mod_tok = jnp.dot(onehot, mod_items, precision=lax.Precision.HIGHEST)
    shift_tok = mod_tok[:, :width]
    scale_tok = mod_tok[:, width:]
    resid_in = tokens.astype(jnp.float32)
    act_one = modulated(resid_in, shift_tok, scale_tok).astype(jnp.bfloat16)
    qkv_low = product(act_one, qkv_full).astype(jnp.bfloat16)
    self_q = qkv_low[:, :width]
    own_keys = qkv_low[:, width : 2 * width]
    own_values = qkv_low[:, 2 * width :]
    key_all, value_all = (
        lax.all_gather(own_keys, "seq", axis=0, tiled=True),
        lax.all_gather(own_values, "seq", axis=0, tiled=True),
    )
    self_mask = my_items[:, None] == tri_items[None, :]
    self_att, self_lse = attend_forward(self_q, key_all, value_all, self_mask)
    self_att_low = self_att.astype(jnp.bfloat16)
    resid_two = resid_in + product(self_att_low, self_out_full)
    act_two = affine_norm(
        resid_two, gain_two.astype(jnp.float32), bias_two.astype(jnp.float32)
    ).astype(jnp.bfloat16)
    cross_q = product(act_two, cross_q_full).astype(jnp.bfloat16)
    cross_kv = product(patches, cross_kv_full).astype(jnp.bfloat16)
    ckey_all, cvalue_all = (
        lax.all_gather(cross_kv[:, :width], "seq", axis=0, tiled=True),
        lax.all_gather(cross_kv[:, width:], "seq", axis=0, tiled=True),
    )
    cross_mask = my_items[:, None] == patch_items[None, :]
    cross_att, cross_lse = attend_forward(cross_q, ckey_all, cvalue_all, cross_mask)
    cross_att_low = cross_att.astype(jnp.bfloat16)
    resid_three = resid_two + product(cross_att_low, cross_out_full)
    act_three = affine_norm(
        resid_three, gain_three.astype(jnp.float32), bias_three.astype(jnp.float32)
    ).astype(jnp.bfloat16)
    hidden_pre = product(act_three, in_full) + in_bias_full.astype(jnp.float32)
    hidden_low = gelu_exact(hidden_pre).astype(jnp.bfloat16)
    block_out = resid_three + product(hidden_low, out_full) + out_bias_full.astype(jnp.float32)
    regathered = (
        lax.all_gather(mod_weight, ("dp", "seq"), axis=0, tiled=True),
        lax.all_gather(qkv_weight, ("dp", "seq"), axis=0, tiled=True),
        lax.all_gather(self_out_weight, ("dp", "seq"), axis=0, tiled=True),
        lax.all_gather(norm2_gain, ("dp", "seq"), axis=0, tiled=True),
        lax.all_gather(norm2_bias, ("dp", "seq"), axis=0, tiled=True),
        lax.all_gather(cross_q_weight, ("dp", "seq"), axis=0, tiled=True),
        lax.all_gather(cross_kv_weight, ("dp", "seq"), axis=0, tiled=True),
        lax.all_gather(cross_out_weight, ("dp", "seq"), axis=0, tiled=True),
        lax.all_gather(norm3_gain, ("dp", "seq"), axis=0, tiled=True),
        lax.all_gather(norm3_bias, ("dp", "seq"), axis=0, tiled=True),
        lax.all_gather(mlp_in_weight, ("dp", "seq"), axis=0, tiled=True),
        lax.all_gather(mlp_in_bias, ("dp", "seq"), axis=0, tiled=True),
        lax.all_gather(mlp_out_weight, ("dp", "seq"), axis=0, tiled=True),
        lax.all_gather(mlp_out_bias, ("dp", "seq"), axis=0, tiled=True),
    )
    (
        mod_full,
        qkv_full,
        self_out_full,
        gain_two,
        bias_two,
        cross_q_full,
        cross_kv_full,
        cross_out_full,
        gain_three,
        bias_three,
        in_full,
        in_bias_full,
        out_full,
        out_bias_full,
    ) = regathered
    grad_out = cotangent.astype(jnp.float32)
    grad_out_bias = jnp.sum(grad_out, axis=0)
    grad_out_weight = contract_rows(hidden_low, cotangent)
    grad_hidden = product_t(cotangent, out_full)
    gelu_value, gelu_pull = jax.vjp(gelu_exact, hidden_pre)
    grad_pre_low = gelu_pull(grad_hidden)[0].astype(jnp.bfloat16)
    grad_in_bias = jnp.sum(grad_pre_low.astype(jnp.float32), axis=0)
    grad_in_weight = contract_rows(act_three, grad_pre_low)
    grad_act_three = product_t(grad_pre_low, in_full)
    norm_value, norm_pull = jax.vjp(
        affine_norm, resid_three, gain_three.astype(jnp.float32), bias_three.astype(jnp.float32)
    )
    grad_resid_three, grad_gain_three, grad_bias_three = norm_pull(grad_act_three)
    grad_resid_three = grad_resid_three + grad_out
    grad_cross_low = grad_resid_three.astype(jnp.bfloat16)
    grad_cross_out = contract_rows(cross_att_low, grad_cross_low)
    grad_cross_att = product_t(grad_cross_low, cross_out_full).astype(jnp.bfloat16)
    grad_cq, grad_ckey, grad_cvalue, cross_delta = attention_reverse_pass(
        cross_q, ckey_all, cvalue_all, cross_mask, cross_lse, grad_cross_att
    )
    ckey_sum, cvalue_sum = (
        lax.psum_scatter(
            grad_ckey.astype(jnp.bfloat16), "seq", scatter_dimension=0, tiled=True
        ).astype(jnp.float32),
        lax.psum_scatter(
            grad_cvalue.astype(jnp.bfloat16), "seq", scatter_dimension=0, tiled=True
        ).astype(jnp.float32),
    )
    grad_ckv_low = jnp.concatenate([ckey_sum, cvalue_sum], axis=1).astype(jnp.bfloat16)
    grad_cross_kv = contract_rows(patches, grad_ckv_low)
    patch_grad = product_t(grad_ckv_low, cross_kv_full)
    grad_cq_low = grad_cq.astype(jnp.bfloat16)
    grad_cross_q = contract_rows(act_two, grad_cq_low)
    grad_act_two = product_t(grad_cq_low, cross_q_full)
    norm_value, norm_pull = jax.vjp(
        affine_norm, resid_two, gain_two.astype(jnp.float32), bias_two.astype(jnp.float32)
    )
    grad_resid_two, grad_gain_two, grad_bias_two = norm_pull(grad_act_two)
    grad_resid_two = grad_resid_two + grad_resid_three
    grad_self_low = grad_resid_two.astype(jnp.bfloat16)
    grad_self_out = contract_rows(self_att_low, grad_self_low)
    grad_self_att = product_t(grad_self_low, self_out_full).astype(jnp.bfloat16)
    self_query_gradient, self_key_gradient, self_value_gradient, self_attention_delta = (
        attention_reverse_pass(self_q, key_all, value_all, self_mask, self_lse, grad_self_att)
    )
    self_key_total, self_value_total = (
        lax.psum_scatter(
            self_key_gradient.astype(jnp.bfloat16), "seq", scatter_dimension=0, tiled=True
        ).astype(jnp.float32),
        lax.psum_scatter(
            self_value_gradient.astype(jnp.bfloat16), "seq", scatter_dimension=0, tiled=True
        ).astype(jnp.float32),
    )
    query_key_value_gradient_reduced = jnp.concatenate(
        [self_query_gradient, self_key_total, self_value_total], axis=1
    ).astype(jnp.bfloat16)
    grad_qkv = contract_rows(act_one, query_key_value_gradient_reduced)
    grad_act_one = product_t(query_key_value_gradient_reduced, qkv_full)
    norm_value, mod_pull = jax.vjp(modulated, resid_in, shift_tok, scale_tok)
    grad_resid_in, grad_shift, grad_scale = mod_pull(grad_act_one)
    input_grad = grad_resid_in + grad_resid_two
    grad_mod_tok = jnp.concatenate([grad_shift, grad_scale], axis=1)
    grad_mod_items = lax.dot_general(
        onehot, grad_mod_tok, (((0,), (0,)), ((), ())), precision=lax.Precision.HIGHEST
    )
    grad_mod = lax.dot_general(
        grad_mod_items, cam_float, (((0,), (0,)), ((), ())), precision=lax.Precision.HIGHEST
    )
    summed = (
        lax.psum_scatter(grad_mod, ("dp", "seq"), scatter_dimension=0, tiled=True),
        lax.psum_scatter(grad_qkv, ("dp", "seq"), scatter_dimension=0, tiled=True),
        lax.psum_scatter(grad_self_out, ("dp", "seq"), scatter_dimension=0, tiled=True),
        lax.psum_scatter(grad_gain_two, ("dp", "seq"), scatter_dimension=0, tiled=True),
        lax.psum_scatter(grad_bias_two, ("dp", "seq"), scatter_dimension=0, tiled=True),
        lax.psum_scatter(grad_cross_q, ("dp", "seq"), scatter_dimension=0, tiled=True),
        lax.psum_scatter(grad_cross_kv, ("dp", "seq"), scatter_dimension=0, tiled=True),
        lax.psum_scatter(grad_cross_out, ("dp", "seq"), scatter_dimension=0, tiled=True),
        lax.psum_scatter(grad_gain_three, ("dp", "seq"), scatter_dimension=0, tiled=True),
        lax.psum_scatter(grad_bias_three, ("dp", "seq"), scatter_dimension=0, tiled=True),
        lax.psum_scatter(grad_in_weight, ("dp", "seq"), scatter_dimension=0, tiled=True),
        lax.psum_scatter(grad_in_bias, ("dp", "seq"), scatter_dimension=0, tiled=True),
        lax.psum_scatter(grad_out_weight, ("dp", "seq"), scatter_dimension=0, tiled=True),
        lax.psum_scatter(grad_out_bias, ("dp", "seq"), scatter_dimension=0, tiled=True),
    )
    return (block_out.astype(jnp.bfloat16), input_grad, patch_grad) + tuple(summed)


def solution(mesh):
    placed = (
        P(("dp", "seq"), None),
        P(("dp", "seq"), None),
        P("dp", None),
        P("dp"),
        P("dp"),
        P(("dp", "seq"), None),
        P(("dp", "seq"), None),
        P(("dp", "seq"), None),
        P(("dp", "seq")),
        P(("dp", "seq")),
        P(("dp", "seq"), None),
        P(("dp", "seq"), None),
        P(("dp", "seq"), None),
        P(("dp", "seq")),
        P(("dp", "seq")),
        P(("dp", "seq"), None),
        P(("dp", "seq")),
        P(("dp", "seq"), None),
        P(("dp", "seq")),
        P(("dp", "seq"), None),
    )
    return jax.shard_map(
        shards,
        mesh=mesh,
        in_specs=placed,
        out_specs=(
            P(("dp", "seq"), None),
            P(("dp", "seq"), None),
            P(("dp", "seq"), None),
            P(("dp", "seq"), None),
            P(("dp", "seq"), None),
            P(("dp", "seq"), None),
            P(("dp", "seq")),
            P(("dp", "seq")),
            P(("dp", "seq"), None),
            P(("dp", "seq"), None),
            P(("dp", "seq"), None),
            P(("dp", "seq")),
            P(("dp", "seq")),
            P(("dp", "seq"), None),
            P(("dp", "seq")),
            P(("dp", "seq"), None),
            P(("dp", "seq")),
        ),
        check_vma=False,
    )
```

profile of v0, /device:TPU:0, one launch (start us, length us, event | category | flops | bytes accessed | tf_op | source)
XLA Modules:
  0.0 3031.2 jit_solution(11519780610486699341)
XLA Ops:
  8.7 67.1 %all-gather.24.cloned.1.call-done = bf16[1024,2048]{1,0:T(8,128)(2,1)} async-done(((bf16[32,2048]{1,0:T(8,128)(2,1)}), bf16[1024,2048]{1,0:T(8,128)(2,1)}) %all-gather.24.cloned.1.call-update) | async-done | bytes 4194320 | tf_op jit(solution)/shard_map/all_gather | solution.py:132
  81.1 68.2 %all-gather = bf16[32,64,16]{1,2,0:T(8,128)(2,1)S(1)} all-gather(bf16[1,64,16]{1,2,0:T(8,128)(2,1)S(1)} %bitcast.308), channel_id=1, replica_groups=mesh['dp'=8,'seq'=4] {'dp','seq'}, dimensions={0}, use_global_device_ids=true | all-gather | bytes 67584 | tf_op jit(solution)/shard_map/all_gather | solution.py:126
  169.5 39.0 %all-reduce.12 = (bf16[1024]{0:T(1024)(128)(2,1)S(1)}, bf16[1024]{0:T(1024)(128)(2,1)S(1)}, bf16[1024]{0:T(1024)(128)(2,1)S(1)}, bf16[1024]{0:T(1024)(128)(2,1)S(1)}, bf16[1024]{0:T(1024)(128)(2,1)}) all-reduce(bf16[1024]{0:T(1024)(128)(2,1)S(1)} %dynamic-update-slice.1, ...), channel_id=1, replica_groups=mesh['dp'=8,'seq'=4] {'dp','seq'}, use_global_device_ids=true, to_apply=%add.1 | all-reduce | flops 5120 | bytes 20480
  208.6 66.2 %all-gather.1 = bf16[32,1,128]{2,1,0:T(2,128)(2,1)S(1)} all-gather(bf16[1,1,128]{2,1,0:T(2,128)(2,1)S(1)} %bitcast.309), channel_id=1, replica_groups=mesh['dp'=8,'seq'=4] {'dp','seq'}, dimensions={0}, use_global_device_ids=true | all-gather | bytes 8448 | tf_op jit(solution)/shard_map/all_gather | solution.py:137
  295.6 27.3 all-gather.16.cloned.1.call-done
  337.9 66.3 %all-gather.18.cloned.1.call-done = bf16[2048,1024]{1,0:T(8,128)(2,1)} async-done(((bf16[512,1024]{1,0:T(8,128)(2,1)}), bf16[2048,1024]{1,0:T(8,128)(2,1)}) %all-gather.18.cloned.1.call-update) | async-done | bytes 4194320 | tf_op jit(solution)/shard_map/all_gather | solution.py:175
  419.3 77.6 %while.56 = (s32[]{:T(128)}, bf16[16,512,64]{1,2,0:T(8,128)(2,1)S(1)}, f32[16,512,1]{1,2,0:T(1,128)S(1)}, bf16[16,512,64]{2,1,0:T(8,128)(2,1)}, bf16[16,2048,64]...) while((s32[]{:T(128)}, ...), condition=%wide.region_5.6_spmd.clone, body=%wide.region_2.5_spmd.clone.sunk | while | flops 277872128 | bytes 13926505 | solution.py:66
  502.1 18.6 all-gather.22.cloned.1.call-done
  527.7 69.5 %while.57 = (s32[]{:T(128)}, bf16[16,512,64]{1,2,0:T(8,128)(2,1)}, f32[16,512,1]{1,2,0:T(1,128)S(1)}, bf16[16,512,64]{2,1,0:T(8,128)(2,1)}, bf16[16,1024,64]{2,1...) while((s32[]{:T(128)}, bf16[16,512,64]{1,2,0:T(8,128)(2,1)}, ...), condition=%wide.region_11.12_spmd.clone, body=%wide.region_8.11_spmd.clone.sunk | while | flops 138935808 | bytes 7106665 | solution.py:66
  602.2 56.1 %all-gather.32.cloned.1.call-done = bf16[1024,4096]{1,0:T(8,128)(2,1)} async-done(((bf16[32,4096]{1,0:T(8,128)(2,1)}), bf16[1024,4096]{1,0:T(8,128)(2,1)}) %all-gather.32.cloned.1.call-update) | async-done | bytes 8388624 | tf_op jit(solution)/shard_map/all_gather | solution.py:136
  658.3 11.9 fusion.121
  670.2 67.0 %all-gather.34.cloned.1.call-done = bf16[4096,1024]{1,0:T(8,128)(2,1)} async-done(((bf16[128,1024]{1,0:T(8,128)(2,1)}), bf16[4096,1024]{1,0:T(8,128)(2,1)}) %all-gather.34.cloned.1.call-update) | async-done | bytes 8388624 | tf_op jit(solution)/shard_map/all_gather | solution.py:138
  737.2 28.7 convert_reduce_fusion
  783.1 149.8 %while.58 = (s32[]{:T(128)}, bf16[16,512,64]{1,2,0:T(8,128)(2,1)}, bf16[16,1024,64]{1,2,0:T(8,128)(2,1)}, bf16[16,1024,64]{1,2,0:T(8,128)(2,1)}, bf16[16,512,64]...) while((s32[]{:T(128)}, bf16[16,512,64]{1,2,0:T(8,128)(2,1)}, ...), condition=%wide.region_18.19_spmd.clone, body=%wide.region_16.18_spmd.clone.sunk | while | flops 340884992 | bytes 17585280 | solution.py:89
  942.5 171.8 %while.59 = (s32[]{:T(128)}, bf16[16,512,64]{1,2,0:T(8,128)(2,1)S(1)}, bf16[16,2048,64]{1,2,0:T(8,128)(2,1)}, bf16[16,2048,64]{1,2,0:T(8,128)(2,1)}, bf16[16,512...) while((s32[]{:T(128)}, ...), condition=%wide.region_23.24_spmd.clone, body=%wide.region_21.23_spmd.clone.sunk | while | flops 681737728 | bytes 34628736 | solution.py:89
  1116.4 73.6 %reduce-scatter.19.cloned.1.call-done = bf16[512,1024]{0,1:T(8,128)(2,1)} async-done(((bf16[2048,1024]{0,1:T(8,128)(2,1)}), bf16[512,1024]{0,1:T(8,128)(2,1)}) %reduce-scatter.19.cloned.1.call-update) | async-done | bytes 1048592 | tf_op jit(solution)/shard_map/reduce_scatter | solution.py:281
  1189.9 79.7 %reduce-scatter.17.cloned.1.call-done = bf16[512,1024]{0,1:T(8,128)(2,1)} async-done(((bf16[2048,1024]{0,1:T(8,128)(2,1)}), bf16[512,1024]{0,1:T(8,128)(2,1)}) %reduce-scatter.17.cloned.1.call-update) | async-done | bytes 1048592 | tf_op jit(solution)/shard_map/reduce_scatter | solution.py:278
  1299.5 16.6 reduce-scatter.21.cloned.1.call-done
  1317.3 44.4 %reduce-scatter.23.cloned.1.call-done = bf16[256,1024]{0,1:T(8,128)(2,1)} async-done(((bf16[1024,1024]{0,1:T(8,128)(2,1)}), bf16[256,1024]{0,1:T(8,128)(2,1)}) %reduce-scatter.23.cloned.1.call-update) | async-done | bytes 524304 | tf_op jit(solution)/shard_map/reduce_scatter | solution.py:256
  1387.5 10.5 fusion.120
  1398.7 9.9 multiply_convert_fusion.2
  1408.6 10.5 fusion.136
  1419.8 40.3 %all-reduce.11 = (f32[1024]{0:T(1024)S(1)}, f32[1024]{0:T(1024)S(1)}, f32[1024]{0:T(1024)S(1)}, f32[1024]{0:T(1024)S(1)}, f32[4096]{0:T(1024)S(1)}, /*index=5*/f32[1024]{0:T(1024)S(1)}) all-reduce(f32[1024]{0:T(1024)S(1)} %get-tuple-element.432, ...), channel_id=9, replica_groups=mesh['dp'=8,'seq'=4] {'dp','seq'}, use_global_device_ids=true, to_apply=%region_34.35.clone | all-reduce | flops 9216 | bytes 73728
  1463.6 10.3 add_convert_fusion.1
  1477.8 20.7 reduce-scatter.37.cloned.1.call-done
  1499.9 145.9 %reduce-scatter.27.cloned.1.call-done = f32[32,1024]{1,0:T(8,128)} async-done(((f32[1024,1024]{1,0:T(8,128)}), f32[32,1024]{1,0:T(8,128)}) %reduce-scatter.27.cloned.1.call-update) | async-done | bytes 131088 | tf_op jit(solution)/shard_map/reduce_scatter | solution.py:303
  1645.9 149.5 %reduce-scatter.29.cloned.1.call-done = f32[32,1024]{1,0:T(8,128)} async-done(((f32[1024,1024]{1,0:T(8,128)}), f32[32,1024]{1,0:T(8,128)}) %reduce-scatter.29.cloned.1.call-update) | async-done | bytes 131088 | tf_op jit(solution)/shard_map/reduce_scatter | solution.py:306
  1795.4 149.1 %reduce-scatter.31.cloned.1.call-done = f32[32,1024]{1,0:T(8,128)} async-done(((f32[1024,1024]{1,0:T(8,128)}), f32[32,1024]{1,0:T(8,128)}) %reduce-scatter.31.cloned.1.call-update) | async-done | bytes 131088 | tf_op jit(solution)/shard_map/reduce_scatter | solution.py:308
  1944.5 187.4 %reduce-scatter.39.cloned.1.call-done = f32[32,2048]{1,0:T(8,128)} async-done(((f32[1024,2048]{1,0:T(8,128)}), f32[32,2048]{1,0:T(8,128)}) %reduce-scatter.39.cloned.1.call-update) | async-done | bytes 262160
  2131.9 161.1 %reduce-scatter.25.cloned.1.call-done = f32[32,3072]{1,0:T(8,128)} async-done(((f32[1024,3072]{1,0:T(8,128)}), f32[32,3072]{1,0:T(8,128)}) %reduce-scatter.25.cloned.1.call-update) | async-done | bytes 393232 | tf_op jit(solution)/shard_map/reduce_scatter | solution.py:302
  2293.0 366.2 %reduce-scatter.33.cloned.1.call-done = f32[32,4096]{1,0:T(8,128)} async-done(((f32[1024,4096]{1,0:T(8,128)}), f32[32,4096]{1,0:T(8,128)}) %reduce-scatter.33.cloned.1.call-update) | async-done | bytes 524304 | tf_op jit(solution)/shard_map/reduce_scatter | solution.py:311
  2659.2 365.1 %reduce-scatter.35.cloned.1.call-done = f32[128,1024]{1,0:T(8,128)} async-done(((f32[4096,1024]{1,0:T(8,128)}), f32[128,1024]{1,0:T(8,128)}) %reduce-scatter.35.cloned.1.call-update) | async-done | bytes 524304 | tf_op jit(solution)/shard_map/reduce_scatter | solution.py:313
  (675 shorter events, 657.3 us)
Async XLA Ops:
  7.2 68.7 %all-gather.24.cloned.1.call-start = ((), (), s32[]{:S(2)}) async-start(), calls=%async_computation.17 | async-start | bytes 4325376 | tf_op jit(solution)/shard_map/all_gather | solution.py:132
  7.9 147.4 %all-gather.14.cloned.1.call-start = ((), (), s32[]{:S(2)}) async-start(), calls=%async_computation.12 | async-start | bytes 6488064 | tf_op jit(solution)/shard_map/all_gather | solution.py:127
  8.7 266.1 %all-gather.26.cloned.1.call-start = ((), (), s32[]{:S(2)}) async-start(), calls=%async_computation.18 | async-start | bytes 2621440 | tf_op jit(solution)/shard_map/all_gather | solution.py:187
  80.4 203.1 %all-gather.28.cloned.1.call-start = ((), (), s32[]{:S(2)}) async-start(), calls=%async_computation.19 | async-start | bytes 2621440 | tf_op jit(solution)/shard_map/all_gather | solution.py:188
  81.0 241.9 %all-gather.16.cloned.1.call-start = ((), (), s32[]{:S(2)}) async-start(), calls=%async_computation.13 | async-start | bytes 5242880 | tf_op jit(solution)/shard_map/all_gather | solution.py:174
  164.1 240.1 %all-gather.18.cloned.1.call-start = ((), (), s32[]{:S(2)}) async-start(), calls=%async_computation.14 | async-start | bytes 5242880 | tf_op jit(solution)/shard_map/all_gather | solution.py:175
  164.7 332.3 %all-gather.20.cloned.1.call-start = ((), (), s32[]{:S(2)}) async-start(), calls=%async_computation.15 | async-start | bytes 2162688 | tf_op jit(solution)/shard_map/all_gather | solution.py:128
  165.4 355.2 %all-gather.22.cloned.1.call-start = ((), (), s32[]{:S(2)}) async-start(), calls=%async_computation.16 | async-start | bytes 2162688 | tf_op jit(solution)/shard_map/all_gather | solution.py:131
  166.2 431.0 %all-gather.30.cloned.1.call-start = ((), (), s32[]{:S(2)}) async-start(), calls=%async_computation.20 | async-start | bytes 2162688 | tf_op jit(solution)/shard_map/all_gather | solution.py:133
  166.9 491.4 %all-gather.32.cloned.1.call-start = ((), (), s32[]{:S(2)}) async-start(), calls=%async_computation.21 | async-start | bytes 8650752 | tf_op jit(solution)/shard_map/all_gather | solution.py:136
  167.5 569.7 %all-gather.34.cloned.1.call-start = ((), (), s32[]{:S(2)}) async-start(), calls=%async_computation.22 | async-start | bytes 8650752 | tf_op jit(solution)/shard_map/all_gather | solution.py:138
  168.2 1021.7 %reduce-scatter.19.cloned.1.call-start = ((), (), s32[]{:S(2)}) async-start(), calls=%async_computation.24 | async-start | bytes 5242880 | tf_op jit(solution)/shard_map/reduce_scatter | solution.py:281
  208.6 312.1 %copy-start.59 = (f32[1024]{0:T(1024)}, f32[1024]{0:T(1024)S(1)}, u32[]{:S(2)}) copy-start(f32[1024]{0:T(1024)S(1)} %convert_element_type.164) | copy-start | bytes 12292
  208.6 312.1 %copy-start.48 = (f32[1024]{0:T(1024)}, f32[1024]{0:T(1024)S(1)}, u32[]{:S(2)}) copy-start(f32[1024]{0:T(1024)S(1)} %convert_element_type.163) | copy-start | bytes 12292
  208.6 449.7 %copy-start.57 = (f32[1024]{0:T(1024)}, f32[1024]{0:T(1024)S(1)}, u32[]{:S(2)}) copy-start(f32[1024]{0:T(1024)S(1)} %convert_element_type.172) | copy-start | bytes 12292
  274.8 462.5 %copy-start.34 = (f32[32,1,128]{2,1,0:T(1,128)}, f32[32,1,128]{2,1,0:T(1,128)S(1)}, u32[]{:S(2)}) copy-start(f32[32,1,128]{2,1,0:T(1,128)S(1)} %convert_element_type.200) | copy-start | bytes 49156
  783.1 149.8 %copy-start.49 = (f32[1024]{0:T(1024)S(1)}, f32[1024]{0:T(1024)}, u32[]{:S(2)}) copy-start(f32[1024]{0:T(1024)} %copy-done.48) | copy-start | bytes 12292
  783.1 149.8 %copy-start.51 = (f32[512]{0:T(512)S(1)}, f32[512]{0:T(512)}, u32[]{:S(2)}) copy-start(f32[512]{0:T(512)} %copy-done.50) | copy-start | bytes 6148
  1114.4 155.2 %copy-start.24 = (bf16[16,512,64]{1,2,0:T(8,128)(2,1)}, bf16[16,512,64]{1,2,0:T(8,128)(2,1)S(1)}, u32[]{:S(2)}) copy-start(bf16[16,512,64]{1,2,0:T(8,128)(2,1)S(1)} %get-tuple-element.206) | copy-start | bytes 3145732
  1114.4 155.2 %reduce-scatter.17.cloned.1.call-start = ((), (), s32[]{:S(2)}) async-start(), calls=%async_computation.23 | async-start | bytes 5242880 | tf_op jit(solution)/shard_map/reduce_scatter | solution.py:278
  1115.2 201.0 %reduce-scatter.21.cloned.1.call-start = ((), (), s32[]{:S(2)}) async-start(), calls=%async_computation.25 | async-start | bytes 2621440 | tf_op jit(solution)/shard_map/reduce_scatter | solution.py:253
  1115.2 154.4 %copy-start.4 = (bf16[512,1024]{1,0:T(8,128)(2,1)S(1)}, bf16[512,1024]{1,0:T(8,128)(2,1)}, u32[]{:S(2)}) copy-start(bf16[512,1024]{1,0:T(8,128)(2,1)} %param.28) | copy-start | bytes 3145732
  1115.2 154.4 %copy-start.38 = (f32[512]{0:T(512)S(1)}, f32[512]{0:T(512)}, u32[]{:S(2)}) copy-start(f32[512]{0:T(512)} %copy-done.37) | copy-start | bytes 6148
  1115.8 245.9 %reduce-scatter.23.cloned.1.call-start = ((), (), s32[]{:S(2)}) async-start(), calls=%async_computation.26 | async-start | bytes 2621440 | tf_op jit(solution)/shard_map/reduce_scatter | solution.py:256
  1116.3 382.2 %reduce-scatter.37.cloned.1.call-start = ((), (), s32[]{:S(2)}) async-start(), calls=%async_computation.33 | async-start | bytes 1081344
  1283.5 362.3 %reduce-scatter.27.cloned.1.call-start = ((), (), s32[]{:S(2)}) async-start(), calls=%async_computation.28 | async-start | bytes 4325376 | tf_op jit(solution)/shard_map/reduce_scatter | solution.py:303
  1288.3 507.1 %reduce-scatter.29.cloned.1.call-start = ((), (), s32[]{:S(2)}) async-start(), calls=%async_computation.29 | async-start | bytes 4325376 | tf_op jit(solution)/shard_map/reduce_scatter | solution.py:306
  1294.7 649.8 %reduce-scatter.31.cloned.1.call-start = ((), (), s32[]{:S(2)}) async-start(), calls=%async_computation.30 | async-start | bytes 4325376 | tf_op jit(solution)/shard_map/reduce_scatter | solution.py:308
  1299.5 832.4 %reduce-scatter.39.cloned.1.call-start = ((), (), s32[]{:S(2)}) async-start(), calls=%async_computation.34 | async-start | bytes 8650752
  1376.4 916.5 %reduce-scatter.25.cloned.1.call-start = ((), (), s32[]{:S(2)}) async-start(), calls=%async_computation.27 | async-start | bytes 12976128 | tf_op jit(solution)/shard_map/reduce_scatter | solution.py:302
  1385.9 1273.3 %reduce-scatter.33.cloned.1.call-start = ((), (), s32[]{:S(2)}) async-start(), calls=%async_computation.31 | async-start | bytes 17301504 | tf_op jit(solution)/shard_map/reduce_scatter | solution.py:311
  1398.0 1626.3 %reduce-scatter.35.cloned.1.call-start = ((), (), s32[]{:S(2)}) async-start(), calls=%async_computation.32 | async-start | bytes 17301504 | tf_op jit(solution)/shard_map/reduce_scatter | solution.py:313
  (62 other events, 821.4 us)
Sparse Core Ops, SparseCore 0:
  11.0 64.7 all-gather.23
  78.7 68.4 all-gather.13
  149.4 45.0 all-gather.25
  196.5 44.7 all-gather.27
  243.3 79.5 all-gather.15
  324.9 79.3 all-gather.17
  407.2 55.1 all-gather.19
  465.3 55.3 all-gather.21
  523.6 55.3 all-gather.29
  581.8 76.4 all-gather.31
  661.2 75.9 all-gather.33
  1114.5 75.3 reduce-scatter.18
  1192.3 77.2 reduce-scatter.16
  1271.8 44.3 reduce-scatter.20
  1318.4 43.1 reduce-scatter.22
  1363.7 134.7 reduce-scatter.36
  1501.3 144.5 reduce-scatter.26
  1648.7 146.6 reduce-scatter.28
  1798.4 146.0 reduce-scatter.30
  1947.3 184.5 reduce-scatter.38
  2139.6 153.3 reduce-scatter.24
  2295.9 363.2 reduce-scatter.32
  2662.1 362.1 reduce-scatter.34
where the time goes:
time: 3050 us; the launch traced here: 3030 us
  waiting for transfers between devices  2070 us (68%)
  matrix products  574 us (19%)
  blocking collectives  214 us (7%)
  local copies, waits for them, and re-layouts  107 us (4%)
  other arithmetic  48.6 us (2%)
    reduce_scatter x1, waiting for transfers between devices, shards(): lax.psum_scatter(grad_in_weight, ('dp', 'seq'), scatter_dimension=0, tile...  366 us
    reduce_scatter x1, waiting for transfers between devices, shards(): lax.psum_scatter(grad_out_weight, ('dp', 'seq'), scatter_dimension=0, til...  365 us
    dot_general x104, matrix products, product_t(): lax.dot_general(left_side, right_side, (((1,), (1,)), ((), ())), preferre...  236 us
    unnamed x25, waiting for transfers between devices  216 us
    dot_general x71, matrix products, product(): return jnp.dot(left_side, right_side, preferred_element_type=jnp.float32)  174 us
    reduce_scatter x1, waiting for transfers between devices, shards(): lax.psum_scatter(grad_qkv, ('dp', 'seq'), scatter_dimension=0, tiled=True)  161 us
    dot_general x71, matrix products, contract_rows(): lax.dot_general(left_side, right_side, (((0,), (0,)), ((), ())), preferre...  159 us
    reduce_scatter x1, waiting for transfers between devices, shards(): lax.psum_scatter(grad_cross_q, ('dp', 'seq'), scatter_dimension=0, tiled=...  150 us
  transfers between devices with their start and end apart: 23, of which 18 were waited for; matrix products, arithmetic and copies ran while one was open for 11% of the time, Pallas kernels for 0%

commit v1 on v0

v1 whole, which is shorter than its diff:
```python
import math

import jax
import jax.numpy as jnp
from jax import lax
from jax.experimental import pallas as pl
from jax.experimental.pallas import tpu as pltpu
from jax.sharding import PartitionSpec as P

HEADS = 16
HEAD = 64
PAIR = 2 * HEAD
BF = jnp.bfloat16
F32 = jnp.float32
LOG2E = math.log2(math.e)
ALL = ("dp", "seq")
NEG = -1e30
VMEM_LIMIT = 48 * 1024 * 1024


def product(a, b):
    return jnp.dot(a, b, preferred_element_type=F32)


def product_t(a, b):
    return lax.dot_general(a, b, (((1,), (1,)), ((), ())), preferred_element_type=F32)


def contract_rows(a, b):
    return lax.dot_general(a, b, (((0,), (0,)), ((), ())), preferred_element_type=F32)


def head_masks(rows):
    lane = lax.broadcasted_iota(jnp.int32, (rows, PAIR), 1)
    return (lane < HEAD, lane >= HEAD)


def only_head(value, h):
    mask = head_masks(value.shape[0])[h]
    return jnp.where(mask, value, jnp.zeros_like(value))


def block_kinds(qs_ref, ks_ref, i, j, qb, kb):
    q_first, q_last = qs_ref[i * qb], qs_ref[i * qb + qb - 1]
    k_first, k_last = ks_ref[j * kb], ks_ref[j * kb + kb - 1]
    live = jnp.logical_and(k_first <= q_last, k_last >= q_first)
    plain = jnp.logical_and(
        jnp.logical_and(q_first == q_last, k_first == k_last), q_first == k_first
    )
    return jnp.logical_and(live, jnp.logical_not(plain)), plain


def attend_kernel(qs_ref, ks_ref, q_ref, k_ref, v_ref, qid_ref, kid_ref, o_ref, lse_ref, vt_ref, m_ref, l_ref, acc_ref, *, kb):
    i = pl.program_id(1)
    qb = q_ref.shape[0]
    nk = k_ref.shape[0]
    scale = LOG2E / math.sqrt(HEAD)

    @pl.when(i == 0)
    def _():
        vt_ref[...] = v_ref[...].T

    m_ref[...] = jnp.full(m_ref.shape, NEG, F32)
    l_ref[...] = jnp.zeros(l_ref.shape, F32)
    acc_ref[...] = jnp.zeros(acc_ref.shape, F32)

    def step(j, masked):
        keys = k_ref[j * kb : (j + 1) * kb, :]
        if masked:
            allowed = kid_ref[j * kb : (j + 1) * kb, :] == qid_ref[...]
        for h in range(2):
            scores = product_t(keys, only_head(q_ref[...], h))
            if masked:
                scores = jnp.where(allowed, scores, NEG)
            m_old = m_ref[h : h + 1, :]
            m_new = jnp.maximum(m_old, jnp.max(scores, axis=0, keepdims=True))
            probs = jnp.exp2((scores - m_new) * scale)
            alpha = jnp.exp2((m_old - m_new) * scale)
            m_ref[h : h + 1, :] = m_new
            l_ref[h : h + 1, :] = l_ref[h : h + 1, :] * alpha + jnp.sum(probs, axis=0, keepdims=True)
            rows = slice(h * HEAD, (h + 1) * HEAD)
            acc_ref[rows, :] = acc_ref[rows, :] * alpha + product(
                vt_ref[rows, j * kb : (j + 1) * kb], probs.astype(BF)
            )

    for j in range(nk // kb):
        mixed, plain = block_kinds(qs_ref, ks_ref, i, j, qb, kb)
        pl.when(mixed)(lambda j=j: step(j, True))
        pl.when(plain)(lambda j=j: step(j, False))

    total = l_ref[0:2, :]
    lse_ref[0] = m_ref[0:2, :] * scale + jnp.log2(total)
    inverse = 1.0 / total
    out_t = jnp.concatenate(
        [acc_ref[0:HEAD, :] * inverse[0:1, :], acc_ref[HEAD:PAIR, :] * inverse[1:2, :]], axis=0
    )
    o_ref[...] = out_t.T.astype(BF)


def attend(q, k, v, offsets, heads, q_ids, k_ids):
    nq, nk = q.shape[0], k.shape[0]
    pairs = heads // 2
    qb, kb = min(256, nq), min(512, nk)
    q_off, k_off, v_off = offsets
    smem = pl.BlockSpec(memory_space=pltpu.SMEM)
    return pl.pallas_call(
        lambda *refs: attend_kernel(*refs, kb=kb),
        grid=(pairs, nq // qb),
        in_specs=[
            smem,
            smem,
            pl.BlockSpec((qb, PAIR), lambda p, i: (i, q_off + p)),
            pl.BlockSpec((nk, PAIR), lambda p, i: (0, k_off + p)),
            pl.BlockSpec((nk, PAIR), lambda p, i: (0, v_off + p)),
            pl.BlockSpec((1, qb), lambda p, i: (0, i)),
            pl.BlockSpec((nk, 1), lambda p, i: (0, 0)),
        ],
        out_specs=[
            pl.BlockSpec((qb, PAIR), lambda p, i: (i, p)),
            pl.BlockSpec((1, 2, qb), lambda p, i: (p, 0, i)),
        ],
        out_shape=[
            jax.ShapeDtypeStruct((nq, pairs * PAIR), BF),
            jax.ShapeDtypeStruct((pairs, 2, nq), F32),
        ],
        scratch_shapes=[
            pltpu.VMEM((PAIR, nk), BF),
            pltpu.VMEM((8, qb), F32),
            pltpu.VMEM((8, qb), F32),
            pltpu.VMEM((PAIR, qb), F32),
        ],
        compiler_params=pltpu.CompilerParams(vmem_limit_bytes=VMEM_LIMIT),
        cost_estimate=pl.CostEstimate(
            flops=8 * 2 * nq * nk * HEAD * heads, bytes_accessed=2 * heads * HEAD * (2 * nq + 2 * nk), transcendentals=nq * nk * heads
        ),
        name="attend",
    )(q_ids, k_ids, q, k, v, q_ids.reshape(1, nq), k_ids.reshape(nk, 1))


def attend_back_kernel(qs_ref, ks_ref, q_ref, k_ref, v_ref, do_ref, o_ref, lse_ref, qid_ref, kid_ref, dq_ref, dk_ref, dv_ref, kt_ref, dqt_ref, dk_acc, dv_acc, *, kb):
    i = pl.program_id(1)
    qb = q_ref.shape[0]
    nk = k_ref.shape[0]
    scale = LOG2E / math.sqrt(HEAD)

    @pl.when(i == 0)
    def _():
        kt_ref[...] = k_ref[...].T
        dk_acc[...] = jnp.zeros(dk_acc.shape, F32)
        dv_acc[...] = jnp.zeros(dv_acc.shape, F32)

    dqt_ref[...] = jnp.zeros(dqt_ref.shape, F32)
    both = (do_ref[...].astype(F32) * o_ref[...].astype(F32)).T
    deltas = (
        jnp.sum(both[0:HEAD, :], axis=0, keepdims=True),
        jnp.sum(both[HEAD:PAIR, :], axis=0, keepdims=True),
    )

    def step(j, masked):
        keys = k_ref[j * kb : (j + 1) * kb, :]
        values = v_ref[j * kb : (j + 1) * kb, :]
        if masked:
            allowed = kid_ref[j * kb : (j + 1) * kb, :] == qid_ref[...]
        for h in range(2):
            q_h = only_head(q_ref[...], h)
            do_h = only_head(do_ref[...], h)
            scores = product_t(keys, q_h)
            probs = jnp.exp2(scores * scale - lse_ref[0, h : h + 1, :])
            if masked:
                probs = jnp.where(allowed, probs, 0.0)
            grad_probs = product_t(values, do_h)
            grad_scores = (probs * (grad_probs - deltas[h])).astype(BF)
            dv_acc[j * kb : (j + 1) * kb, :] += product(probs.astype(BF), do_h)
            dk_acc[j * kb : (j + 1) * kb, :] += product(grad_scores, q_h)
            rows = slice(h * HEAD, (h + 1) * HEAD)
            dqt_ref[rows, :] += product(kt_ref[rows, j * kb : (j + 1) * kb], grad_scores)

    for j in range(nk // kb):
        mixed, plain = block_kinds(qs_ref, ks_ref, i, j, qb, kb)
        pl.when(mixed)(lambda j=j: step(j, True))
        pl.when(plain)(lambda j=j: step(j, False))

    dq_ref[...] = (dqt_ref[...] * (1.0 / math.sqrt(HEAD))).T.astype(BF)

    @pl.when(i == pl.num_programs(1) - 1)
    def _():
        dk_ref[...] = (dk_acc[...] * (1.0 / math.sqrt(HEAD))).astype(BF)
        dv_ref[...] = dv_acc[...].astype(BF)


def attend_back(q, k, v, offsets, heads, q_ids, k_ids, out, lse, grad_out):
    nq, nk = q.shape[0], k.shape[0]
    pairs = heads // 2
    qb, kb = min(256, nq), min(512, nk)
    q_off, k_off, v_off = offsets
    smem = pl.BlockSpec(memory_space=pltpu.SMEM)
    return pl.pallas_call(
        lambda *refs: attend_back_kernel(*refs, kb=kb),
        grid=(pairs, nq // qb),
        in_specs=[
            smem,
            smem,
            pl.BlockSpec((qb, PAIR), lambda p, i: (i, q_off + p)),
            pl.BlockSpec((nk, PAIR), lambda p, i: (0, k_off + p)),
            pl.BlockSpec((nk, PAIR), lambda p, i: (0, v_off + p)),
            pl.BlockSpec((qb, PAIR), lambda p, i: (i, p)),
            pl.BlockSpec((qb, PAIR), lambda p, i: (i, p)),
            pl.BlockSpec((1, 2, qb), lambda p, i: (p, 0, i)),
            pl.BlockSpec((1, qb), lambda p, i: (0, i)),
            pl.BlockSpec((nk, 1), lambda p, i: (0, 0)),
        ],
        out_specs=[
            pl.BlockSpec((qb, PAIR), lambda p, i: (i, p)),
            pl.BlockSpec((nk, PAIR), lambda p, i: (0, p)),
            pl.BlockSpec((nk, PAIR), lambda p, i: (0, p)),
        ],
        out_shape=[
            jax.ShapeDtypeStruct((nq, pairs * PAIR), BF),
            jax.ShapeDtypeStruct((nk, pairs * PAIR), BF),
            jax.ShapeDtypeStruct((nk, pairs * PAIR), BF),
        ],
        scratch_shapes=[
            pltpu.VMEM((PAIR, nk), BF),
            pltpu.VMEM((PAIR, qb), F32),
            pltpu.VMEM((nk, PAIR), F32),
            pltpu.VMEM((nk, PAIR), F32),
        ],
        compiler_params=pltpu.CompilerParams(vmem_limit_bytes=VMEM_LIMIT),
        cost_estimate=pl.CostEstimate(
            flops=20 * 2 * nq * nk * HEAD * heads, bytes_accessed=2 * heads * HEAD * (4 * nq + 4 * nk), transcendentals=nq * nk * heads
        ),
        name="attend_back",
    )(q_ids, k_ids, q, k, v, grad_out, out, lse, q_ids.reshape(1, nq), k_ids.reshape(nk, 1))


def bits_of(size):
    return [1 << b for b in range(size.bit_length() - 1)]


def swap(value, axis, bit, size):
    return lax.ppermute(value, axis, [(r, r ^ bit) for r in range(size)])


def my_bit(axis, bit):
    return (lax.axis_index(axis) // bit) % 2


def halve(value, axis_name, bit, size, where, last=False):
    mine = my_bit(axis_name, bit)
    keep = lax.dynamic_index_in_dim(value, mine, where, keepdims=False)
    send = lax.dynamic_index_in_dim(value, 1 - mine, where, keepdims=False)
    got = swap(send, axis_name, bit, size)
    total = keep.astype(F32) + got.astype(F32)
    return total if last else total.astype(value.dtype)


def scatter_dp(half, nd, dtype=BF):
    bits = bits_of(nd)[1:]
    cols = half.shape[-1]
    parts = []
    for part, order in enumerate((bits, bits[::-1])):
        piece = half[..., part * (cols // 2) : (part + 1) * (cols // 2)]
        piece = piece.reshape((2,) * len(bits) + piece.shape[1:])
        left = bits[::-1]
        for bit in order:
            where = left.index(bit)
            piece = halve(piece, "dp", bit, nd, where)
            left = [b for b in left if b != bit]
        parts.append(piece)
    return jnp.concatenate(parts, axis=-1)


def scatter_seq(rows, ns):
    bits = bits_of(ns)
    piece = rows.reshape((2,) * len(bits) + (rows.shape[0] // ns, rows.shape[1]))
    left = bits[::-1]
    for n, bit in enumerate(bits):
        where = left.index(bit)
        piece = halve(piece, "seq", bit, ns, where, last=n == len(bits) - 1)
        left = [b for b in left if b != bit]
    return piece


def core_half(x, grad, nd):
    rows = x.shape[1] // nd
    view = x.reshape(x.shape[0], nd // 2, 2, rows)
    mine = my_bit("dp", 1)
    x_keep = lax.dynamic_index_in_dim(view, mine, 2, keepdims=False).reshape(x.shape[0], -1)
    x_send = lax.dynamic_index_in_dim(view, 1 - mine, 2, keepdims=False).reshape(x.shape[0], -1)
    got = swap(contract_rows(x_send, grad).astype(BF), "dp", 1, nd)
    total = (contract_rows(x_keep, grad) + got.astype(F32)).astype(BF)
    return total.reshape(nd // 2, rows, grad.shape[1])


def weight_grad(x, grad, nd, ns):
    return scatter_seq(scatter_dp(core_half(x, grad, nd), nd), ns)


def norm_parts(values):
    centre = values - jnp.mean(values, axis=-1, keepdims=True)
    spread = jnp.mean(centre * centre, axis=-1, keepdims=True)
    inverse = lax.rsqrt(spread + 1e-05)
    return centre * inverse, inverse


def norm_back(unit, inverse, grad):
    return inverse * (
        grad
        - jnp.mean(grad, axis=-1, keepdims=True)
        - unit * jnp.mean(grad * unit, axis=-1, keepdims=True)
    )


def per_item(ids, rows):
    out = jnp.broadcast_to(rows[0:1, :], (ids.shape[0], rows.shape[1]))
    for n in range(1, rows.shape[0]):
        out = jnp.where(ids[:, None] == n, rows[n : n + 1, :], out)
    return out


def gelu_parts(pre):
    cdf = 0.5 * (1.0 + lax.erf(pre * (1.0 / math.sqrt(2.0))))
    density = jnp.exp(-0.5 * pre * pre) * (1.0 / math.sqrt(2.0 * math.pi))
    return (pre * cdf).astype(BF), (cdf + pre * density).astype(BF)


def block(nd, ns, tokens, patches, cameras, tri_items, patch_items, mod_weight, qkv_weight, self_out_weight, norm2_gain, norm2_bias, cross_q_weight, cross_kv_weight, cross_out_weight, norm3_gain, norm3_bias, mlp_in_weight, mlp_in_bias, mlp_out_weight, mlp_out_bias, cotangent):
    rows, width = tokens.shape
    ff = mlp_in_weight.shape[1]
    heads_here = HEADS // ns
    cols_here = width // ns
    seq = lax.axis_index("seq")

    def gather(w):
        return lax.all_gather(w, ALL, axis=0, tiled=True)

    token_all = lax.all_gather(tokens, "seq", axis=0, tiled=True)
    patch_all = lax.all_gather(patches, "seq", axis=0, tiled=True)
    qkv_mine = (
        qkv_weight.reshape(qkv_weight.shape[0], 3, ns, cols_here)
        .transpose(2, 0, 1, 3)
        .reshape(ns * qkv_weight.shape[0], 3 * cols_here)
    )
    qkv_mine = lax.all_to_all(qkv_mine, "seq", 0, 0, tiled=True)
    qkv_mine = lax.all_gather(qkv_mine, "dp", axis=0, tiled=True)

    small = jnp.concatenate(
        [
            mod_weight.reshape(-1),
            norm2_gain,
            norm2_bias,
            norm3_gain,
            norm3_bias,
            mlp_out_bias,
            mlp_in_bias,
        ]
    )
    small = lax.all_gather(small.reshape(1, -1), ALL, axis=0, tiled=True)
    mod_n = mod_weight.size
    own = norm2_gain.shape[0]
    mod_full = small[:, :mod_n].reshape(-1, mod_weight.shape[1])
    vectors = [small[:, mod_n + n * own : mod_n + (n + 1) * own].reshape(1, -1).astype(F32) for n in range(5)]
    gain_two, bias_two, gain_three, bias_three, out_bias = vectors
    in_bias = small[:, mod_n + 5 * own :].reshape(1, -1).astype(F32)

    w_self_out = gather(self_out_weight)
    w_cross_kv = gather(cross_kv_weight)
    w_cross_q = gather(cross_q_weight)
    w_cross_out = gather(cross_out_weight)
    w_in = gather(mlp_in_weight)
    w_out = gather(mlp_out_weight)

    my_items = lax.dynamic_slice_in_dim(tri_items, seq * rows, rows)

    mod_items = product_t(cameras, mod_full)
    unit_one, inv_one = norm_parts(token_all.astype(F32))
    act_one = (
        unit_one * (1.0 + per_item(tri_items, mod_items[:, width:])) + per_item(tri_items, mod_items[:, :width])
    ).astype(BF)
    qkv = product(act_one, qkv_mine).astype(BF)
    pairs_here = heads_here // 2
    self_off = (0, pairs_here, 2 * pairs_here)
    self_mine, self_lse = attend(qkv, qkv, qkv, self_off, heads_here, tri_items, tri_items)
    self_att = lax.all_to_all(self_mine, "seq", 0, 1, tiled=True)
    resid_in = tokens.astype(F32)
    resid_two = resid_in + product(self_att, w_self_out)

    unit_two, inv_two = norm_parts(resid_two)
    act_two = (unit_two * gain_two + bias_two).astype(BF)
    cross_q = product(act_two, w_cross_q).astype(BF)
    cross_kv = product(patch_all, w_cross_kv).astype(BF)
    cross_off = (0, 0, HEADS // 2)
    cross_att, cross_lse = attend(cross_q, cross_kv, cross_kv, cross_off, HEADS, my_items, patch_items)
    resid_three = resid_two + product(cross_att, w_cross_out)

    unit_three, inv_three = norm_parts(resid_three)
    act_three = (unit_three * gain_three + bias_three).astype(BF)
    pre = product(act_three, w_in) + in_bias
    hid, slope = gelu_parts(pre)
    block_out = (resid_three + product(hid, w_out) + out_bias).astype(BF)

    grad_out = cotangent.astype(F32)
    g_out_bias = jnp.sum(grad_out, axis=0)
    g_w_out = weight_grad(hid, cotangent, nd, ns)
    d_pre = (product_t(cotangent, w_out) * slope.astype(F32)).astype(BF)
    g_in_bias = jnp.sum(d_pre.astype(F32), axis=0)
    d_act_three = product_t(d_pre, w_in)
    g_w_in = weight_grad(act_three, d_pre, nd, ns)
    g_gain_three = jnp.sum(d_act_three * unit_three, axis=0)
    g_bias_three = jnp.sum(d_act_three, axis=0)
    d_resid_three = grad_out + norm_back(unit_three, inv_three, d_act_three * gain_three)

    d_cross_out = d_resid_three.astype(BF)
    d_cross = product_t(d_cross_out, w_cross_out).astype(BF)
    g_cross_out = weight_grad(cross_att, d_cross_out, nd, ns)
    d_cq, d_ck, d_cv = attend_back(
        cross_q, cross_kv, cross_kv, cross_off, HEADS, my_items, patch_items, cross_att, cross_lse, d_cross
    )
    d_ckv = jnp.concatenate([d_ck, d_cv], axis=1)
    d_act_two = product_t(d_cq, w_cross_q)
    g_gain_two = jnp.sum(d_act_two * unit_two, axis=0)
    g_bias_two = jnp.sum(d_act_two, axis=0)
    d_resid_two = d_resid_three + norm_back(unit_two, inv_two, d_act_two * gain_two)

    d_self_out = d_resid_two.astype(BF)
    d_self = product_t(d_self_out, w_self_out).astype(BF)
    d_self_mine = lax.all_to_all(d_self, "seq", 1, 0, tiled=True)
    g_cross_q = weight_grad(act_two, d_cq, nd, ns)
    g_cross_kv = weight_grad(patch_all, d_ckv, nd, ns)
    patch_grad = lax.psum_scatter(
        product_t(d_ckv, w_cross_kv).astype(BF), "seq", scatter_dimension=0, tiled=True
    ).astype(F32)
    g_self_out = weight_grad(self_att, d_self_out, nd, ns)
    d_q, d_k, d_v = attend_back(
        qkv, qkv, qkv, self_off, heads_here, tri_items, tri_items, self_mine, self_lse, d_self_mine
    )
    d_qkv = jnp.concatenate([d_q, d_k, d_v], axis=1)
    d_act_one_part = product_t(d_qkv, qkv_mine)

    shares = []
    for n in range(cameras.shape[0]):
        chosen = (tri_items == n)[:, None]
        shares.append(
            jnp.concatenate(
                [
                    jnp.sum(jnp.where(chosen, d_act_one_part, 0.0), axis=0),
                    jnp.sum(jnp.where(chosen, d_act_one_part * unit_one, 0.0), axis=0),
                ]
            )
        )
    g_mod_items = jnp.stack(shares)
    g_mod = lax.dot_general(
        g_mod_items, cameras.astype(F32), (((0,), (0,)), ((), ())), precision=lax.Precision.HIGHEST
    )

    d_act_one = lax.psum_scatter(d_act_one_part.astype(BF), "seq", scatter_dimension=0, tiled=True).astype(F32)
    g_qkv_dp = scatter_dp(core_half(act_one, d_qkv, nd), nd)
    g_qkv = lax.all_to_all(g_qkv_dp.astype(F32), "seq", 0, 0, tiled=True)
    g_qkv = (
        g_qkv.reshape(ns, qkv_weight.shape[0], 3, cols_here)
        .transpose(1, 2, 0, 3)
        .reshape(qkv_weight.shape)
    )
    unit_own, inv_own = norm_parts(resid_in)
    scale_own = per_item(my_items, mod_items[:, width:])
    input_grad = d_resid_two + norm_back(unit_own, inv_own, d_act_one * (1.0 + scale_own))

    def scatter_vector(value):
        return lax.psum_scatter(value, ALL, scatter_dimension=0, tiled=True)

    n_dev = nd * ns
    vector_grads = jnp.concatenate(
        [v.reshape(n_dev, -1) for v in (g_gain_two, g_bias_two, g_gain_three, g_bias_three, g_out_bias, g_in_bias)],
        axis=1,
    )
    vector_grads = scatter_vector(vector_grads.reshape(-1))
    g_mod = scatter_vector(g_mod)
    cut = [vector_grads[n * own : (n + 1) * own] for n in range(5)]
    return (
        block_out,
        input_grad,
        patch_grad,
        g_mod,
        g_qkv,
        g_self_out,
        cut[0],
        cut[1],
        g_cross_q,
        g_cross_kv,
        g_cross_out,
        cut[2],
        cut[3],
        g_w_in,
        vector_grads[5 * own :],
        g_w_out,
        cut[4],
    )


def solution(mesh):
    nd, ns = mesh.shape["dp"], mesh.shape["seq"]
    rows2, rows1 = P(ALL, None), P(ALL)
    placed = (rows2, rows2, P("dp", None), P("dp"), P("dp"), rows2, rows2, rows2, rows1, rows1, rows2, rows2, rows2, rows1, rows1, rows2, rows1, rows2, rows1, rows2)
    given = (rows2, rows2, rows2, rows2, rows2, rows2, rows1, rows1, rows2, rows2, rows2, rows1, rows1, rows2, rows1, rows2, rows1)

    def shards(*args):
        return block(nd, ns, *args)

    return jax.shard_map(shards, mesh=mesh, in_specs=placed, out_specs=given, check_vma=False)
```

time: 3050 us -> 1140 us (0.37)
  waiting for transfers between devices: 2070 us -> 465 us
  matrix products: 574 us -> 133 us
  Pallas kernels: 0 us -> 177 us
  blocking collectives: 214 us -> 58.8 us
  starting transfers between devices: 1.38 us -> 66.6 us
  local copies, waits for them, and re-layouts: 107 us -> 160 us
    reduce_scatter x10 -> x2, waiting for transfers between devices: 1550 us -> 0.01 us  [the longest x1 0.01 us: block(): lax.psum_scatter(product_t(d_ckv, w_cross_kv).astype(BF), 'seq', scatter_...]
    dot_general x248 -> x29, matrix products: 572 us -> 131 us  [the longest x7 47.6 us: product(): return jnp.dot(a, b, preferred_element_type=F32)]
    all_gather x11 -> x9, waiting for transfers between devices: 303 us -> 113 us  [the longest x6 113 us: gather(): return lax.all_gather(w, ALL, axis=0, tiled=True)]
    pallas_call x0 -> x4, Pallas kernels: none -> 177 us  [the longest x2 88.5 us: attend_back(): pl.pallas_call(lambda *refs: attend_back_kernel(*refs, kb=kb), grid=(pair...]
    ppermute x0 -> x47, waiting for transfers between devices: none -> 160 us  [swap(): return lax.ppermute(value, axis, [(r, r ^ bit) for r in range(size)])]
    all_gather x2 -> x0, blocking collectives: 134 us -> none  [the longest x1 68.2 us: shards(): lax.all_gather(mod_weight, ('dp', 'seq'), axis=0, tiled=True)]
    ppermute x0 -> x47, starting transfers between devices: none -> 53.7 us  [swap(): return lax.ppermute(value, axis, [(r, r ^ bit) for r in range(size)])]
    unnamed x2 -> x1, blocking collectives: 79.3 us -> 44.9 us
  transfers between devices with their start and end apart: 23 -> 63, of which waited for: 18 -> 32; matrix products, arithmetic and copies ran while one was open for 11% -> 27% of each run, Pallas kernels for 0% -> 13%
where the time goes in v1:
time: 1140 us
  waiting for transfers between devices  465 us (41%)
  Pallas kernels  177 us (16%)
  local copies, waits for them, and re-layouts  160 us (14%)
  matrix products  133 us (12%)
  starting transfers between devices  66.6 us (6%)
  other arithmetic  60.9 us (5%)
  blocking collectives  58.8 us (5%)
  between operations  17.9 us (2%)
    unnamed x15, waiting for transfers between devices  188 us
    ppermute x47, waiting for transfers between devices, swap(): return lax.ppermute(value, axis, [(r, r ^ bit) for r in range(size)])  160 us
    all_gather x6, waiting for transfers between devices, gather(): return lax.all_gather(w, ALL, axis=0, tiled=True)  113 us
    pallas_call x2, Pallas kernels, attend_back(): pl.pallas_call(lambda *refs: attend_back_kernel(*refs, kb=kb), grid=(pair...  88.5 us
    pallas_call x2, Pallas kernels, attend(): pl.pallas_call(lambda *refs: attend_kernel(*refs, kb=kb), grid=(pairs, nq...  88 us
    unnamed x191, local copies, waits for them, and re-layouts  78.2 us
    ppermute x47, starting transfers between devices, swap(): return lax.ppermute(value, axis, [(r, r ^ bit) for r in range(size)])  53.7 us
    dot_general x7, matrix products, product(): return jnp.dot(a, b, preferred_element_type=F32)  47.6 us
  transfers between devices with their start and end apart: 63, of which 32 were waited for; matrix products, arithmetic and copies ran while one was open for 27% of the time, Pallas kernels for 13%

profile of v1, /device:TPU:0, one launch (start us, length us, event | category | flops | bytes accessed | tf_op | source)
XLA Modules:
  0.0 1139.0 jit_solution(5718605674571904383)
XLA Ops:
  16.1 14.0 %all_to_all.56 = bf16[4,32,768]{2,1,0:T(8,128)(2,1)} all-to-all(bf16[4,32,768]{2,1,0:T(8,128)(2,1)S(1)} %all_to_all.40), channel_id=1, replica_groups=mesh['dp'=8,'seq'=4] {'seq'}, dimensions={0} | all-to-all | bytes 393216 | tf_op jit(solution)/shard_map/all_to_all | solution.py:344
  37.7 183.4 %all-reduce.4.cloned.1.call-done = bf16[41984]{0:T(1024)(128)(2,1)} async-done(((bf16[41984]{0:T(1024)(128)(2,1)}), bf16[41984]{0:T(1024)(128)(2,1)}) %all-reduce.4.cloned.1.call-update) | async-done | bytes 83984
  228.2 18.0 %fusion.5 = bf16[2048,1024]{1,0:T(8,128)(2,1)} fusion(bf16[2048,1024]{1,0:T(8,128)(2,1)S(1)} %copy-done.10, f32[1024]{0:T(1024)S(1)} %bitcast.438, f32[1024]{0:T(1024)S(1)} %bitcast.439, f32[1024]{0:T(1024)S(1)} %bitcast.440, f32[1024]{0:T(1024)S(1)} %bitcast.441, f32[1024]{0:T(1024)S(1)} %bitcast.425, f32[1024]{0:T(1024)S(1)} %bitcast.428, ...), kind=kLoop, calls=%fused_computation.8 | loop fusion | flops 27262976 | bytes 8443904 | tf_op jit(solution)/shard_map/convert_element_type | solution.py:379
  252.3 59.6 %attend.2 = (bf16[2048,256]{1,0:T(8,128)(2,1)S(1)}, f32[2,2,2048]{2,1,0:T(2,128)S(1)}) custom-call(s32[2048]{0:T(1024)S(1)} %copy-done.2, s32[2048]{0:T(1024)S(1)} %copy-done.2, bf16[2048,768]{1,0:T(8,128)(2,1)S(1)} %convolution_convert_fusion.3.refs_2_.refs_3_.refs_4_, bf16[2048,768]{1,0:T(8,128)(2,1)S(1)} %convolution_convert_fusion.3.refs_2_.refs_3_.refs_4_, ...), custom_call_target="tpu_custom_call" | custom-call | flops 17179869184 | bytes 4194304 | tf_op jit(solution)/shard_map/attend/pallas_call | solution.py:106
  323.9 7.7 reshape.496
  331.6 11.3 constant_dynamic-slice_fusion.12
  342.9 10.7 copy.114
  353.6 10.6 copy.113
  377.0 9.5 convolution_convert_fusion.2.refs_3_.refs_4_
  386.5 28.4 %attend.3 = (bf16[512,1024]{1,0:T(8,128)(2,1)S(1)}, f32[8,2,512]{2,1,0:T(2,128)S(1)}) custom-call(s32[512]{0:T(512)S(1)} %get-tuple-element.60.refs_0_, s32[1024]{0:T(1024)S(1)} %copy-done.3, bf16[512,1024]{1,0:T(8,128)(2,1)S(1)} %copy-done.7, bf16[1024,2048]{1,0:T(8,128)(2,1)} %convolution_convert_fusion.2.refs_3_.refs_4_, ...), custom_call_target="tpu_custom_call" | custom-call | flops 8589934592 | bytes 6291456 | tf_op jit(solution)/shard_map/attend/pallas_call | solution.py:106
  416.5 7.9 all-gather.23.cloned.1.call-done
  433.3 7.7 constant_dynamic-slice_fusion.2
  466.0 37.6 %all-gather.25.cloned.1.call-done = bf16[1024,4096]{1,0:T(8,128)(2,1)} async-done(((bf16[32,4096]{1,0:T(8,128)(2,1)}), bf16[1024,4096]{1,0:T(8,128)(2,1)}) %all-gather.25.cloned.1.call-update) | async-done | bytes 8388624 | tf_op jit(solution)/shard_map/all_gather | solution.py:335
  503.6 10.9 multiply_convert_fusion.1
  514.5 67.9 %all-gather.27.cloned.1.call-done = bf16[4096,1024]{1,0:T(8,128)(2,1)} async-done(((bf16[128,1024]{1,0:T(8,128)(2,1)}), bf16[4096,1024]{1,0:T(8,128)(2,1)}) %all-gather.27.cloned.1.call-update) | async-done | bytes 8388624 | tf_op jit(solution)/shard_map/all_gather | solution.py:335
  582.4 13.1 %convert_reduce_fusion.1 = (f32[4096]{0:T(1024)}, bf16[512,4096]{1,0:T(8,128)(2,1)}) fusion(f32[512,4096]{1,0:T(8,128)} %get-tuple-element.121, f32[4096]{0:T(1024)S(1)} %fusion.64, bf16[512,1024]{1,0:T(8,128)(2,1)} %param.39, bf16[4096,1024]{1,0:T(8,128)(2,1)} %all-gather.27.cloned.1.call-done), kind=kOutput, calls=%fused_computation.17 | convolution fusion | flops 4326420480 | bytes 22052864 | tf_op jit(solution)/shard_map/dot_general | solution.py:26
  605.6 30.6 %attend_back.2 = (bf16[512,1024]{1,0:T(8,128)(2,1)S(1)}, bf16[1024,1024]{1,0:T(8,128)(2,1)}, bf16[1024,1024]{1,0:T(8,128)(2,1)}) custom-call(s32[512]{0:T(512)S(1)} %get-tuple-element.60.refs_0_, s32[1024]{0:T(1024)S(1)} %copy-done.3, bf16[512,1024]{1,0:T(8,128)(2,1)S(1)} %copy-done.8, bf16[1024,2048]{1,0:T(8,128)(2,1)} %convolution_convert_fusion.2.refs_3_.refs_4_, ...), custom_call_target="tpu_custom_call" | custom-call | flops 21474836480 | bytes 12582912 | tf_op jit(solution)/shard_map/attend_back/pallas_call | solution.py:197
  671.0 57.8 %attend_back.3 = (bf16[2048,256]{1,0:T(8,128)(2,1)S(1)}, bf16[2048,256]{1,0:T(8,128)(2,1)S(1)}, bf16[2048,256]{1,0:T(8,128)(2,1)S(1)}) custom-call(s32[2048]{0:T(1024)S(1)} %copy-done.2, s32[2048]{0:T(1024)S(1)} %copy-done.2, bf16[2048,768]{1,0:T(8,128)(2,1)} %copy-done.9, bf16[2048,768]{1,0:T(8,128)(2,1)} %copy-done.9, bf16[2048,768]{1,0:T(8,128)(2,1)} %copy-done.9, ...), custom_call_target="tpu_custom_call" | custom-call | flops 42949672960 | bytes 8388608 | tf_op jit(solution)/shard_map/attend_back/pallas_call | solution.py:197
  735.6 9.7 select_reduce_fusion.6
  747.4 9.3 convolution_convert_fusion.5
  756.7 7.8 reshape.546
  766.1 10.3 add_convert_fusion.6
  776.4 9.8 constant_dynamic-slice_fusion
  786.3 9.1 copy.125
  800.3 44.9 %all-reduce.1 = f32[9216]{0:T(1024)S(1)} all-reduce(f32[9216]{0:T(1024)S(1)} %reshape.517), channel_id=6, replica_groups=mesh['dp'=8,'seq'=4] {'dp','seq'}, use_global_device_ids=true, to_apply=%region_31.32.clone | all-reduce | flops 9216 | bytes 73728
  845.9 11.0 copy.124
  918.5 8.0 collective-permute-done.17
  927.5 8.0 collective-permute-done.31
  999.3 19.4 %collective-permute-done.24 = bf16[2,32,2048]{2,1,0:T(8,128)(2,1)} collective-permute-done((bf16[2,32,2048]{2,1,0:T(8,128)(2,1)S(1)}, bf16[2,32,2048]{2,1,0:T(8,128)(2,1)}, u32[]{:S(2)}, u32[]{:S(2)}) %collective-permute-start.24) | collective-permute-done | bytes 262176 | tf_op jit(solution)/shard_map/ppermute | solution.py:241
  1043.5 16.0 %collective-permute-done.36 = bf16[2,128,2048]{2,1,0:T(8,128)(2,1)S(1)} collective-permute-done((bf16[2,128,2048]{2,1,0:T(8,128)(2,1)S(1)}, bf16[2,128,2048]{2,1,0:T(8,128)(2,1)S(1)}, u32[]{:S(2)}, u32[]{:S(2)}) %collective-permute-start.36) | collective-permute-done | bytes 1048608 | tf_op jit(solution)/shard_map/ppermute | solution.py:241
  1063.7 18.3 %collective-permute-done.43 = bf16[2,512,512]{2,1,0:T(8,128)(2,1)S(1)} collective-permute-done((bf16[2,512,512]{2,1,0:T(8,128)(2,1)S(1)}, bf16[2,512,512]{2,1,0:T(8,128)(2,1)S(1)}, u32[]{:S(2)}, u32[]{:S(2)}) %collective-permute-start.43) | collective-permute-done | bytes 1048608 | tf_op jit(solution)/shard_map/ppermute | solution.py:241
  1115.3 7.4 collective-permute-done.46
  (508 shorter events, 345.2 us)
Async XLA Ops:
  8.0 213.1 %all-reduce.4.cloned.1.call-start = ((), (), s32[]{:S(2)}) async-start(), calls=%async_computation.18 | async-start | bytes 167936
  14.1 208.9 %all-gather.11.cloned.1.call-start = ((), (), s32[]{:S(2)}) async-start(), calls=%async_computation.7 | async-start | bytes 5242880 | tf_op jit(solution)/shard_map/all_gather | solution.py:337
  14.7 231.5 %all-gather.13.cloned.1.call-start = ((), (), s32[]{:S(2)}) async-start(), calls=%async_computation.8 | async-start | bytes 1769472 | tf_op jit(solution)/shard_map/all_gather | solution.py:345
  30.1 290.7 %all-gather.19.cloned.1.call-start = ((), (), s32[]{:S(2)}) async-start(), calls=%async_computation.11 | async-start | bytes 2621440 | tf_op jit(solution)/shard_map/all_gather | solution.py:338
  31.2 333.0 %all-gather.15.cloned.1.call-start = ((), (), s32[]{:S(2)}) async-start(), calls=%async_computation.9 | async-start | bytes 2162688 | tf_op jit(solution)/shard_map/all_gather | solution.py:335
  32.0 341.2 %all-gather.17.cloned.1.call-start = ((), (), s32[]{:S(2)}) async-start(), calls=%async_computation.10 | async-start | bytes 2162688 | tf_op jit(solution)/shard_map/all_gather | solution.py:335
  32.7 344.3 %all-gather.21.cloned.1.call-start = ((), (), s32[]{:S(2)}) async-start(), calls=%async_computation.12 | async-start | bytes 4325376 | tf_op jit(solution)/shard_map/all_gather | solution.py:335
  33.4 391.0 %all-gather.23.cloned.1.call-start = ((), (), s32[]{:S(2)}) async-start(), calls=%async_computation.13 | async-start | bytes 2162688 | tf_op jit(solution)/shard_map/all_gather | solution.py:335
  34.0 469.6 %all-gather.25.cloned.1.call-start = ((), (), s32[]{:S(2)}) async-start(), calls=%async_computation.14 | async-start | bytes 8650752 | tf_op jit(solution)/shard_map/all_gather | solution.py:335
  34.6 547.8 %all-gather.27.cloned.1.call-start = ((), (), s32[]{:S(2)}) async-start(), calls=%async_computation.15 | async-start | bytes 8650752 | tf_op jit(solution)/shard_map/all_gather | solution.py:335
  313.3 50.9 %all-to-all-start.1 = ((bf16[4,512,256]{1,2,0:T(8,128)(2,1)}), bf16[4,512,256]{1,2,0:T(8,128)(2,1)}, u32[]{:S(2)}, u32[]{:S(2)}) async-start(bf16[4,512,256]{1,2,0:T(8,128)(2,1)} %copy.91), calls=%async_computation.1 | async-start | bytes 2097152 | tf_op jit(solution)/shard_map/all_to_all | solution.py:384
  642.1 28.9 %all-to-all-start.2 = ((bf16[512,4,256]{2,0,1:T(8,128)(2,1)}), bf16[512,4,256]{2,0,1:T(8,128)(2,1)S(1)}, u32[]{:S(2)}, u32[]{:S(2)}) async-start(bf16[512,4,256]{2,0,1:T(8,128)(2,1)} %bitcast.344), calls=%async_computation.2 | async-start | bytes 2097152 | tf_op jit(solution)/shard_map/all_to_all | solution.py:427
  645.6 308.1 %reduce-scatter.10.cloned.1.call-start = ((), (), s32[]{:S(2)}) async-start(), calls=%async_computation.19 | async-start | bytes 1081344
  649.6 207.9 %collective-permute-start.5 = (bf16[512,1024]{1,0:T(8,128)(2,1)}, bf16[512,1024]{1,0:T(8,128)(2,1)}, u32[]{:S(2)}, u32[]{:S(2)}) collective-permute-start(bf16[512,1024]{1,0:T(8,128)(2,1)} %convolution_convert_fusion.11), channel_id=1, source_target_pairs={{0,4},{4,0},{8,12},{12,8},{16,20},{20,16},{24,28},{28,24},{1,5},{5... | collective-permute-start | bytes 3145736 | tf_op jit(solution)/shard_map/ppermute | solution.py:241
  658.6 201.0 %collective-permute-start.12 = (bf16[512,1024]{1,0:T(8,128)(2,1)}, bf16[512,1024]{1,0:T(8,128)(2,1)}, u32[]{:S(2)}, u32[]{:S(2)}) collective-permute-start(bf16[512,1024]{1,0:T(8,128)(2,1)} %convolution_convert_fusion.10), channel_id=1, source_target_pairs={{0,4},{4,0},{8,12},{12,8},{16,20},{20,16},{24,28},{28,24},{1,5},{5... | collective-permute-start | bytes 3145736 | tf_op jit(solution)/shard_map/ppermute | solution.py:241
  663.8 291.3 %collective-permute-start.19 = (bf16[512,2048]{1,0:T(8,128)(2,1)}, bf16[512,2048]{1,0:T(8,128)(2,1)}, u32[]{:S(2)}, u32[]{:S(2)}) collective-permute-start(bf16[512,2048]{1,0:T(8,128)(2,1)} %convolution_convert_fusion.4), channel_id=1, source_target_pairs={{0,4},{4,0},{8,12},{12,8},{16,20},{20,16},{24,28},{28,24},{1,5},{5... | collective-permute-start | bytes 6291464 | tf_op jit(solution)/shard_map/ppermute | solution.py:241
  666.0 198.1 %collective-permute-start.26 = (bf16[512,1024]{1,0:T(8,128)(2,1)}, bf16[512,1024]{1,0:T(8,128)(2,1)}, u32[]{:S(2)}, u32[]{:S(2)}) collective-permute-start(bf16[512,1024]{1,0:T(8,128)(2,1)} %convolution_convert_fusion.9), channel_id=1, source_target_pairs={{0,4},{4,0},{8,12},{12,8},{16,20},{20,16},{24,28},{28,24},{1,5},{5... | collective-permute-start | bytes 3145736 | tf_op jit(solution)/shard_map/ppermute | solution.py:241
  670.5 356.2 %collective-permute-start.33 = (bf16[512,4096]{1,0:T(8,128)(2,1)}, bf16[512,4096]{1,0:T(8,128)(2,1)}, u32[]{:S(2)}, u32[]{:S(2)}) collective-permute-start(bf16[512,4096]{1,0:T(8,128)(2,1)} %convolution_convert_fusion), channel_id=1, source_target_pairs={{0,4},{4,0},{8,12},{12,8},{16,20},{20,16},{24,28},{28,24},{1,5},{5... | collective-permute-start | bytes 12582920 | tf_op jit(solution)/shard_map/ppermute | solution.py:241
  747.4 365.8 %reduce-scatter.8.cloned.1.call-start = ((), (), s32[]{:S(2)}) async-start(), calls=%async_computation.17 | async-start | bytes 2621440 | tf_op jit(solution)/shard_map/reduce_scatter | solution.py:430
  764.5 361.9 %reduce-scatter.6.cloned.1.call-start = ((), (), s32[]{:S(2)}) async-start(), calls=%async_computation.16 | async-start | bytes 5242880 | tf_op jit(solution)/shard_map/reduce_scatter | solution.py:456
  857.5 179.2 %collective-permute-start.40 = (bf16[2048,1024]{1,0:T(8,128)(2,1)}, bf16[2048,1024]{1,0:T(8,128)(2,1)}, u32[]{:S(2)}, u32[]{:S(2)}) collective-permute-start(bf16[2048,1024]{1,0:T(8,128)(2,1)} %convolution_convert_fusion.1), channel_id=1, source_target_pairs={{0,4},{4,0},{8,12},{12,8},{16,20},{20,16},{24,28},{28,24},{1,5},{5... | collective-permute-start | bytes 12582920 | tf_op jit(solution)/shard_map/ppermute | solution.py:241
  926.4 36.1 %collective-permute-start = (bf16[512,768]{1,0:T(8,128)(2,1)}, bf16[512,768]{1,0:T(8,128)(2,1)}, u32[]{:S(2)}, u32[]{:S(2)}) collective-permute-start(bf16[512,768]{1,0:T(8,128)(2,1)} %convolution_convert_fusion.12), channel_id=1, source_target_pairs={{0,4},{4,0},{8,12},{12,8},{16,20},{20,16},{24,28},{28,24},{1,5},{5... | collective-permute-start | bytes 2359304 | tf_op jit(solution)/shard_map/ppermute | solution.py:241
  960.7 24.9 %collective-permute-start.22 = (bf16[2,128,1024]{2,1,0:T(8,128)(2,1)S(1)}, bf16[2,128,1024]{2,1,0:T(8,128)(2,1)S(1)}, u32[]{:S(2)}, u32[]{:S(2)}) collective-permute-start(bf16[2,128,1024]{2,1,0:T(8,128)(2,1)S(1)} %dynamic-slice_bitcast_fusion.10), channel_id=1, source_target_pairs={{0,16},{4,20},{8,24},{12,28},{16,0},{20,4},{24,8},{28,12},{1,17},{... | collective-permute-start | bytes 1572872 | tf_op jit(solution)/shard_map/ppermute | solution.py:241
  994.6 24.1 %collective-permute-start.24 = (bf16[2,32,2048]{2,1,0:T(8,128)(2,1)S(1)}, bf16[2,32,2048]{2,1,0:T(8,128)(2,1)}, u32[]{:S(2)}, u32[]{:S(2)}) collective-permute-start(bf16[2,32,2048]{2,1,0:T(8,128)(2,1)S(1)} %dynamic-slice_bitcast_fusion.16), channel_id=1, source_target_pairs={{0,1},{1,0},{2,3},{3,2},{4,5},{5,4},{6,7},{7,6},{8,9},{9,8},{10,11... | collective-permute-start | bytes 786440 | tf_op jit(solution)/shard_map/ppermute | solution.py:241
  995.5 29.7 %all-to-all-start.3 = ((f32[4,32,768]{2,1,0:T(8,128)}), f32[4,32,768]{2,1,0:T(8,128)S(1)}, u32[]{:S(2)}, u32[]{:S(2)}) async-start(f32[4,32,768]{2,1,0:T(8,128)} %maximum_convert_fusion), calls=%async_computation.5 | async-start | bytes 786432 | tf_op jit(solution)/shard_map/all_to_all | solution.py:458
  1020.5 91.9 %collective-permute-start.25 = (bf16[32,2048]{1,0:T(8,128)(2,1)}, bf16[32,2048]{1,0:T(8,128)(2,1)S(1)}, u32[]{:S(2)}, u32[]{:S(2)}) collective-permute-start(bf16[32,2048]{1,0:T(8,128)(2,1)} %dynamic-slice_bitcast_fusion.28), channel_id=1, source_target_pairs={{0,2},{1,3},{2,0},{3,1},{4,6},{5,7},{6,4},{7,5},{8,10},{9,11},{10,... | collective-permute-start | bytes 393224 | tf_op jit(solution)/shard_map/ppermute | solution.py:241
  1033.4 26.2 %collective-permute-start.36 = (bf16[2,128,2048]{2,1,0:T(8,128)(2,1)S(1)}, bf16[2,128,2048]{2,1,0:T(8,128)(2,1)S(1)}, u32[]{:S(2)}, u32[]{:S(2)}) collective-permute-start(bf16[2,128,2048]{2,1,0:T(8,128)(2,1)S(1)} %dynamic-slice_bitcast_fusion.2), channel_id=1, source_target_pairs={{0,16},{4,20},{8,24},{12,28},{16,0},{20,4},{24,8},{28,12},{1,17},{... | collective-permute-start | bytes 3145736 | tf_op jit(solution)/shard_map/ppermute | solution.py:241
  1034.6 27.7 %collective-permute-start.34 = (bf16[2,128,2048]{2,1,0:T(8,128)(2,1)S(1)}, bf16[2,128,2048]{2,1,0:T(8,128)(2,1)S(1)}, u32[]{:S(2)}, u32[]{:S(2)}) collective-permute-start(bf16[2,128,2048]{2,1,0:T(8,128)(2,1)S(1)} %dynamic-slice_bitcast_fusion.3), channel_id=1, source_target_pairs={{0,8},{4,12},{8,0},{12,4},{16,24},{20,28},{24,16},{28,20},{1,9},{5... | collective-permute-start | bytes 3145736 | tf_op jit(solution)/shard_map/ppermute | solution.py:241
  1041.8 40.3 %collective-permute-start.43 = (bf16[2,512,512]{2,1,0:T(8,128)(2,1)S(1)}, bf16[2,512,512]{2,1,0:T(8,128)(2,1)S(1)}, u32[]{:S(2)}, u32[]{:S(2)}) collective-permute-start(bf16[2,512,512]{2,1,0:T(8,128)(2,1)S(1)} %dynamic-slice_bitcast_fusion), channel_id=1, source_target_pairs={{0,16},{4,20},{8,24},{12,28},{16,0},{20,4},{24,8},{28,12},{1,17},{... | collective-permute-start | bytes 3145736 | tf_op jit(solution)/shard_map/ppermute | solution.py:241
  1043.1 41.6 %collective-permute-start.41 = (bf16[2,512,512]{2,1,0:T(8,128)(2,1)S(1)}, bf16[2,512,512]{2,1,0:T(8,128)(2,1)S(1)}, u32[]{:S(2)}, u32[]{:S(2)}) collective-permute-start(bf16[2,512,512]{2,1,0:T(8,128)(2,1)S(1)} %dynamic-slice_bitcast_fusion.1), channel_id=1, source_target_pairs={{0,8},{4,12},{8,0},{12,4},{16,24},{20,28},{24,16},{28,20},{1,9},{5... | collective-permute-start | bytes 3145736 | tf_op jit(solution)/shard_map/ppermute | solution.py:241
  1060.0 30.6 %collective-permute-start.37 = (bf16[128,2048]{1,0:T(8,128)(2,1)S(1)}, bf16[128,2048]{1,0:T(8,128)(2,1)S(1)}, u32[]{:S(2)}, u32[]{:S(2)}) collective-permute-start(bf16[128,2048]{1,0:T(8,128)(2,1)S(1)} %dynamic-slice_bitcast_fusion.8), channel_id=1, source_target_pairs={{0,8},{4,12},{8,0},{12,4},{16,24},{20,28},{24,16},{28,20},{1,9},{5... | collective-permute-start | bytes 1572872 | tf_op jit(solution)/shard_map/ppermute | solution.py:241
  1062.8 28.0 %collective-permute-start.35 = (bf16[128,2048]{1,0:T(8,128)(2,1)S(1)}, bf16[128,2048]{1,0:T(8,128)(2,1)S(1)}, u32[]{:S(2)}, u32[]{:S(2)}) collective-permute-start(bf16[128,2048]{1,0:T(8,128)(2,1)S(1)} %dynamic-slice_bitcast_fusion.9), channel_id=1, source_target_pairs={{0,16},{4,20},{8,24},{12,28},{16,0},{20,4},{24,8},{28,12},{1,17},{... | collective-permute-start | bytes 1572872 | tf_op jit(solution)/shard_map/ppermute | solution.py:241
  (117 other events, 2307.3 us)
Sparse Core Ops, SparseCore 0:
  15.0 206.0 all-reduce.3
  747.5 142.5 reduce-scatter.9
  892.4 50.6 reduce-scatter.7
  945.3 91.3 reduce-scatter.5
Sparse Core Ops, SparseCore 1:
  16.1 83.6 all-gather.10
  101.5 24.0 all-gather.12
  127.6 46.3 all-gather.18
  176.9 54.8 all-gather.14
  234.7 55.6 all-gather.16
  293.4 72.7 all-gather.20
  369.0 55.4 all-gather.22
  427.2 76.3 all-gather.24
  506.4 76.0 all-gather.26

commit v2 on v1

v2 whole, which is shorter than its diff:
```python
import functools
import math

import jax
import jax.numpy as jnp
from jax import lax
from jax.experimental import pallas as pl
from jax.experimental.pallas import tpu as pltpu
from jax.sharding import PartitionSpec as P

HEADS = 16
HEAD = 64
PAIR = 2 * HEAD
BF = jnp.bfloat16
F32 = jnp.float32
LOG2E = math.log2(math.e)
ALL = ("dp", "seq")
SOFT = LOG2E / math.sqrt(HEAD)
NEG = -1e30
VMEM_LIMIT = 56 * 1024 * 1024


def product(a, b):
    return jnp.dot(a, b, preferred_element_type=F32)


def product_t(a, b):
    return lax.dot_general(a, b, (((1,), (1,)), ((), ())), preferred_element_type=F32)


def contract_rows(a, b):
    return lax.dot_general(a, b, (((0,), (0,)), ((), ())), preferred_element_type=F32)


SHORT = pl.CostEstimate(flops=1, bytes_accessed=1, transcendentals=0)


def kernel_params():
    return pltpu.CompilerParams(vmem_limit_bytes=VMEM_LIMIT)


def head_lanes(rows, h):
    lane = lax.broadcasted_iota(jnp.int32, (rows, PAIR), 1)
    return (lane < HEAD, lane - HEAD) if h == 0 else (lane >= HEAD, lane)


def only_head(value, h):
    mine, _ = head_lanes(value.shape[0], h)
    return jnp.where(mine, value, jnp.zeros_like(value))


def tag_query(q, ids, h, items):
    mine, slot = head_lanes(q.shape[0], h)
    barred = jnp.where((slot != ids) & (slot >= 0) & (slot < items), NEG, 0.0)
    return jnp.where(mine, q.astype(F32), barred).astype(BF)


def tag_key(k, ids, h):
    mine, slot = head_lanes(k.shape[0], h)
    return jnp.where(mine, k.astype(F32), jnp.where(slot == ids, 1.0, 0.0)).astype(BF)


def with_ones(v, h):
    mine, _ = head_lanes(v.shape[0], h)
    return jnp.where(mine, v, jnp.ones_like(v))


def attend_kernel(q_ref, k_ref, v_ref, qid_ref, kid_ref, o_ref, lse_ref, key_ref, val_ref, *, items, heads):
    qb = q_ref.shape[0]

    @pl.when(pl.program_id(1) == 0)
    def _():
        for p in range(heads // 2):
            lanes = slice(p * PAIR, (p + 1) * PAIR)
            for h in range(2):
                key_ref[2 * p + h] = tag_key(k_ref[:, lanes], kid_ref[...], h)
                val_ref[2 * p + h] = with_ones(v_ref[:, lanes], h)

    for p in range(heads // 2):
        lanes = slice(p * PAIR, (p + 1) * PAIR)
        sums, tops = [], []
        for h in range(2):
            scores = product_t(tag_query(q_ref[:, lanes], qid_ref[...], h, items), key_ref[2 * p + h])
            top = jnp.max(scores, axis=1, keepdims=True)
            probs = jnp.exp2((scores - top) * SOFT).astype(BF)
            sums.append(product(probs, val_ref[2 * p + h]))
            tops.append(top)
        first = lax.broadcasted_iota(jnp.int32, (qb, PAIR), 1) < HEAD
        total = jnp.where(first, pltpu.roll(sums[0], HEAD, 1), pltpu.roll(sums[1], HEAD, 1))
        o_ref[:, lanes] = (jnp.where(first, sums[0], sums[1]) / total).astype(BF)
        lse = (jnp.where(first, tops[0], tops[1]) * SOFT + jnp.log2(total)).T
        lse_ref[p] = jnp.concatenate([lse[0:1], lse[HEAD : HEAD + 1]], axis=0)


def attend(q, k, v, starts, heads, q_ids, k_ids, items, first=0):
    nq, nk = q.shape[0], k.shape[0]
    step = min(4, heads)
    cols = step * HEAD
    qb = min(256, nq)
    q_off, k_off, v_off = (s // cols + first // step for s in starts)
    return pl.pallas_call(
        functools.partial(attend_kernel, items=items, heads=step),
        grid=(heads // step, nq // qb),
        in_specs=[
            pl.BlockSpec((qb, cols), lambda p, i: (i, q_off + p)),
            pl.BlockSpec((nk, cols), lambda p, i: (0, k_off + p)),
            pl.BlockSpec((nk, cols), lambda p, i: (0, v_off + p)),
            pl.BlockSpec((qb, 1), lambda p, i: (i, 0)),
            pl.BlockSpec((nk, 1), lambda p, i: (0, 0)),
        ],
        out_specs=[
            pl.BlockSpec((qb, cols), lambda p, i: (i, p)),
            pl.BlockSpec((step // 2, 2, qb), lambda p, i: (p, 0, i)),
        ],
        out_shape=[
            jax.ShapeDtypeStruct((nq, heads * HEAD), BF),
            jax.ShapeDtypeStruct((heads // 2, 2, nq), F32),
        ],
        scratch_shapes=[pltpu.VMEM((step, nk, PAIR), BF), pltpu.VMEM((step, nk, PAIR), BF)],
        compiler_params=kernel_params(),
        cost_estimate=SHORT,
        name="attend",
    )(q, k, v, q_ids, k_ids)


def attend_back_kernel(q_ref, k_ref, v_ref, do_ref, o_ref, lse_ref, qid_ref, kid_ref, dq_ref, dk_ref, dv_ref, key_ref, kt_ref, dk_sum, dv_sum, *, items, kb):
    i = pl.program_id(1)
    nk = k_ref.shape[0]

    @pl.when(i == 0)
    def _():
        kt_ref[...] = k_ref[...].T
        for h in range(2):
            key_ref[h] = tag_key(k_ref[...], kid_ref[...], h)
        dk_sum[...] = jnp.zeros(dk_sum.shape, F32)
        dv_sum[...] = jnp.zeros(dv_sum.shape, F32)

    q, do = q_ref[...], do_ref[...]
    both = (do.astype(F32) * o_ref[...].astype(F32)).T
    q_own = [only_head(q, h) for h in range(2)]
    do_own = [only_head(do, h) for h in range(2)]
    q_tag = [tag_query(q, qid_ref[...], h, items) for h in range(2)]
    delta = [jnp.sum(both[h * HEAD : (h + 1) * HEAD], axis=0, keepdims=True) for h in range(2)]
    dq = [None, None]
    for j in range(nk // kb):
        rows = slice(j * kb, (j + 1) * kb)
        probs_low, grads_low = [], []
        for h in range(2):
            scores = product_t(key_ref[h, rows, :], q_tag[h])
            probs = jnp.exp2(scores * SOFT - lse_ref[0, h : h + 1, :])
            grad_probs = product_t(v_ref[rows, :], do_own[h])
            grads_low.append((probs * (grad_probs - delta[h])).astype(BF))
            probs_low.append(probs.astype(BF))
            term = product(kt_ref[h * HEAD : (h + 1) * HEAD, rows], grads_low[h])
            dq[h] = term if dq[h] is None else dq[h] + term
        dv_sum[rows, :] += product(jnp.concatenate(probs_low, axis=1), jnp.concatenate(do_own, axis=0))
        dk_sum[rows, :] += product(jnp.concatenate(grads_low, axis=1), jnp.concatenate(q_own, axis=0))
    dq_ref[...] = (jnp.concatenate(dq, axis=0) * (1.0 / math.sqrt(HEAD))).T.astype(BF)

    @pl.when(i == pl.num_programs(1) - 1)
    def _():
        dk_ref[...] = (dk_sum[...] * (1.0 / math.sqrt(HEAD))).astype(BF)
        dv_ref[...] = dv_sum[...].astype(BF)


def attend_back(q, k, v, starts, heads, q_ids, k_ids, items, out, lse, grad_out, first=0):
    nq, nk = q.shape[0], k.shape[0]
    pairs = heads // 2
    qb, kb = min(512, nq), min(2048, nk)
    base = first // 2
    q_off, k_off, v_off = (s // PAIR + base for s in starts)
    mine = pl.BlockSpec((qb, PAIR), lambda p, i: (i, p + base))
    return pl.pallas_call(
        functools.partial(attend_back_kernel, items=items, kb=kb),
        grid=(pairs, nq // qb),
        in_specs=[
            pl.BlockSpec((qb, PAIR), lambda p, i: (i, q_off + p)),
            pl.BlockSpec((nk, PAIR), lambda p, i: (0, k_off + p)),
            pl.BlockSpec((nk, PAIR), lambda p, i: (0, v_off + p)),
            mine,
            mine,
            pl.BlockSpec((1, 2, qb), lambda p, i: (p + base, 0, i)),
            pl.BlockSpec((qb, 1), lambda p, i: (i, 0)),
            pl.BlockSpec((nk, 1), lambda p, i: (0, 0)),
        ],
        out_specs=[
            pl.BlockSpec((qb, PAIR), lambda p, i: (i, p)),
            pl.BlockSpec((nk, PAIR), lambda p, i: (0, p)),
            pl.BlockSpec((nk, PAIR), lambda p, i: (0, p)),
        ],
        out_shape=[
            jax.ShapeDtypeStruct((nq, pairs * PAIR), BF),
            jax.ShapeDtypeStruct((nk, pairs * PAIR), BF),
            jax.ShapeDtypeStruct((nk, pairs * PAIR), BF),
        ],
        scratch_shapes=[
            pltpu.VMEM((2, nk, PAIR), BF),
            pltpu.VMEM((PAIR, nk), BF),
            pltpu.VMEM((nk, PAIR), F32),
            pltpu.VMEM((nk, PAIR), F32),
        ],
        compiler_params=kernel_params(),
        cost_estimate=SHORT,
        name="attend_back",
    )(q, k, v, grad_out, out, lse, q_ids, k_ids)


def mlp_up_kernel(a_ref, w_ref, b_ref, hid_ref, slope_ref):
    pre = product(a_ref[...], w_ref[...]) + b_ref[...]
    cdf = 0.5 * (1.0 + lax.erf(pre * (1.0 / math.sqrt(2.0))))
    density = jnp.exp(-0.5 * pre * pre) * (1.0 / math.sqrt(2.0 * math.pi))
    hid_ref[...] = (pre * cdf).astype(BF)
    slope_ref[...] = (cdf + pre * density).astype(BF)


def mlp_up(act, w, bias):
    rows, ff = act.shape[0], w.shape[1]
    cb = 512
    block = pl.BlockSpec((rows, cb), lambda g: (0, g))
    return pl.pallas_call(
        mlp_up_kernel,
        grid=(ff // cb,),
        in_specs=[
            pl.BlockSpec(act.shape, lambda g: (0, 0)),
            pl.BlockSpec((w.shape[0], cb), lambda g: (0, g)),
            pl.BlockSpec((1, cb), lambda g: (0, g)),
        ],
        out_specs=[block, block],
        out_shape=[jax.ShapeDtypeStruct((rows, ff), BF)] * 2,
        compiler_params=kernel_params(),
        cost_estimate=SHORT,
        name="mlp_up",
    )(act, w, bias)


def mlp_back_kernel(g_ref, w_ref, slope_ref, out_ref, sum_ref):
    grad = product_t(g_ref[...], w_ref[...]) * slope_ref[...].astype(F32)
    low = grad.astype(BF)
    out_ref[...] = low
    sum_ref[...] = jnp.sum(low.astype(F32), axis=0, keepdims=True)


def mlp_back(grad, w, slope):
    rows, ff = slope.shape
    cb = 512
    block = pl.BlockSpec((rows, cb), lambda g: (0, g))
    return pl.pallas_call(
        mlp_back_kernel,
        grid=(ff // cb,),
        in_specs=[
            pl.BlockSpec(grad.shape, lambda g: (0, 0)),
            pl.BlockSpec((cb, w.shape[1]), lambda g: (g, 0)),
            block,
        ],
        out_specs=[block, pl.BlockSpec((1, cb), lambda g: (0, g))],
        out_shape=[jax.ShapeDtypeStruct((rows, ff), BF), jax.ShapeDtypeStruct((1, ff), F32)],
        compiler_params=kernel_params(),
        cost_estimate=SHORT,
        name="mlp_back",
    )(grad, w, slope)


def norm_parts(values):
    centre = values - jnp.mean(values, axis=-1, keepdims=True)
    spread = jnp.mean(centre * centre, axis=-1, keepdims=True)
    inverse = lax.rsqrt(spread + 1e-05)
    return centre * inverse, inverse


def norm_back(unit, inverse, grad):
    return inverse * (
        grad
        - jnp.mean(grad, axis=-1, keepdims=True)
        - unit * jnp.mean(grad * unit, axis=-1, keepdims=True)
    )


def per_item(ids, rows):
    out = jnp.broadcast_to(rows[0:1, :], (ids.shape[0], rows.shape[1]))
    for n in range(1, rows.shape[0]):
        out = jnp.where(ids == n, rows[n : n + 1, :], out)
    return out


def modulate_kernel(x_ref, id_ref, mod_ref, out_ref):
    width = x_ref.shape[1]
    unit, _ = norm_parts(x_ref[...].astype(F32))
    ids = id_ref[...]
    shift = per_item(ids, mod_ref[:, :width])
    scale = per_item(ids, mod_ref[:, width:])
    out_ref[...] = (unit * (1.0 + scale) + shift).astype(BF)


def modulate(x, ids, mod_items):
    rows, width = x.shape
    rb = 256
    return pl.pallas_call(
        modulate_kernel,
        grid=(rows // rb,),
        in_specs=[
            pl.BlockSpec((rb, width), lambda i: (i, 0)),
            pl.BlockSpec((rb, 1), lambda i: (i, 0)),
            pl.BlockSpec(mod_items.shape, lambda i: (0, 0)),
        ],
        out_specs=pl.BlockSpec((rb, width), lambda i: (i, 0)),
        out_shape=jax.ShapeDtypeStruct((rows, width), BF),
        compiler_params=kernel_params(),
        cost_estimate=SHORT,
        name="modulate",
    )(x, ids, mod_items)


def modulate_back_kernel(dq_ref, dk_ref, dv_ref, w_ref, x_ref, id_ref, out_ref, sum_ref):
    width = x_ref.shape[1]
    c = dq_ref.shape[1]
    items = sum_ref.shape[0]
    grad = product_t(dq_ref[...], w_ref[:, 0:c])
    grad += product_t(dk_ref[...], w_ref[:, c : 2 * c])
    grad += product_t(dv_ref[...], w_ref[:, 2 * c :])
    out_ref[...] = grad.astype(BF)

    @pl.when(pl.program_id(0) == 0)
    def _():
        sum_ref[...] = jnp.zeros(sum_ref.shape, F32)

    unit, _ = norm_parts(x_ref[...].astype(F32))
    times = grad * unit
    ids = id_ref[...]
    low, high = jnp.min(ids), jnp.max(ids)
    for n in range(items):
        @pl.when((low <= n) & (n <= high))
        def _():
            here = ids == n
            sum_ref[n : n + 1, :width] += jnp.sum(jnp.where(here, grad, 0.0), axis=0, keepdims=True)
            sum_ref[n : n + 1, width:] += jnp.sum(jnp.where(here, times, 0.0), axis=0, keepdims=True)


def modulate_back(d_q, d_k, d_v, w, x, ids, items):
    rows, width = x.shape
    rb = 256
    c = d_q.shape[1]
    part = pl.BlockSpec((rb, c), lambda i: (i, 0))
    return pl.pallas_call(
        modulate_back_kernel,
        grid=(rows // rb,),
        in_specs=[
            part,
            part,
            part,
            pl.BlockSpec(w.shape, lambda i: (0, 0)),
            pl.BlockSpec((rb, width), lambda i: (i, 0)),
            pl.BlockSpec((rb, 1), lambda i: (i, 0)),
        ],
        out_specs=[
            pl.BlockSpec((rb, width), lambda i: (i, 0)),
            pl.BlockSpec((items, 2 * width), lambda i: (0, 0)),
        ],
        out_shape=[jax.ShapeDtypeStruct((rows, width), BF), jax.ShapeDtypeStruct((items, 2 * width), F32)],
        compiler_params=kernel_params(),
        cost_estimate=SHORT,
        name="modulate_back",
    )(d_q, d_k, d_v, w, x, ids)


def grads_kernel(*refs, spans):
    n = len(spans)
    g = pl.program_id(0)
    x_refs, y_refs, out_ref, xt_ref = refs[:n], refs[n : 2 * n], refs[-2], refs[-1]
    for i, (start, stop) in enumerate(spans):
        rows = y_refs[i].shape[0]

        @pl.when(g == start)
        def _():
            xt_ref[:, :rows] = x_refs[i][...].T

        @pl.when((g >= start) & (g < stop))
        def _():
            out_ref[...] = product(xt_ref[:, :rows], y_refs[i][...]).astype(BF)


def weight_grads(pairs):
    width = pairs[0][0].shape[1]
    cb = min(1024, min(y.shape[1] for _, y in pairs))
    spans, at = [], 0
    for _, y in pairs:
        spans.append((at, at + y.shape[1] // cb))
        at = spans[-1][1]
    in_specs = [pl.BlockSpec(x.shape, lambda g: (0, 0), pipeline_mode=pl.Buffered(1)) for x, _ in pairs]
    for (_, y), (start, stop) in zip(pairs, spans):
        in_specs.append(
            pl.BlockSpec((y.shape[0], cb), lambda g, start=start, stop=stop: (0, jnp.clip(g - start, 0, stop - start - 1)))
        )
    longest = max(x.shape[0] for x, _ in pairs)
    return pl.pallas_call(
        functools.partial(grads_kernel, spans=tuple(spans)),
        grid=(at,),
        in_specs=in_specs,
        out_specs=pl.BlockSpec((width, cb), lambda g: (0, g)),
        scratch_shapes=[pltpu.VMEM((width, longest), BF)],
        out_shape=jax.ShapeDtypeStruct((width, at * cb), BF),
        compiler_params=kernel_params(),
        cost_estimate=SHORT,
        name="weight_grads",
    )(*[x for x, _ in pairs], *[y for _, y in pairs])


def bits_of(size):
    return [1 << b for b in range(size.bit_length() - 1)]


def swap(value, axis, bit, size):
    return lax.ppermute(value, axis, [(r, r ^ bit) for r in range(size)])


def my_bit(axis, bit):
    return (lax.axis_index(axis) // bit) % 2


def pick(value, index, where):
    return lax.dynamic_index_in_dim(value, index, where, keepdims=False)


def tie(first, rest):
    kept, rest = lax.optimization_barrier((first, rest))
    return kept, rest


def sum_xor(value, axis, size):
    me = lax.axis_index(axis)
    got = [swap(pick(value, me ^ m, 0), axis, m, size) for m in range(1, size)]
    return pick(value, me, 0), got


def add_all(own, got, dtype=F32):
    total = own.astype(F32)
    for value in got:
        total = total + value.astype(F32)
    return total.astype(dtype)


def gather_xor(value, axis, size):
    have = [value] + [swap(value, axis, m, size) for m in range(1, size)]
    return jnp.concatenate(natural(have, axis, size), axis=0)


def to_dp(whole):
    return lax.psum_scatter(whole, "dp", scatter_dimension=0, tiled=True)


def sync(*values):
    return lax.optimization_barrier(values)


def line_step(up, down, ns):
    return (
        lax.ppermute(up, "seq", [(r, r + 1) for r in range(ns - 1)]),
        lax.ppermute(down, "seq", [(r + 1, r) for r in range(ns - 1)]),
    )


def line_join(ups, downs, ns):
    turned = [ups[0]] + [downs[r] + ups[ns - r] for r in range(1, ns)]
    rows = ups[0].shape[0]
    twice = jnp.concatenate(turned + turned[:-1], axis=0)
    first = (ns - lax.axis_index("seq")) % ns
    return lax.dynamic_slice_in_dim(twice, first * rows, ns * rows)


class LineSum:
    def __init__(self, parts, ns):
        self.parts, self.ns, self.k = parts, ns, 0
        self.moved = None

    def chunk(self, d):
        rows = self.parts.shape[0] // self.ns
        return lax.dynamic_slice_in_dim(self.parts, jnp.clip(d, 0, self.ns - 1) * rows, rows).astype(F32)

    def start(self):
        self.k += 1
        k, ns, me = self.k, self.ns, lax.axis_index("seq")
        above, below = self.chunk(me + ns - k), self.chunk(me - ns + k)
        if self.moved is not None:
            above, below = above + self.moved[0].astype(F32), below + self.moved[1].astype(F32)
        self.moved = (
            lax.ppermute(above.astype(BF), "seq", [(r, r + 1) for r in range(k)]),
            lax.ppermute(below.astype(BF), "seq", [(ns - 1 - r, ns - 2 - r) for r in range(k)]),
        )

    def total(self):
        return self.chunk(lax.axis_index("seq")) + self.moved[0].astype(F32) + self.moved[1].astype(F32)


def natural(pieces, axis, size):
    pieces = list(pieces)
    for bit in bits_of(size):
        flip = my_bit(axis, bit) == 1
        out = list(pieces)
        for m in range(size):
            if not m & bit:
                out[m] = jnp.where(flip, pieces[m | bit], pieces[m])
                out[m | bit] = jnp.where(flip, pieces[m], pieces[m | bit])
        pieces = out
    return pieces


def exchange_start(blocks, ns):
    me = lax.axis_index("seq")
    return [pick(blocks, me, 0)] + [swap(pick(blocks, me ^ m, 0), "seq", m, ns) for m in range(1, ns)]


def join(pieces, axis, size):
    return jnp.concatenate(natural(pieces, axis, size), axis=0)


def xor_start(value, axis, size):
    return [value] + [swap(value, axis, m, size) for m in range(1, size)]


def double_start(have, bit, ns):
    return {**have, **{m | bit: swap(v, "seq", bit, ns) for m, v in have.items()}}


def block(nd, ns, tokens, patches, cameras, tri_items, patch_items, mod_weight, qkv_weight, self_out_weight, norm2_gain, norm2_bias, cross_q_weight, cross_kv_weight, cross_out_weight, norm3_gain, norm3_bias, mlp_in_weight, mlp_in_bias, mlp_out_weight, mlp_out_bias, cotangent):
    rows, width = tokens.shape
    heads_here = HEADS // ns
    cols_here = width // ns
    items = cameras.shape[0]
    seq = lax.axis_index("seq")

    seq_bits = bits_of(ns)[::-1]

    def over_dp(held):
        return lax.all_gather(join([held[m] for m in range(ns)], "seq", ns), "dp", axis=0, tiled=True)

    bundle = {0: jnp.concatenate([self_out_weight, cross_q_weight, cross_kv_weight, cross_out_weight], axis=1)}
    small = jnp.concatenate(
        [mod_weight.reshape(-1), norm2_gain, norm2_bias, norm3_gain, norm3_bias, mlp_out_bias, mlp_in_bias]
    )
    length = small.shape[0]
    small = jnp.pad(small, (0, -length % 2048)).reshape(-1, 128)
    qkv_cut = qkv_weight.reshape(qkv_weight.shape[0], 3, ns, cols_here).transpose(2, 0, 1, 3)
    qkv_cut = qkv_cut.reshape(ns, qkv_weight.shape[0], 3 * cols_here)

    ups, downs = [tokens], [tokens]
    qkv_mine = small_all = None
    todo = list(seq_bits)
    for k in range(1, ns):
        up, down = line_step(ups[-1], downs[-1], ns)
        if k == 1:
            small_got, qkv_got = xor_start(small, "seq", ns), exchange_start(qkv_cut, ns)
            bundle = double_start(bundle, todo.pop(0), ns)
            up, down, small_got, qkv_got, bundle = sync(up, down, small_got, qkv_got, bundle)
            qkv_mine = lax.all_gather(join(qkv_got, "seq", ns), "dp", axis=0, tiled=True)
        elif k == 2:
            small_got = xor_start(join(small_got, "seq", ns), "dp", nd)
            if todo:
                bundle = double_start(bundle, todo.pop(0), ns)
            up, down, small_got, bundle = sync(up, down, small_got, bundle)
            small_all = join(small_got, "dp", nd)
        else:
            up, down, small_all = sync(up, down, small_all)
        ups.append(up)
        downs.append(down)
    while todo:
        bundle = double_start(bundle, todo.pop(0), ns)
    if small_all is None:
        small_all = join(xor_start(join(small_got, "seq", ns), "dp", nd), "dp", nd)
    bundle = over_dp(bundle)
    small = small_all.reshape(nd * ns, -1)
    mod_n = mod_weight.size
    own = norm2_gain.shape[0]
    mod_full = small[:, :mod_n].reshape(-1, mod_weight.shape[1])
    vectors = [small[:, mod_n + n * own : mod_n + (n + 1) * own].reshape(1, -1).astype(F32) for n in range(5)]
    gain_two, bias_two, gain_three, bias_three, out_bias = vectors
    in_bias = small[:, mod_n + 5 * own : length].reshape(1, -1).astype(F32)

    tri_col, patch_col = tri_items.reshape(-1, 1), patch_items.reshape(-1, 1)
    my_col = lax.dynamic_slice_in_dim(tri_items, seq * rows, rows).reshape(-1, 1)

    mod_items = product_t(cameras, mod_full)
    token_all = line_join(ups, downs, ns)
    token_all, qkv_mine, patches, mlp_in_weight = sync(token_all, qkv_mine, patches, mlp_in_weight)
    patch_got = xor_start(patches, "seq", ns)
    act_one = modulate(token_all, tri_col, mod_items)
    w_in = double_start({0: mlp_in_weight}, seq_bits[0], ns)
    act_one, w_in = sync(act_one, w_in)
    for bit in seq_bits[1:]:
        w_in = double_start(w_in, bit, ns)
    qkv = product(act_one, qkv_mine).astype(BF)
    qkv, w_in, mlp_out_weight = sync(qkv, w_in, mlp_out_weight)
    w_in = over_dp(w_in)
    self_at = (0, cols_here, 2 * cols_here)
    self_mine, self_lse = attend(qkv, qkv, qkv, self_at, heads_here, tri_col, tri_col, items)
    self_mine, bundle, patch_got, mlp_out_weight = sync(self_mine, bundle, patch_got, mlp_out_weight)
    self_att = lax.all_to_all(self_mine, "seq", 0, 1, tiled=True)
    w_self_out = bundle[:, :width]
    w_cross_q = bundle[:, width : 2 * width]
    w_cross_kv = bundle[:, 2 * width : 4 * width]
    w_cross_out = bundle[:, 4 * width :]
    w_out = double_start({0: mlp_out_weight}, seq_bits[0], ns)
    patch_all = join(patch_got, "seq", ns)
    cross_kv = product(patch_all, w_cross_kv).astype(BF)
    self_att, cross_kv, w_out = sync(self_att, cross_kv, w_out)
    resid_in = tokens.astype(F32)
    resid_two = resid_in + product(self_att, w_self_out)

    unit_two, inv_two = norm_parts(resid_two)
    act_two = (unit_two * gain_two + bias_two).astype(BF)
    cross_q = product(act_two, w_cross_q).astype(BF)
    for bit in seq_bits[1:]:
        w_out = double_start(w_out, bit, ns)
    cross_q, w_out = sync(cross_q, w_out)
    w_out = over_dp(w_out)
    cross_at = (0, 0, width)
    cross_att, cross_lse = attend(cross_q, cross_kv, cross_kv, cross_at, HEADS, my_col, patch_col, items)
    resid_three = resid_two + product(cross_att, w_cross_out)

    unit_three, inv_three = norm_parts(resid_three)
    act_three = (unit_three * gain_three + bias_three).astype(BF)
    act_three, w_in = sync(act_three, w_in)
    hid, slope = mlp_up(act_three, w_in, in_bias)

    g_w_out = contract_rows(hid, cotangent).astype(BF)
    slope, g_w_out, w_out = sync(slope, g_w_out, w_out)
    g_w_out = to_dp(g_w_out)
    grad_out = cotangent.astype(F32)
    g_out_bias = jnp.sum(grad_out, axis=0)
    d_pre, g_in_bias = mlp_back(cotangent, w_out, slope)
    g_w_in = contract_rows(act_three, d_pre).astype(BF)
    d_pre, g_w_in = tie(d_pre, g_w_in)
    g_w_in = to_dp(g_w_in)
    d_act_three = product_t(d_pre, w_in)
    g_gain_three = jnp.sum(d_act_three * unit_three, axis=0)
    g_bias_three = jnp.sum(d_act_three, axis=0)
    d_resid_three = grad_out + norm_back(unit_three, inv_three, d_act_three * gain_three)

    d_cross_out = d_resid_three.astype(BF)
    d_cross = product_t(d_cross_out, w_cross_out).astype(BF)
    d_cq, d_ck, d_cv = attend_back(cross_q, cross_kv, cross_kv, cross_at, HEADS, my_col, patch_col, items, cross_att, cross_lse, d_cross)
    d_act_two = product_t(d_cq, w_cross_q)
    g_gain_two = jnp.sum(d_act_two * unit_two, axis=0)
    g_bias_two = jnp.sum(d_act_two, axis=0)
    d_resid_two = d_resid_three + norm_back(unit_two, inv_two, d_act_two * gain_two)

    d_self_out = d_resid_two.astype(BF)
    d_self = product_t(d_self_out, w_self_out).astype(BF)
    d_self_mine = lax.all_to_all(d_self, "seq", 1, 0, tiled=True)
    g_mid = weight_grads(
        [(self_att, d_self_out), (act_two, d_cq), (patch_all, d_ck), (patch_all, d_cv), (cross_att, d_cross_out)]
    )
    patch_part = (product_t(d_ck, w_cross_kv[:, :width]) + product_t(d_cv, w_cross_kv[:, width:])).astype(BF)
    block_out = (resid_three + product(hid, w_out) + out_bias).astype(BF)
    d_self_mine, g_mid, patch_part, block_out, g_w_out = sync(d_self_mine, g_mid, patch_part, block_out, g_w_out)

    def over_seq(value):
        return sum_xor(value.reshape((ns, -1) + value.shape[1:]), "seq", ns)

    g_mid = to_dp(g_mid)
    patch_sum, out_sum, in_sum = over_seq(patch_part), over_seq(g_w_out), None
    backs = []
    for first in range(0, heads_here, 2):
        back = attend_back(
            qkv, qkv, qkv, self_at, 2, tri_col, tri_col, items, self_mine, self_lse, d_self_mine, first=first
        )
        if in_sum is None:
            back, d_self_mine, g_w_in = sync(back, d_self_mine, g_w_in)
            in_sum = over_seq(g_w_in)
        backs.append(back)
    backs, patch_sum, out_sum = sync(backs, patch_sum, out_sum)
    d_q, d_k, d_v = (jnp.concatenate(p, axis=1) if len(p) > 1 else p[0] for p in zip(*backs))
    d_act_one_part, g_mod_items = modulate_back(d_q, d_k, d_v, qkv_mine, token_all, tri_col, items)
    d_act_one_part, g_mod_items, d_q, d_k, d_v, in_sum, patch_sum, out_sum = sync(
        d_act_one_part, g_mod_items, d_q, d_k, d_v, in_sum, patch_sum, out_sum
    )
    line = LineSum(d_act_one_part, ns)
    line.start()
    g_mod = lax.dot_general(
        g_mod_items, cameras.astype(F32), (((0,), (0,)), ((), ())), precision=lax.Precision.HIGHEST
    )
    n_dev = nd * ns
    tail = jnp.concatenate(
        [g_mod.reshape(n_dev, -1)]
        + [v.reshape(n_dev, -1) for v in (g_gain_two, g_bias_two, g_gain_three, g_bias_three, g_out_bias, g_in_bias)],
        axis=1,
    )
    tail_n = tail.shape[1]
    tail = jnp.pad(tail, ((0, 0), (0, -tail_n % 1024))).reshape(nd, ns, -1, 128)
    tail = sum_xor(tail, "dp", nd)
    g_qkv = weight_grads([(act_one, d_q), (act_one, d_k), (act_one, d_v)])
    g_qkv, line.moved, tail, patch_sum, out_sum, in_sum = sync(g_qkv, line.moved, tail, patch_sum, out_sum, in_sum)
    g_qkv = to_dp(g_qkv)
    for k in range(2, ns):
        line.start()
        if k == 2:
            tail = sum_xor(add_all(*tail), "seq", ns)
            patch_grad, g_w_out, g_w_in = add_all(*patch_sum), add_all(*out_sum), add_all(*in_sum)
            line.moved, tail, patch_grad, g_w_out, g_w_in, g_mid = sync(
                line.moved, tail, patch_grad, g_w_out, g_w_in, g_mid
            )
            g_mid = over_seq(g_mid)
            tail = add_all(*tail).reshape(-1)
    line.moved, g_mid, g_qkv = sync(line.moved, g_mid, g_qkv)
    d_act_one = line.total()
    g_mod = tail[:mod_n].reshape(mod_weight.shape)
    cut = [tail[mod_n + n * own : mod_n + (n + 1) * own] for n in range(5)]
    g_in_bias = tail[mod_n + 5 * own : tail_n]
    g_qkv = join(exchange_start(g_qkv.reshape(ns, -1, g_qkv.shape[1]), ns), "seq", ns).astype(F32)
    g_qkv = (
        g_qkv.reshape(ns, qkv_weight.shape[0], 3, cols_here)
        .transpose(1, 2, 0, 3)
        .reshape(qkv_weight.shape)
    )
    g_mid = add_all(*g_mid)
    unit_own, inv_own = norm_parts(resid_in)
    scale_own = per_item(my_col, mod_items[:, width:])
    input_grad = d_resid_two + norm_back(unit_own, inv_own, d_act_one * (1.0 + scale_own))
    return (
        block_out,
        input_grad,
        patch_grad,
        g_mod,
        g_qkv,
        g_mid[:, :width],
        cut[0],
        cut[1],
        g_mid[:, width : 2 * width],
        g_mid[:, 2 * width : 4 * width],
        g_mid[:, 4 * width :],
        cut[2],
        cut[3],
        g_w_in,
        g_in_bias,
        g_w_out,
        cut[4],
    )


def solution(mesh):
    nd, ns = mesh.shape["dp"], mesh.shape["seq"]
    rows2, rows1 = P(ALL, None), P(ALL)
    placed = (rows2, rows2, P("dp", None), P("dp"), P("dp"), rows2, rows2, rows2, rows1, rows1, rows2, rows2, rows2, rows1, rows1, rows2, rows1, rows2, rows1, rows2)
    given = (rows2, rows2, rows2, rows2, rows2, rows2, rows1, rows1, rows2, rows2, rows2, rows1, rows1, rows2, rows1, rows2, rows1)

    def shards(*args):
        return block(nd, ns, *args)

    return jax.shard_map(shards, mesh=mesh, in_specs=placed, out_specs=given, check_vma=False)
```

time: 1140 us -> 705 us (0.62)
  waiting for transfers between devices: 465 us -> 170 us
  local copies, waits for them, and re-layouts: 160 us -> 43 us
  blocking collectives: 58.8 us -> 0 us
  starting transfers between devices: 66.6 us -> 117 us
  matrix products: 133 us -> 84.9 us
  Pallas kernels: 177 us -> 221 us
  other arithmetic: 60.9 us -> 46.5 us
    unnamed x15 -> x8, waiting for transfers between devices: 188 us -> 0.13 us
    all_gather x9 -> x4, waiting for transfers between devices: 113 us -> 0.01 us  [the longest x3 0.01 us: over_dp(): lax.all_gather(join([held[m] for m in range(ns)], 'seq', ns), 'dp', axis=...]
    unnamed x191 -> x173, local copies, waits for them, and re-layouts: 78.2 us -> 14 us
    unnamed x1 -> x0, blocking collectives: 44.9 us -> none
    pallas_call x4 -> x11, Pallas kernels: 177 us -> 221 us  [the longest x3 80.5 us: attend_back(): pl.pallas_call(functools.partial(attend_back_kernel, items=items, kb=kb),...]
    ppermute x47 -> x50, waiting for transfers between devices: 160 us -> 122 us  [swap(): return lax.ppermute(value, axis, [(r, r ^ bit) for r in range(size)])]
    ppermute x0 -> x12, waiting for transfers between devices: none -> 36.3 us  [the longest x3 17.5 us: line_step(): lax.ppermute(up, 'seq', [(r, r + 1) for r in range(ns - 1)])]
    ppermute x0 -> x12, starting transfers between devices: none -> 35.2 us  [the longest x3 14.9 us: line_step(): lax.ppermute(up, 'seq', [(r, r + 1) for r in range(ns - 1)])]
  transfers between devices with their start and end apart: 63 -> 72, of which waited for: 32 -> 27; matrix products, arithmetic and copies ran while one was open for 27% -> 23% of each run, Pallas kernels for 13% -> 32%
where the time goes in v2:
time: 705 us; the launch traced here: 698 us
  Pallas kernels  221 us (31%)
  waiting for transfers between devices  170 us (24%)
  starting transfers between devices  117 us (17%)
  matrix products  84.9 us (12%)
  other arithmetic  46.5 us (7%)
  local copies, waits for them, and re-layouts  43 us (6%)
  between operations  15.7 us (2%)
    ppermute x50, waiting for transfers between devices, swap(): return lax.ppermute(value, axis, [(r, r ^ bit) for r in range(size)])  122 us
    pallas_call x3, Pallas kernels, attend_back(): pl.pallas_call(functools.partial(attend_back_kernel, items=items, kb=kb),...  80.5 us
    ppermute x50, starting transfers between devices, swap(): return lax.ppermute(value, axis, [(r, r ^ bit) for r in range(size)])  73.9 us
    pallas_call x2, Pallas kernels, attend(): pl.pallas_call(functools.partial(attend_kernel, items=items, heads=step),...  54.9 us
    pallas_call x2, Pallas kernels, weight_grads(): pl.pallas_call(functools.partial(grads_kernel, spans=tuple(spans)), grid=...  34.9 us
    dot_general x6, matrix products, product(): return jnp.dot(a, b, preferred_element_type=F32)  33.9 us
    dot_general x7, matrix products, product_t(): lax.dot_general(a, b, (((1,), (1,)), ((), ())), preferred_element_type=F32)  31.3 us
    dot_general x2, matrix products, contract_rows(): lax.dot_general(a, b, (((0,), (0,)), ((), ())), preferred_element_type=F32)  18.7 us
  transfers between devices with their start and end apart: 72, of which 27 were waited for; matrix products, arithmetic and copies ran while one was open for 23% of the time, Pallas kernels for 32%

profile of v2, /device:TPU:0, one launch (start us, length us, event | category | flops | bytes accessed | tf_op | source)
XLA Modules:
  0.0 697.6 jit_solution(17040126814144548505)
XLA Ops:
  7.3 5.0 collective-permute-start
  26.4 22.9 %collective-permute-done.4 = bf16[16,128]{1,0:T(8,128)(2,1)S(1)} collective-permute-done((bf16[16,128]{1,0:T(8,128)(2,1)S(1)}, bf16[16,128]{1,0:T(8,128)(2,1)S(1)}, u32[]{:S(2)}, u32[]{:S(2)}) %collective-permute-start.4) | collective-permute-done | bytes 4128 | tf_op jit(solution)/shard_map/ppermute | solution.py:412
  49.3 6.6 collective-permute-start.3
  70.7 5.5 collective-permute-start.9
  116.6 17.5 %collective-permute-done.20 = bf16[512,1024]{1,0:T(8,128)(2,1)S(1)} collective-permute-done((bf16[512,1024]{1,0:T(8,128)(2,1)}, bf16[512,1024]{1,0:T(8,128)(2,1)S(1)}, u32[]{:S(2)}, u32[]{:S(2)}) %collective-permute-start.20) | collective-permute-done | bytes 1048608 | tf_op jit(solution)/shard_map/ppermute | solution.py:456
  146.9 10.5 %modulate.1.refs_0_.refs_1_.refs_2_ = bf16[2048,1024]{1,0:T(8,128)(2,1)} custom-call(bf16[2048,1024]{1,0:T(8,128)(2,1)} %constant_dynamic-slice_fusion.6.x_ref, s32[2048,1]{1,0:T(8,128)} %copy.80.id_ref.qid_ref.kid_ref, f32[4,2048]{1,0:T(4,128)} %convolution_bitcast_fusion.mod_ref), custom_call_target="tpu_custom_call" | custom-call | flops 1 | bytes 1 | tf_op jit(solution)/shard_map/modulate/pallas_call | solution.py:297
  159.5 7.6 %convolution_convert_fusion.2.q_ref.k_ref.v_ref = bf16[2048,768]{1,0:T(8,128)(2,1)} fusion(bf16[2048,1024]{1,0:T(8,128)(2,1)} %modulate.1.refs_0_.refs_1_.refs_2_, bf16[1024,768]{1,0:T(8,128)(2,1)S(1)} %copy-done.24), kind=kOutput, calls=%fused_computation.6 | convolution fusion | flops 3222798336 | bytes 8912896 | tf_op jit(solution)/shard_map/dot_general | solution.py:24
  172.7 30.7 %attend.2 = (bf16[2048,256]{1,0:T(8,128)(2,1)}, f32[2,2,2048]{2,1,0:T(2,128)}) custom-call(bf16[2048,768]{1,0:T(8,128)(2,1)} %convolution_convert_fusion.2.q_ref.k_ref.v_ref, bf16[2048,768]{1,0:T(8,128)(2,1)} %convolution_convert_fusion.2.q_ref.k_ref.v_ref, bf16[2048,768]{1,0:T(8,128)(2,1)} %convolution_convert_fusion.2.q_ref.k_ref.v_ref, ...), custom_call_target="tpu_custom_call" | custom-call | flops 1 | bytes 1 | tf_op jit(solution)/shard_map/attend/pallas_call | solution.py:101
  203.4 7.2 %collective-permute-done.26 = bf16[256,1024]{1,0:T(8,128)(2,1)S(1)} collective-permute-done((bf16[256,1024]{1,0:T(8,128)(2,1)S(1)}, bf16[256,1024]{1,0:T(8,128)(2,1)S(1)}, u32[]{:S(2)}, u32[]{:S(2)}) %collective-permute-start.26) | collective-permute-done | bytes 524320 | tf_op jit(solution)/shard_map/ppermute | solution.py:412
  223.7 10.4 %fusion.2.k_ref.v_ref = bf16[1024,2048]{1,0:T(8,128)(2,1)} fusion(bf16[1024,5120]{1,0:T(8,128)(2,1)} %all-gather.7.cloned.1.call-done, bf16[256,1024]{1,0:T(8,128)(2,1)S(1)} %get-tuple-element.442, bf16[256,1024]{1,0:T(8,128)(2,1)S(1)} %get-tuple-element.441, bf16[256,1024]{1,0:T(8,128)(2,1)S(1)} %get-tuple-element.440, ...), kind=kOutput, calls=%fused_computation.5 | convolution fusion | flops 4305453056 | bytes 10485760 | tf_op jit(solution)/shard_map/dot_general | solution.py:24
  234.1 11.5 %all-to-all-done = bf16[4,512,256]{2,1,0:T(8,128)(2,1)S(1)} async-done(((bf16[4,512,256]{2,1,0:T(8,128)(2,1)}), bf16[4,512,256]{2,1,0:T(8,128)(2,1)S(1)}, u32[]{:S(2)}, u32[]{:S(2)}) %all-to-all-start) | async-done | bytes 1048608 | tf_op jit(solution)/shard_map/all_to_all | solution.py:595
  245.7 4.5 collective-permute-done.28
  269.3 24.3 %attend.3 = (bf16[512,1024]{1,0:T(8,128)(2,1)}, f32[8,2,512]{2,1,0:T(2,128)}) custom-call(bf16[512,1024]{1,0:T(8,128)(2,1)} %fusion.40.q_ref, bf16[1024,2048]{1,0:T(8,128)(2,1)} %fusion.2.k_ref.v_ref, bf16[1024,2048]{1,0:T(8,128)(2,1)} %fusion.2.k_ref.v_ref, s32[512,1]{1,0:T(8,128)} %copy.84.qid_ref, s32[1024,1]{1,0:T(8,128)} %copy.85.kid_ref), custom_call_target="tpu_custom_call" | custom-call | flops 1 | bytes 1 | tf_op jit(solution)/shard_map/attend/pallas_call | solution.py:101
  299.6 13.3 %mlp_up.1 = (bf16[512,4096]{1,0:T(8,128)(2,1)}, bf16[512,4096]{1,0:T(8,128)(2,1)}) custom-call(bf16[512,1024]{1,0:T(8,128)(2,1)} %add_convert_fusion.6.a_ref, bf16[1024,4096]{1,0:T(8,128)(2,1)} %all-gather.9.cloned.1.call-done.w_ref, f32[1,4096]{1,0:T(1,128)} %bitcast.159), custom_call_target="tpu_custom_call" | custom-call | flops 1 | bytes 1 | tf_op jit(solution)/shard_map/mlp_up/pallas_call | solution.py:220
  312.9 9.1 %convolution_convert_fusion.1 = bf16[4096,1024]{1,0:T(8,128)(2,1)} fusion(bf16[512,4096]{1,0:T(8,128)(2,1)} %get-tuple-element.241, bf16[512,1024]{1,0:T(8,128)(2,1)S(1)} %copy-done.15), kind=kOutput, calls=%fused_computation.1 | convolution fusion | flops 4299161600 | bytes 13631488 | tf_op jit(solution)/shard_map/dot_general | solution.py:32
  322.1 13.1 %mlp_back.1 = (bf16[512,4096]{1,0:T(8,128)(2,1)}, f32[1,4096]{1,0:T(1,128)}) custom-call(bf16[512,1024]{1,0:T(8,128)(2,1)} %g_ref.1, bf16[4096,1024]{1,0:T(8,128)(2,1)} %all-gather.11.cloned.1.call-done.w_ref, bf16[512,4096]{1,0:T(8,128)(2,1)} %get-tuple-element.247.slope_ref), custom_call_target="tpu_custom_call" | custom-call | flops 1 | bytes 1 | tf_op jit(solution)/shard_map/mlp_back/pallas_call | solution.py:247
  335.2 9.6 %convolution_convert_fusion = bf16[1024,4096]{1,0:T(8,128)(2,1)} fusion(bf16[512,1024]{1,0:T(8,128)(2,1)S(1)} %copy-done.13, bf16[512,4096]{1,0:T(8,128)(2,1)} %get-tuple-element.249), kind=kOutput, calls=%fused_computation | convolution fusion | flops 4299161600 | bytes 13631488 | tf_op jit(solution)/shard_map/dot_general | solution.py:32
  349.3 8.9 %multiply_reduce_fusion = (f32[1024]{0:T(1024)S(1)}, f32[512]{0:T(512)S(1)}, f32[512]{0:T(512)S(1)}, f32[1024]{0:T(1024)S(1)}, f32[512,1024]{1,0:T(8,128)S(1)}) fusion(f32[512,1024]{1,0:T(8,128)S(1)} %copy-done.3, f32[512]{0:T(512)S(1)} %add_rsqrt_fusion.1, f32[512]{0:T(512)S(1)} %broadcast_multiply_fusion.7, f32[1024]{0:T(1024)S(1)} %reshape.283, ...), kind=kOutput, calls=%fused_computation.28 | convolution fusion | flops 4299682816 | bytes 16797696 | tf_op jit(solution)/shard_map/dot_general | solution.py:28
  363.5 27.0 %attend_back.3 = (bf16[512,1024]{1,0:T(8,128)(2,1)}, bf16[1024,1024]{1,0:T(8,128)(2,1)}, bf16[1024,1024]{1,0:T(8,128)(2,1)}) custom-call(bf16[512,1024]{1,0:T(8,128)(2,1)} %fusion.40.q_ref, bf16[1024,2048]{1,0:T(8,128)(2,1)} %fusion.2.k_ref.v_ref, bf16[1024,2048]{1,0:T(8,128)(2,1)} %fusion.2.k_ref.v_ref, bf16[512,1024]{1,0:T(8,128)(2,1)} %fusion.43.do_ref, ...), custom_call_target="tpu_custom_call" | custom-call | flops 1 | bytes 1 | tf_op jit(solution)/shard_map/attend_back/pallas_call | solution.py:173
  404.2 20.6 %weight_grads.2 = bf16[1024,5120]{1,0:T(8,128)(2,1)} custom-call(bf16[512,1024]{1,0:T(8,128)(2,1)} %bitcast.147, bf16[512,1024]{1,0:T(8,128)(2,1)} %copy-done.12, bf16[1024,1024]{1,0:T(8,128)(2,1)} %pad_maximum_fusion.refs_2_.refs_3_, bf16[1024,1024]{1,0:T(8,128)(2,1)} %pad_maximum_fusion.refs_2_.refs_3_, ...), custom_call_target="tpu_custom_call" | custom-call | flops 1 | bytes 1 | tf_op jit(solution)/shard_map/weight_grads/pallas_call | solution.py:394
  424.9 4.7 fusion.14
  429.7 5.6 add_convert_fusion
  435.3 5.5 add_convert_fusion.5
  455.5 26.0 %attend_back.4 = (bf16[2048,128]{1,0:T(8,128)(2,1)}, bf16[2048,128]{1,0:T(8,128)(2,1)}, bf16[2048,128]{1,0:T(8,128)(2,1)}) custom-call(bf16[2048,768]{1,0:T(8,128)(2,1)} %convolution_convert_fusion.2.q_ref.k_ref.v_ref, bf16[2048,768]{1,0:T(8,128)(2,1)} %convolution_convert_fusion.2.q_ref.k_ref.v_ref, ...), custom_call_target="tpu_custom_call" | custom-call | flops 1 | bytes 1 | tf_op jit(solution)/shard_map/attend_back/pallas_call | solution.py:173
  481.5 27.4 %attend_back.5 = (bf16[2048,128]{1,0:T(8,128)(2,1)}, bf16[2048,128]{1,0:T(8,128)(2,1)}, bf16[2048,128]{1,0:T(8,128)(2,1)}) custom-call(bf16[2048,768]{1,0:T(8,128)(2,1)} %convolution_convert_fusion.2.q_ref.k_ref.v_ref, bf16[2048,768]{1,0:T(8,128)(2,1)} %convolution_convert_fusion.2.q_ref.k_ref.v_ref, ...), custom_call_target="tpu_custom_call" | custom-call | flops 1 | bytes 1 | tf_op jit(solution)/shard_map/attend_back/pallas_call | solution.py:173
  514.9 8.7 %collective-permute-done.34 = bf16[128,1024]{1,0:T(8,128)(2,1)S(1)} collective-permute-done((bf16[128,1024]{1,0:T(8,128)(2,1)S(1)}, bf16[128,1024]{1,0:T(8,128)(2,1)S(1)}, u32[]{:S(2)}, u32[]{:S(2)}) %collective-permute-start.34) | collective-permute-done | bytes 262176 | tf_op jit(solution)/shard_map/ppermute | solution.py:412
  530.3 14.0 %modulate_back.1 = (bf16[2048,1024]{1,0:T(8,128)(2,1)}, f32[4,2048]{1,0:T(4,128)}) custom-call(bf16[2048,256]{1,0:T(8,128)(2,1)} %copy-done.9, bf16[2048,256]{1,0:T(8,128)(2,1)} %copy-done.8, bf16[2048,256]{1,0:T(8,128)(2,1)} %copy-done.7, bf16[1024,768]{1,0:T(8,128)(2,1)} %all-gather.5.cloned.1.call-done.w_ref, ...), custom_call_target="tpu_custom_call" | custom-call | flops 1 | bytes 1 | tf_op jit(solution)/shard_map/modulate_back/pallas_call | solution.py:343
  564.7 14.3 %weight_grads.3 = bf16[1024,768]{1,0:T(8,128)(2,1)} custom-call(bf16[2048,1024]{1,0:T(8,128)(2,1)} %modulate.1.refs_0_.refs_1_.refs_2_, bf16[2048,1024]{1,0:T(8,128)(2,1)} %modulate.1.refs_0_.refs_1_.refs_2_, bf16[2048,1024]{1,0:T(8,128)(2,1)} %modulate.1.refs_0_.refs_1_.refs_2_, bf16[2048,256]{1,0:T(8,128)(2,1)} %copy-done.9, bf16[2048,256]{1,0:T(8,128)(2,1)} %copy-done.8, ...), custom_call_target="tpu_custom_call" | custom-call | flops 1 | bytes 1 | tf_op jit(solution)/shard_map/weight_grads/pallas_call | solution.py:394
  599.2 14.8 %collective-permute-done.49 = bf16[512,1024]{1,0:T(8,128)(2,1)} collective-permute-done((bf16[512,1024]{1,0:T(8,128)(2,1)}, bf16[512,1024]{1,0:T(8,128)(2,1)}, u32[]{:S(2)}, u32[]{:S(2)}) %collective-permute-start.49) | collective-permute-done | bytes 1048608 | tf_op jit(solution)/shard_map/ppermute | solution.py:485
  619.6 5.3 collective-permute-start.54
  632.3 25.2 %collective-permute-done.58 = bf16[32,5120]{1,0:T(8,128)(2,1)} collective-permute-done((bf16[32,5120]{1,0:T(8,128)(2,1)}, bf16[32,5120]{1,0:T(8,128)(2,1)}, u32[]{:S(2)}, u32[]{:S(2)}) %collective-permute-start.58) | collective-permute-done | bytes 327712 | tf_op jit(solution)/shard_map/ppermute | solution.py:412
  657.5 17.3 %collective-permute-done.57 = bf16[32,5120]{1,0:T(8,128)(2,1)} collective-permute-done((bf16[32,5120]{1,0:T(8,128)(2,1)}, bf16[32,5120]{1,0:T(8,128)(2,1)}, u32[]{:S(2)}, u32[]{:S(2)}) %collective-permute-start.57) | collective-permute-done | bytes 327712 | tf_op jit(solution)/shard_map/ppermute | solution.py:412
  (430 shorter events, 247.4 us)
Async XLA Ops:
  7.3 136.5 %all-gather.5.cloned.1.call-start = ((), (), s32[]{:S(2)}) async-start(), calls=%async_computation.6 | async-start | bytes 1769472 | tf_op jit(solution)/shard_map/all_gather | solution.py:553
  7.3 61.3 %collective-permute-start = (bf16[512,1024]{1,0:T(8,128)(2,1)}, bf16[512,1024]{1,0:T(8,128)(2,1)S(1)}, u32[]{:S(2)}, u32[]{:S(2)}) collective-permute-start(bf16[512,1024]{1,0:T(8,128)(2,1)} %param.20), channel_id=1, source_target_pairs={{0,1},{1,2},{2,3},{4,5},{5,6},{6,7},{8,9},{9,10},{10,11},{12,13},{... | collective-permute-start | bytes 3145736 | tf_op jit(solution)/shard_map/ppermute | solution.py:456
  12.3 56.3 %collective-permute-start.1 = (bf16[512,1024]{1,0:T(8,128)(2,1)}, bf16[512,1024]{1,0:T(8,128)(2,1)S(1)}, u32[]{:S(2)}, u32[]{:S(2)}) collective-permute-start(bf16[512,1024]{1,0:T(8,128)(2,1)} %param.20), channel_id=1, source_target_pairs={{1,0},{2,1},{3,2},{5,4},{6,5},{7,6},{9,8},{10,9},{11,10},{13,12},{... | collective-permute-start | bytes 3145736 | tf_op jit(solution)/shard_map/ppermute | solution.py:457
  17.1 51.6 %collective-permute-start.8 = (bf16[32,5120]{1,0:T(8,128)(2,1)S(1)}, bf16[32,5120]{1,0:T(8,128)(2,1)S(1)}, u32[]{:S(2)}, u32[]{:S(2)}) collective-permute-start(bf16[32,5120]{1,0:T(8,128)(2,1)S(1)} %constant_dynamic-update-slice_fusion), channel_id=1, source_target_pairs={{0,2},{1,3},{2,0},{3,1},{4,6},{5,7},{6,4},{7,5},{8,10},{9,11},{10,... | collective-permute-start | bytes 983048 | tf_op jit(solution)/shard_map/ppermute | solution.py:412
  22.1 41.9 %collective-permute-start.7 = (bf16[32,768]{1,0:T(8,128)(2,1)S(1)}, bf16[32,768]{1,0:T(8,128)(2,1)S(1)}, u32[]{:S(2)}, u32[]{:S(2)}) collective-permute-start(bf16[32,768]{1,0:T(8,128)(2,1)S(1)} %get-tuple-element.490), channel_id=1, source_target_pairs={{0,3},{1,2},{2,1},{3,0},{4,7},{5,6},{6,5},{7,4},{8,11},{9,10},{10,... | collective-permute-start | bytes 147464 | tf_op jit(solution)/shard_map/ppermute | solution.py:412
  69.4 37.4 %collective-permute-start.10 = (bf16[512,1024]{1,0:T(8,128)(2,1)S(1)}, bf16[512,1024]{1,0:T(8,128)(2,1)S(1)}, u32[]{:S(2)}, u32[]{:S(2)}) collective-permute-start(bf16[512,1024]{1,0:T(8,128)(2,1)S(1)} %collective-permute-done.1), channel_id=1, source_target_pairs={{1,0},{2,1},{3,2},{5,4},{6,5},{7,6},{9,8},{10,9},{11,10},{13,12},{... | collective-permute-start | bytes 3145736 | tf_op jit(solution)/shard_map/ppermute | solution.py:457
  70.7 36.1 %collective-permute-start.9 = (bf16[512,1024]{1,0:T(8,128)(2,1)S(1)}, bf16[512,1024]{1,0:T(8,128)(2,1)}, u32[]{:S(2)}, u32[]{:S(2)}) collective-permute-start(bf16[512,1024]{1,0:T(8,128)(2,1)S(1)} %collective-permute-done), channel_id=1, source_target_pairs={{0,1},{1,2},{2,3},{4,5},{5,6},{6,7},{8,9},{9,10},{10,11},{12,13},{... | collective-permute-start | bytes 3145736 | tf_op jit(solution)/shard_map/ppermute | solution.py:456
  77.8 133.6 %all-gather.7.cloned.1.call-start = ((), (), s32[]{:S(2)}) async-start(), calls=%async_computation.7 | async-start | bytes 11796480 | tf_op jit(solution)/shard_map/all_gather | solution.py:533
  110.1 189.6 %all-gather.9.cloned.1.call-start = ((), (), s32[]{:S(2)}) async-start(), calls=%async_computation.8 | async-start | bytes 9437184 | tf_op jit(solution)/shard_map/all_gather | solution.py:533
  168.3 35.1 %collective-permute-start.27 = (bf16[256,1024]{1,0:T(8,128)(2,1)S(1)}, bf16[256,1024]{1,0:T(8,128)(2,1)S(1)}, u32[]{:S(2)}, u32[]{:S(2)}) collective-permute-start(bf16[256,1024]{1,0:T(8,128)(2,1)S(1)} %copy-done.31), channel_id=1, source_target_pairs={{0,3},{1,2},{2,1},{3,0},{4,7},{5,6},{6,5},{7,4},{8,11},{9,10},{10,... | collective-permute-start | bytes 1572872 | tf_op jit(solution)/shard_map/ppermute | solution.py:412
  171.1 39.5 %collective-permute-start.26 = (bf16[256,1024]{1,0:T(8,128)(2,1)S(1)}, bf16[256,1024]{1,0:T(8,128)(2,1)S(1)}, u32[]{:S(2)}, u32[]{:S(2)}) collective-permute-start(bf16[256,1024]{1,0:T(8,128)(2,1)S(1)} %copy-done.31), channel_id=1, source_target_pairs={{0,2},{1,3},{2,0},{3,1},{4,6},{5,7},{6,4},{7,5},{8,10},{9,11},{10,... | collective-permute-start | bytes 1572872 | tf_op jit(solution)/shard_map/ppermute | solution.py:412
  172.1 39.3 %collective-permute-start.25 = (bf16[256,1024]{1,0:T(8,128)(2,1)S(1)}, bf16[256,1024]{1,0:T(8,128)(2,1)}, u32[]{:S(2)}, u32[]{:S(2)}) collective-permute-start(bf16[256,1024]{1,0:T(8,128)(2,1)S(1)} %copy-done.31), channel_id=1, source_target_pairs={{0,1},{1,0},{2,3},{3,2},{4,5},{5,4},{6,7},{7,6},{8,9},{9,8},{10,11... | collective-permute-start | bytes 1572872 | tf_op jit(solution)/shard_map/ppermute | solution.py:412
  211.4 34.2 %all-to-all-start = ((bf16[4,512,256]{2,1,0:T(8,128)(2,1)}), bf16[4,512,256]{2,1,0:T(8,128)(2,1)S(1)}, u32[]{:S(2)}, u32[]{:S(2)}) async-start(bf16[4,512,256]{2,1,0:T(8,128)(2,1)} %bitcast.141), calls=%async_computation | async-start | bytes 2097152 | tf_op jit(solution)/shard_map/all_to_all | solution.py:595
  215.1 107.0 %all-gather.11.cloned.1.call-start = ((), (), s32[]{:S(2)}) async-start(), calls=%async_computation.9 | async-start | bytes 9437184 | tf_op jit(solution)/shard_map/all_gather | solution.py:533
  218.0 32.3 %collective-permute-start.28 = (bf16[128,1024]{1,0:T(8,128)(2,1)S(1)}, bf16[128,1024]{1,0:T(8,128)(2,1)}, u32[]{:S(2)}, u32[]{:S(2)}) collective-permute-start(bf16[128,1024]{1,0:T(8,128)(2,1)S(1)} %copy-done.46), channel_id=1, source_target_pairs={{0,2},{1,3},{2,0},{3,1},{4,6},{5,7},{6,4},{7,5},{8,10},{9,11},{10,... | collective-permute-start | bytes 786440 | tf_op jit(solution)/shard_map/ppermute | solution.py:412
  265.3 175.5 %reduce-scatter.5.cloned.1.call-start = ((), (), s32[]{:S(2)}) async-start(), calls=%async_computation.10 | async-start | bytes 9437184 | tf_op jit(solution)/shard_map/reduce_scatter | solution.py:447
  322.1 159.4 %reduce-scatter.7.cloned.1.call-start = ((), (), s32[]{:S(2)}) async-start(), calls=%async_computation.11 | async-start | bytes 9437184 | tf_op jit(solution)/shard_map/reduce_scatter | solution.py:447
  400.7 40.1 %all-to-all-start.1 = ((bf16[512,4,256]{2,0,1:T(8,128)(2,1)}), bf16[512,4,256]{2,0,1:T(8,128)(2,1)S(1)}, u32[]{:S(2)}, u32[]{:S(2)}) async-start(bf16[512,4,256]{2,0,1:T(8,128)(2,1)} %bitcast.139), calls=%async_computation.1 | async-start | bytes 2097152 | tf_op jit(solution)/shard_map/all_to_all | solution.py:647
  404.2 209.7 %reduce-scatter.9.cloned.1.call-start = ((), (), s32[]{:S(2)}) async-start(), calls=%async_computation.12 | async-start | bytes 11796480 | tf_op jit(solution)/shard_map/reduce_scatter | solution.py:447
  441.7 190.5 %reduce-scatter.11.cloned.1.call-start = ((), (), s32[]{:S(2)}) async-start(), calls=%async_computation.13 | async-start | bytes 1769472 | tf_op jit(solution)/shard_map/reduce_scatter | solution.py:447
  443.3 65.7 %collective-permute-start.36 = (bf16[128,1024]{1,0:T(8,128)(2,1)}, bf16[128,1024]{1,0:T(8,128)(2,1)}, u32[]{:S(2)}, u32[]{:S(2)}) collective-permute-start(bf16[128,1024]{1,0:T(8,128)(2,1)} %get-tuple-element.456), channel_id=1, source_target_pairs={{0,3},{1,2},{2,1},{3,0},{4,7},{5,6},{6,5},{7,4},{8,11},{9,10},{10,... | collective-permute-start | bytes 786440 | tf_op jit(solution)/shard_map/ppermute | solution.py:412
  448.4 75.6 %collective-permute-start.33 = (bf16[256,1024]{1,0:T(8,128)(2,1)}, bf16[256,1024]{1,0:T(8,128)(2,1)S(1)}, u32[]{:S(2)}, u32[]{:S(2)}) collective-permute-start(bf16[256,1024]{1,0:T(8,128)(2,1)} %get-tuple-element.435), channel_id=1, source_target_pairs={{0,3},{1,2},{2,1},{3,0},{4,7},{5,6},{6,5},{7,4},{8,11},{9,10},{10,... | collective-permute-start | bytes 1572872 | tf_op jit(solution)/shard_map/ppermute | solution.py:412
  448.6 77.9 %collective-permute-start.32 = (bf16[256,1024]{1,0:T(8,128)(2,1)}, bf16[256,1024]{1,0:T(8,128)(2,1)S(1)}, u32[]{:S(2)}, u32[]{:S(2)}) collective-permute-start(bf16[256,1024]{1,0:T(8,128)(2,1)} %get-tuple-element.436), channel_id=1, source_target_pairs={{0,2},{1,3},{2,0},{3,1},{4,6},{5,7},{6,4},{7,5},{8,10},{9,11},{10,... | collective-permute-start | bytes 1572872 | tf_op jit(solution)/shard_map/ppermute | solution.py:412
  449.6 76.9 %collective-permute-start.31 = (bf16[256,1024]{1,0:T(8,128)(2,1)}, bf16[256,1024]{1,0:T(8,128)(2,1)}, u32[]{:S(2)}, u32[]{:S(2)}) collective-permute-start(bf16[256,1024]{1,0:T(8,128)(2,1)} %get-tuple-element.437), channel_id=1, source_target_pairs={{0,1},{1,0},{2,3},{3,2},{4,5},{5,4},{6,7},{7,6},{8,9},{9,8},{10,11... | collective-permute-start | bytes 1572872 | tf_op jit(solution)/shard_map/ppermute | solution.py:412
  455.5 57.0 %collective-permute-start.35 = (bf16[128,1024]{1,0:T(8,128)(2,1)}, bf16[128,1024]{1,0:T(8,128)(2,1)}, u32[]{:S(2)}, u32[]{:S(2)}) collective-permute-start(bf16[128,1024]{1,0:T(8,128)(2,1)} %get-tuple-element.457), channel_id=1, source_target_pairs={{0,2},{1,3},{2,0},{3,1},{4,6},{5,7},{6,4},{7,5},{8,10},{9,11},{10,... | collective-permute-start | bytes 786440 | tf_op jit(solution)/shard_map/ppermute | solution.py:412
  512.5 31.8 %collective-permute-start.39 = (bf16[32,4096]{1,0:T(8,128)(2,1)}, bf16[32,4096]{1,0:T(8,128)(2,1)}, u32[]{:S(2)}, u32[]{:S(2)}) collective-permute-start(bf16[32,4096]{1,0:T(8,128)(2,1)} %get-tuple-element.452), channel_id=1, source_target_pairs={{0,3},{1,2},{2,1},{3,0},{4,7},{5,6},{6,5},{7,4},{8,11},{9,10},{10,... | collective-permute-start | bytes 786440 | tf_op jit(solution)/shard_map/ppermute | solution.py:412
  547.0 31.9 %collective-permute-start.41 = (bf16[512,1024]{1,0:T(8,128)(2,1)}, bf16[512,1024]{1,0:T(8,128)(2,1)}, u32[]{:S(2)}, u32[]{:S(2)}) collective-permute-start(bf16[512,1024]{1,0:T(8,128)(2,1)} %get-tuple-element.433), channel_id=1, source_target_pairs={{3,2},{7,6},{11,10},{15,14},{19,18},{23,22},{27,26},{31,30}} | collective-permute-start | bytes 3145736 | tf_op jit(solution)/shard_map/ppermute | solution.py:486
  618.2 56.6 %collective-permute-start.55 = (bf16[512,1024]{1,0:T(8,128)(2,1)}, bf16[512,1024]{1,0:T(8,128)(2,1)S(1)}, u32[]{:S(2)}, u32[]{:S(2)}) collective-permute-start(bf16[512,1024]{1,0:T(8,128)(2,1)} %get-tuple-element.429), channel_id=1, source_target_pairs={{3,2},{2,1},{1,0},{7,6},{6,5},{5,4},{11,10},{10,9},{9,8},{15,14},{... | collective-permute-start | bytes 3145736 | tf_op jit(solution)/shard_map/ppermute | solution.py:486
  619.6 55.2 %collective-permute-start.54 = (bf16[512,1024]{1,0:T(8,128)(2,1)}, bf16[512,1024]{1,0:T(8,128)(2,1)S(1)}, u32[]{:S(2)}, u32[]{:S(2)}) collective-permute-start(bf16[512,1024]{1,0:T(8,128)(2,1)} %get-tuple-element.430), channel_id=1, source_target_pairs={{0,1},{1,2},{2,3},{4,5},{5,6},{6,7},{8,9},{9,10},{10,11},{12,13},{... | collective-permute-start | bytes 3145736 | tf_op jit(solution)/shard_map/ppermute | solution.py:485
  625.9 31.6 %collective-permute-start.58 = (bf16[32,5120]{1,0:T(8,128)(2,1)}, bf16[32,5120]{1,0:T(8,128)(2,1)}, u32[]{:S(2)}, u32[]{:S(2)}) collective-permute-start(bf16[32,5120]{1,0:T(8,128)(2,1)} %get-tuple-element.443), channel_id=1, source_target_pairs={{0,3},{1,2},{2,1},{3,0},{4,7},{5,6},{6,5},{7,4},{8,11},{9,10},{10,... | collective-permute-start | bytes 983048 | tf_op jit(solution)/shard_map/ppermute | solution.py:412
  628.5 46.3 %collective-permute-start.57 = (bf16[32,5120]{1,0:T(8,128)(2,1)}, bf16[32,5120]{1,0:T(8,128)(2,1)}, u32[]{:S(2)}, u32[]{:S(2)}) collective-permute-start(bf16[32,5120]{1,0:T(8,128)(2,1)} %get-tuple-element.444), channel_id=1, source_target_pairs={{0,2},{1,3},{2,0},{3,1},{4,6},{5,7},{6,4},{7,5},{8,10},{9,11},{10,... | collective-permute-start | bytes 983048 | tf_op jit(solution)/shard_map/ppermute | solution.py:412
  629.7 45.1 %collective-permute-start.56 = (bf16[32,5120]{1,0:T(8,128)(2,1)}, bf16[32,5120]{1,0:T(8,128)(2,1)}, u32[]{:S(2)}, u32[]{:S(2)}) collective-permute-start(bf16[32,5120]{1,0:T(8,128)(2,1)} %get-tuple-element.445), channel_id=1, source_target_pairs={{0,1},{1,0},{2,3},{3,2},{4,5},{5,4},{6,7},{7,6},{8,9},{9,8},{10,11... | collective-permute-start | bytes 983048 | tf_op jit(solution)/shard_map/ppermute | solution.py:412
  (120 other events, 1264.3 us)
Sparse Core Ops, SparseCore 0:
  77.9 24.8 all-gather.4
  110.2 64.7 all-gather.6
  176.9 54.3 all-gather.8
  265.4 52.8 all-gather.10
  322.2 70.6 reduce-scatter.4
  396.6 71.2 reduce-scatter.6
  471.4 81.5 reduce-scatter.8
  592.4 36.9 reduce-scatter.10

commit v3 on v2

--- a/solution.py
+++ b/solution.py
@@ -39,33 +39,26 @@
     return pltpu.CompilerParams(vmem_limit_bytes=VMEM_LIMIT)
 
 
-def head_lanes(rows, h):
-    lane = lax.broadcasted_iota(jnp.int32, (rows, PAIR), 1)
-    return (lane < HEAD, lane - HEAD) if h == 0 else (lane >= HEAD, lane)
+def query_tags(ids, items):
+    slot = lax.broadcasted_iota(jnp.int32, (ids.shape[0], PAIR), 1) % HEAD
+    return jnp.where((slot != ids[:, None]) & (slot < items), NEG, 0.0).astype(BF)
+
+
+def key_tags(ids):
+    slot = lax.broadcasted_iota(jnp.int32, (ids.shape[0], PAIR), 1) % HEAD
+    return jnp.where(slot == ids[:, None], 1.0, 0.0).astype(BF)
+
+
+def in_head(value, h, other):
+    lane = lax.broadcasted_iota(jnp.int32, value.shape, 1)
+    return jnp.where((lane < HEAD) if h == 0 else (lane >= HEAD), value, other)
 
 
 def only_head(value, h):
-    mine, _ = head_lanes(value.shape[0], h)
-    return jnp.where(mine, value, jnp.zeros_like(value))
-
-
-def tag_query(q, ids, h, items):
-    mine, slot = head_lanes(q.shape[0], h)
-    barred = jnp.where((slot != ids) & (slot >= 0) & (slot < items), NEG, 0.0)
-    return jnp.where(mine, q.astype(F32), barred).astype(BF)
-
-
-def tag_key(k, ids, h):
-    mine, slot = head_lanes(k.shape[0], h)
-    return jnp.where(mine, k.astype(F32), jnp.where(slot == ids, 1.0, 0.0)).astype(BF)
-
-
-def with_ones(v, h):
-    mine, _ = head_lanes(v.shape[0], h)
-    return jnp.where(mine, v, jnp.ones_like(v))
-
-
-def attend_kernel(q_ref, k_ref, v_ref, qid_ref, kid_ref, o_ref, lse_ref, key_ref, val_ref, *, items, heads):
+    return in_head(value, h, jnp.zeros_like(value))
+
+
+def attend_kernel(q_ref, k_ref, v_ref, qtag_ref, ktag_ref, o_ref, lse_ref, key_ref, val_ref, *, heads):
     qb = q_ref.shape[0]
 
     @pl.when(pl.program_id(1) == 0)
@@ -73,14 +66,14 @@
         for p in range(heads // 2):
             lanes = slice(p * PAIR, (p + 1) * PAIR)
             for h in range(2):
-                key_ref[2 * p + h] = tag_key(k_ref[:, lanes], kid_ref[...], h)
-                val_ref[2 * p + h] = with_ones(v_ref[:, lanes], h)
+                key_ref[2 * p + h] = in_head(k_ref[:, lanes], h, ktag_ref[...])
+                val_ref[2 * p + h] = in_head(v_ref[:, lanes], h, jnp.ones_like(ktag_ref))
 
     for p in range(heads // 2):
         lanes = slice(p * PAIR, (p + 1) * PAIR)
         sums, tops = [], []
         for h in range(2):
-            scores = product_t(tag_query(q_ref[:, lanes], qid_ref[...], h, items), key_ref[2 * p + h])
+            scores = product_t(in_head(q_ref[:, lanes], h, qtag_ref[...]), key_ref[2 * p + h])
             top = jnp.max(scores, axis=1, keepdims=True)
             probs = jnp.exp2((scores - top) * SOFT).astype(BF)
             sums.append(product(probs, val_ref[2 * p + h]))
@@ -92,21 +85,21 @@
         lse_ref[p] = jnp.concatenate([lse[0:1], lse[HEAD : HEAD + 1]], axis=0)
 
 
-def attend(q, k, v, starts, heads, q_ids, k_ids, items, first=0):
+def attend(q, k, v, starts, heads, q_tags, k_tags):
     nq, nk = q.shape[0], k.shape[0]
     step = min(4, heads)
     cols = step * HEAD
-    qb = min(256, nq)
-    q_off, k_off, v_off = (s // cols + first // step for s in starts)
+    qb = min(256 * max(1, 2048 // nk), nq)
+    q_off, k_off, v_off = (s // cols for s in starts)
     return pl.pallas_call(
-        functools.partial(attend_kernel, items=items, heads=step),
+        functools.partial(attend_kernel, heads=step),
         grid=(heads // step, nq // qb),
         in_specs=[
             pl.BlockSpec((qb, cols), lambda p, i: (i, q_off + p)),
             pl.BlockSpec((nk, cols), lambda p, i: (0, k_off + p)),
             pl.BlockSpec((nk, cols), lambda p, i: (0, v_off + p)),
-            pl.BlockSpec((qb, 1), lambda p, i: (i, 0)),
-            pl.BlockSpec((nk, 1), lambda p, i: (0, 0)),
+            pl.BlockSpec((qb, PAIR), lambda p, i: (i, 0)),
+            pl.BlockSpec((nk, PAIR), lambda p, i: (0, 0)),
         ],
         out_specs=[
             pl.BlockSpec((qb, cols), lambda p, i: (i, p)),
@@ -120,10 +113,10 @@
         compiler_params=kernel_params(),
         cost_estimate=SHORT,
         name="attend",
-    )(q, k, v, q_ids, k_ids)
-
-
-def attend_back_kernel(q_ref, k_ref, v_ref, do_ref, o_ref, lse_ref, qid_ref, kid_ref, dq_ref, dk_ref, dv_ref, key_ref, kt_ref, dk_sum, dv_sum, *, items, kb):
+    )(q, k, v, q_tags, k_tags)
+
+
+def attend_back_kernel(q_ref, k_ref, v_ref, do_ref, o_ref, lse_ref, qtag_ref, ktag_ref, dq_ref, dk_ref, dv_ref, key_ref, kt_ref, dk_sum, dv_sum, *, kb):
     i = pl.program_id(1)
     nk = k_ref.shape[0]
 
@@ -131,7 +124,7 @@
     def _():
         kt_ref[...] = k_ref[...].T
         for h in range(2):
-            key_ref[h] = tag_key(k_ref[...], kid_ref[...], h)
+            key_ref[h] = in_head(k_ref[...], h, ktag_ref[...])
         dk_sum[...] = jnp.zeros(dk_sum.shape, F32)
         dv_sum[...] = jnp.zeros(dv_sum.shape, F32)
 
@@ -139,7 +132,7 @@
     both = (do.astype(F32) * o_ref[...].astype(F32)).T
     q_own = [only_head(q, h) for h in range(2)]
     do_own = [only_head(do, h) for h in range(2)]
-    q_tag = [tag_query(q, qid_ref[...], h, items) for h in range(2)]
+    q_tag = [in_head(q, h, qtag_ref[...]) for h in range(2)]
     delta = [jnp.sum(both[h * HEAD : (h + 1) * HEAD], axis=0, keepdims=True) for h in range(2)]
     dq = [None, None]
     for j in range(nk // kb):
@@ -163,7 +156,7 @@
         dv_ref[...] = dv_sum[...].astype(BF)
 
 
-def attend_back(q, k, v, starts, heads, q_ids, k_ids, items, out, lse, grad_out, first=0):
+def attend_back(q, k, v, starts, heads, q_tags, k_tags, out, lse, grad_out, first=0):
     nq, nk = q.shape[0], k.shape[0]
     pairs = heads // 2
     qb, kb = min(512, nq), min(2048, nk)
@@ -171,7 +164,7 @@
     q_off, k_off, v_off = (s // PAIR + base for s in starts)
     mine = pl.BlockSpec((qb, PAIR), lambda p, i: (i, p + base))
     return pl.pallas_call(
-        functools.partial(attend_back_kernel, items=items, kb=kb),
+        functools.partial(attend_back_kernel, kb=kb),
         grid=(pairs, nq // qb),
         in_specs=[
             pl.BlockSpec((qb, PAIR), lambda p, i: (i, q_off + p)),
@@ -180,8 +173,8 @@
             mine,
             mine,
             pl.BlockSpec((1, 2, qb), lambda p, i: (p + base, 0, i)),
-            pl.BlockSpec((qb, 1), lambda p, i: (i, 0)),
-            pl.BlockSpec((nk, 1), lambda p, i: (0, 0)),
+            pl.BlockSpec((qb, PAIR), lambda p, i: (i, 0)),
+            pl.BlockSpec((nk, PAIR), lambda p, i: (0, 0)),
         ],
         out_specs=[
             pl.BlockSpec((qb, PAIR), lambda p, i: (i, p)),
@@ -202,7 +195,7 @@
         compiler_params=kernel_params(),
         cost_estimate=SHORT,
         name="attend_back",
-    )(q, k, v, grad_out, out, lse, q_ids, k_ids)
+    )(q, k, v, grad_out, out, lse, q_tags, k_tags)
 
 
 def mlp_up_kernel(a_ref, w_ref, b_ref, hid_ref, slope_ref):
@@ -282,8 +275,15 @@
     return out
 
 
-def modulate_kernel(x_ref, id_ref, mod_ref, out_ref):
-    width = x_ref.shape[1]
+def modulate_kernel(me_ref, *refs, per, offsets):
+    pieces, (id_ref, mod_ref, out_ref, x_ref) = refs[:-4], refs[-4:]
+    width = out_ref.shape[1]
+    block = pl.program_id(0) // per
+    for off, piece in zip(offsets, pieces):
+        @pl.when(me_ref[0] + off == block)
+        def _():
+            x_ref[...] = piece[...]
+
     unit, _ = norm_parts(x_ref[...].astype(F32))
     ids = id_ref[...]
     shift = per_item(ids, mod_ref[:, :width])
@@ -291,23 +291,32 @@
     out_ref[...] = (unit * (1.0 + scale) + shift).astype(BF)
 
 
-def modulate(x, ids, mod_items):
-    rows, width = x.shape
-    rb = 256
+def modulate(pieces, offsets, me, ids, mod_items):
+    rows, width = pieces[0].shape
+    rb = min(256, rows)
+    per = rows // rb
+    total = ids.shape[0]
+    block = pl.BlockSpec((rb, width), lambda i, me: (i, 0))
     return pl.pallas_call(
-        modulate_kernel,
-        grid=(rows // rb,),
-        in_specs=[
-            pl.BlockSpec((rb, width), lambda i: (i, 0)),
-            pl.BlockSpec((rb, 1), lambda i: (i, 0)),
-            pl.BlockSpec(mod_items.shape, lambda i: (0, 0)),
-        ],
-        out_specs=pl.BlockSpec((rb, width), lambda i: (i, 0)),
-        out_shape=jax.ShapeDtypeStruct((rows, width), BF),
+        functools.partial(modulate_kernel, per=per, offsets=offsets),
+        grid_spec=pltpu.PrefetchScalarGridSpec(
+            num_scalar_prefetch=1,
+            grid=(total // rb,),
+            in_specs=[
+                pl.BlockSpec((rb, width), lambda i, me, off=off: (jnp.where(me[0] + off == i // per, i % per, 0), 0))
+                for off in offsets
+            ]
+            + [
+                pl.BlockSpec((rb, 1), lambda i, me: (i, 0)),
+                pl.BlockSpec(mod_items.shape, lambda i, me: (0, 0)),
+            ],
+            out_specs=[block, block],
+        ),
+        out_shape=[jax.ShapeDtypeStruct((total, width), BF)] * 2,
         compiler_params=kernel_params(),
         cost_estimate=SHORT,
         name="modulate",
-    )(x, ids, mod_items)
+    )(me.reshape(1), *pieces, ids, mod_items)
 
 
 def modulate_back_kernel(dq_ref, dk_ref, dv_ref, w_ref, x_ref, id_ref, out_ref, sum_ref):
@@ -408,62 +417,54 @@
     return [1 << b for b in range(size.bit_length() - 1)]
 
 
-def swap(value, axis, bit, size):
-    return lax.ppermute(value, axis, [(r, r ^ bit) for r in range(size)])
-
-
-def my_bit(axis, bit):
-    return (lax.axis_index(axis) // bit) % 2
+class Axis:
+    def __init__(self, name, length, size, me, flip):
+        self.name, self.length, self.size, self.me, self.flip = name, length, size, me, flip
+
+    def send(self, value, m):
+        return lax.ppermute(value, self.name, [(r, r ^ self.flip(m)) for r in range(self.length)])
+
+    def mine(self, bit):
+        return (self.me // bit) % 2
 
 
 def pick(value, index, where):
     return lax.dynamic_index_in_dim(value, index, where, keepdims=False)
 
 
-def tie(first, rest):
-    kept, rest = lax.optimization_barrier((first, rest))
-    return kept, rest
-
-
-def sum_xor(value, axis, size):
-    me = lax.axis_index(axis)
-    got = [swap(pick(value, me ^ m, 0), axis, m, size) for m in range(1, size)]
-    return pick(value, me, 0), got
-
-
-def add_all(own, got, dtype=F32):
-    total = own.astype(F32)
-    for value in got:
-        total = total + value.astype(F32)
-    return total.astype(dtype)
-
-
-def gather_xor(value, axis, size):
-    have = [value] + [swap(value, axis, m, size) for m in range(1, size)]
-    return jnp.concatenate(natural(have, axis, size), axis=0)
-
-
-def to_dp(whole):
-    return lax.psum_scatter(whole, "dp", scatter_dimension=0, tiled=True)
-
-
 def sync(*values):
     return lax.optimization_barrier(values)
 
 
-def line_step(up, down, ns):
-    return (
-        lax.ppermute(up, "seq", [(r, r + 1) for r in range(ns - 1)]),
-        lax.ppermute(down, "seq", [(r + 1, r) for r in range(ns - 1)]),
-    )
-
-
-def line_join(ups, downs, ns):
-    turned = [ups[0]] + [downs[r] + ups[ns - r] for r in range(1, ns)]
-    rows = ups[0].shape[0]
-    twice = jnp.concatenate(turned + turned[:-1], axis=0)
-    first = (ns - lax.axis_index("seq")) % ns
-    return lax.dynamic_slice_in_dim(twice, first * rows, ns * rows)
+def natural(pieces, axis):
+    pieces = list(pieces)
+    for bit in bits_of(axis.size):
+        flip = axis.mine(bit) == 1
+        out = list(pieces)
+        for m in range(axis.size):
+            if not m & bit:
+                out[m] = jnp.where(flip, pieces[m | bit], pieces[m])
+                out[m | bit] = jnp.where(flip, pieces[m], pieces[m | bit])
+        pieces = out
+    return pieces
+
+
+def join(pieces, axis):
+    if isinstance(pieces, dict):
+        pieces = [pieces[m] for m in range(axis.size)]
+    return jnp.concatenate(natural(pieces, axis), axis=0)
+
+
+def exchange_start(blocks, axis):
+    return [pick(blocks, axis.me ^ m, 0) if m == 0 else axis.send(pick(blocks, axis.me ^ m, 0), m) for m in range(axis.size)]
+
+
+def xor_start(value, axis):
+    return [value] + [axis.send(value, m) for m in range(1, axis.size)]
+
+
+def double_start(have, bit, axis):
+    return {**have, **{m | bit: axis.send(v, bit) for m, v in have.items()}}
 
 
 class LineSum:
@@ -490,34 +491,22 @@
         return self.chunk(lax.axis_index("seq")) + self.moved[0].astype(F32) + self.moved[1].astype(F32)
 
 
-def natural(pieces, axis, size):
-    pieces = list(pieces)
-    for bit in bits_of(size):
-        flip = my_bit(axis, bit) == 1
-        out = list(pieces)
-        for m in range(size):
-            if not m & bit:
-                out[m] = jnp.where(flip, pieces[m | bit], pieces[m])
-                out[m | bit] = jnp.where(flip, pieces[m], pieces[m | bit])
-        pieces = out
-    return pieces
-
-
-def exchange_start(blocks, ns):
-    me = lax.axis_index("seq")
-    return [pick(blocks, me, 0)] + [swap(pick(blocks, me ^ m, 0), "seq", m, ns) for m in range(1, ns)]
-
-
-def join(pieces, axis, size):
-    return jnp.concatenate(natural(pieces, axis, size), axis=0)
-
-
-def xor_start(value, axis, size):
-    return [value] + [swap(value, axis, m, size) for m in range(1, size)]
-
-
-def double_start(have, bit, ns):
-    return {**have, **{m | bit: swap(v, "seq", bit, ns) for m, v in have.items()}}
+def line_step(up, down, ns):
+    return (
+        lax.ppermute(up, "seq", [(r, r + 1) for r in range(ns - 1)]),
+        lax.ppermute(down, "seq", [(r + 1, r) for r in range(ns - 1)]),
+    )
+
+
+def add_all(pieces, dtype=F32):
+    total = pieces[0].astype(F32)
+    for value in pieces[1:]:
+        total = total + value.astype(F32)
+    return total.astype(dtype)
+
+
+def to_dp(whole):
+    return lax.psum_scatter(whole, "dp", scatter_dimension=0, tiled=True)
 
 
 def block(nd, ns, tokens, patches, cameras, tri_items, patch_items, mod_weight, qkv_weight, self_out_weight, norm2_gain, norm2_bias, cross_q_weight, cross_kv_weight, cross_out_weight, norm3_gain, norm3_bias, mlp_in_weight, mlp_in_bias, mlp_out_weight, mlp_out_bias, cotangent):
@@ -525,48 +514,46 @@
     heads_here = HEADS // ns
     cols_here = width // ns
     items = cameras.shape[0]
-    seq = lax.axis_index("seq")
-
-    seq_bits = bits_of(ns)[::-1]
+    w_rows = qkv_weight.shape[0]
+    n_dev = nd * ns
+    seq = Axis("seq", ns, ns, lax.axis_index("seq"), lambda m: m)
 
     def over_dp(held):
-        return lax.all_gather(join([held[m] for m in range(ns)], "seq", ns), "dp", axis=0, tiled=True)
+        return lax.all_gather(join(held, seq), "dp", axis=0, tiled=True)
+
+    down_bits = bits_of(ns)[::-1]
 
     bundle = {0: jnp.concatenate([self_out_weight, cross_q_weight, cross_kv_weight, cross_out_weight], axis=1)}
     small = jnp.concatenate(
         [mod_weight.reshape(-1), norm2_gain, norm2_bias, norm3_gain, norm3_bias, mlp_out_bias, mlp_in_bias]
     )
     length = small.shape[0]
-    small = jnp.pad(small, (0, -length % 2048)).reshape(-1, 128)
-    qkv_cut = qkv_weight.reshape(qkv_weight.shape[0], 3, ns, cols_here).transpose(2, 0, 1, 3)
-    qkv_cut = qkv_cut.reshape(ns, qkv_weight.shape[0], 3 * cols_here)
+    extra = -(-length // w_rows)
+    extra += -extra % 128
+    small = jnp.pad(small, (0, extra * w_rows - length)).reshape(w_rows, extra)
+    cut = qkv_weight.reshape(w_rows, 3, ns, cols_here).transpose(2, 0, 1, 3).reshape(ns, w_rows, 3 * cols_here)
+    cut = jnp.concatenate([cut, jnp.broadcast_to(small[None], (ns, w_rows, extra))], axis=2)
 
     ups, downs = [tokens], [tokens]
-    qkv_mine = small_all = None
-    todo = list(seq_bits)
+    todo = list(down_bits)
     for k in range(1, ns):
         up, down = line_step(ups[-1], downs[-1], ns)
         if k == 1:
-            small_got, qkv_got = xor_start(small, "seq", ns), exchange_start(qkv_cut, ns)
-            bundle = double_start(bundle, todo.pop(0), ns)
-            up, down, small_got, qkv_got, bundle = sync(up, down, small_got, qkv_got, bundle)
-            qkv_mine = lax.all_gather(join(qkv_got, "seq", ns), "dp", axis=0, tiled=True)
-        elif k == 2:
-            small_got = xor_start(join(small_got, "seq", ns), "dp", nd)
+            cut = exchange_start(cut, seq)
+            up, down, cut = sync(up, down, cut)
+            cut = lax.all_gather(join(cut, seq), "dp", axis=0, tiled=True)
+        else:
             if todo:
-                bundle = double_start(bundle, todo.pop(0), ns)
-            up, down, small_got, bundle = sync(up, down, small_got, bundle)
-            small_all = join(small_got, "dp", nd)
-        else:
-            up, down, small_all = sync(up, down, small_all)
+                bundle = double_start(bundle, todo.pop(0), seq)
+            up, down, bundle = sync(up, down, bundle)
         ups.append(up)
         downs.append(down)
     while todo:
-        bundle = double_start(bundle, todo.pop(0), ns)
-    if small_all is None:
-        small_all = join(xor_start(join(small_got, "seq", ns), "dp", nd), "dp", nd)
+        bundle = double_start(bundle, todo.pop(0), seq)
+    ups, downs, cut, patches, mlp_in_weight = sync(ups, downs, cut, patches, mlp_in_weight)
+    qkv_mine = cut[:, : 3 * cols_here]
+    small = cut[:, 3 * cols_here :].reshape(n_dev, -1)
     bundle = over_dp(bundle)
-    small = small_all.reshape(nd * ns, -1)
     mod_n = mod_weight.size
     own = norm2_gain.shape[0]
     mod_full = small[:, :mod_n].reshape(-1, mod_weight.shape[1])
@@ -574,45 +561,48 @@
     gain_two, bias_two, gain_three, bias_three, out_bias = vectors
     in_bias = small[:, mod_n + 5 * own : length].reshape(1, -1).astype(F32)
 
-    tri_col, patch_col = tri_items.reshape(-1, 1), patch_items.reshape(-1, 1)
-    my_col = lax.dynamic_slice_in_dim(tri_items, seq * rows, rows).reshape(-1, 1)
+    tri_col = tri_items.reshape(-1, 1)
+    tri_query, tri_key = query_tags(tri_items, items), key_tags(tri_items)
+    my_items = lax.dynamic_slice_in_dim(tri_items, seq.me * rows, rows)
+    my_query, patch_key = query_tags(my_items, items), key_tags(patch_items)
 
     mod_items = product_t(cameras, mod_full)
-    token_all = line_join(ups, downs, ns)
-    token_all, qkv_mine, patches, mlp_in_weight = sync(token_all, qkv_mine, patches, mlp_in_weight)
-    patch_got = xor_start(patches, "seq", ns)
-    act_one = modulate(token_all, tri_col, mod_items)
-    w_in = double_start({0: mlp_in_weight}, seq_bits[0], ns)
+    patch_all = xor_start(patches, seq)
+    w_in = double_start({0: mlp_in_weight}, down_bits[0], seq)
+    steps = range(1, ns)
+    act_one, token_all = modulate(
+        [tokens] + ups[1:] + downs[1:], [0] + [-k for k in steps] + list(steps), seq.me, tri_col, mod_items
+    )
     act_one, w_in = sync(act_one, w_in)
-    for bit in seq_bits[1:]:
-        w_in = double_start(w_in, bit, ns)
+    for bit in down_bits[1:]:
+        w_in = double_start(w_in, bit, seq)
     qkv = product(act_one, qkv_mine).astype(BF)
     qkv, w_in, mlp_out_weight = sync(qkv, w_in, mlp_out_weight)
     w_in = over_dp(w_in)
+    w_out = double_start({0: mlp_out_weight}, down_bits[0], seq)
     self_at = (0, cols_here, 2 * cols_here)
-    self_mine, self_lse = attend(qkv, qkv, qkv, self_at, heads_here, tri_col, tri_col, items)
-    self_mine, bundle, patch_got, mlp_out_weight = sync(self_mine, bundle, patch_got, mlp_out_weight)
-    self_att = lax.all_to_all(self_mine, "seq", 0, 1, tiled=True)
+    self_mine, self_lse = attend(qkv, qkv, qkv, self_at, heads_here, tri_query, tri_key)
+    self_mine, bundle, patch_all, w_out = sync(self_mine, bundle, patch_all, w_out)
     w_self_out = bundle[:, :width]
     w_cross_q = bundle[:, width : 2 * width]
     w_cross_kv = bundle[:, 2 * width : 4 * width]
     w_cross_out = bundle[:, 4 * width :]
-    w_out = double_start({0: mlp_out_weight}, seq_bits[0], ns)
-    patch_all = join(patch_got, "seq", ns)
+    self_att = lax.all_to_all(self_mine, "seq", 0, 1, tiled=True)
+    patch_all = join(patch_all, seq)
     cross_kv = product(patch_all, w_cross_kv).astype(BF)
-    self_att, cross_kv, w_out = sync(self_att, cross_kv, w_out)
+    self_att, cross_kv = sync(self_att, cross_kv)
+    for bit in down_bits[1:]:
+        w_out = double_start(w_out, bit, seq)
     resid_in = tokens.astype(F32)
     resid_two = resid_in + product(self_att, w_self_out)
 
     unit_two, inv_two = norm_parts(resid_two)
     act_two = (unit_two * gain_two + bias_two).astype(BF)
     cross_q = product(act_two, w_cross_q).astype(BF)
-    for bit in seq_bits[1:]:
-        w_out = double_start(w_out, bit, ns)
     cross_q, w_out = sync(cross_q, w_out)
     w_out = over_dp(w_out)
     cross_at = (0, 0, width)
-    cross_att, cross_lse = attend(cross_q, cross_kv, cross_kv, cross_at, HEADS, my_col, patch_col, items)
+    cross_att, cross_lse = attend(cross_q, cross_kv, cross_kv, cross_at, HEADS, my_query, patch_key)
     resid_three = resid_two + product(cross_att, w_cross_out)
 
     unit_three, inv_three = norm_parts(resid_three)
@@ -627,7 +617,7 @@
     g_out_bias = jnp.sum(grad_out, axis=0)
     d_pre, g_in_bias = mlp_back(cotangent, w_out, slope)
     g_w_in = contract_rows(act_three, d_pre).astype(BF)
-    d_pre, g_w_in = tie(d_pre, g_w_in)
+    d_pre, g_w_in = sync(d_pre, g_w_in)
     g_w_in = to_dp(g_w_in)
     d_act_three = product_t(d_pre, w_in)
     g_gain_three = jnp.sum(d_act_three * unit_three, axis=0)
@@ -636,7 +626,9 @@
 
     d_cross_out = d_resid_three.astype(BF)
     d_cross = product_t(d_cross_out, w_cross_out).astype(BF)
-    d_cq, d_ck, d_cv = attend_back(cross_q, cross_kv, cross_kv, cross_at, HEADS, my_col, patch_col, items, cross_att, cross_lse, d_cross)
+    d_cq, d_ck, d_cv = attend_back(
+        cross_q, cross_kv, cross_kv, cross_at, HEADS, my_query, patch_key, cross_att, cross_lse, d_cross
+    )
     d_act_two = product_t(d_cq, w_cross_q)
     g_gain_two = jnp.sum(d_act_two * unit_two, axis=0)
     g_bias_two = jnp.sum(d_act_two, axis=0)
@@ -653,67 +645,66 @@
     d_self_mine, g_mid, patch_part, block_out, g_w_out = sync(d_self_mine, g_mid, patch_part, block_out, g_w_out)
 
     def over_seq(value):
-        return sum_xor(value.reshape((ns, -1) + value.shape[1:]), "seq", ns)
+        return exchange_start(value.reshape((ns, -1) + value.shape[1:]), seq)
 
     g_mid = to_dp(g_mid)
-    patch_sum, out_sum, in_sum = over_seq(patch_part), over_seq(g_w_out), None
+    out_sum, in_sum = over_seq(g_w_out), None
+    patch_line = LineSum(patch_part, ns)
+    patch_line.start()
     backs = []
     for first in range(0, heads_here, 2):
         back = attend_back(
-            qkv, qkv, qkv, self_at, 2, tri_col, tri_col, items, self_mine, self_lse, d_self_mine, first=first
+            qkv, qkv, qkv, self_at, 2, tri_query, tri_key, self_mine, self_lse, d_self_mine, first=first
         )
         if in_sum is None:
-            back, d_self_mine, g_w_in = sync(back, d_self_mine, g_w_in)
+            back, d_self_mine, g_w_in, patch_line.moved = sync(back, d_self_mine, g_w_in, patch_line.moved)
             in_sum = over_seq(g_w_in)
+            patch_line.start()
         backs.append(back)
-    backs, patch_sum, out_sum = sync(backs, patch_sum, out_sum)
+    backs, patch_line.moved, out_sum = sync(backs, patch_line.moved, out_sum)
+    for _ in range(patch_line.k, ns - 1):
+        patch_line.start()
     d_q, d_k, d_v = (jnp.concatenate(p, axis=1) if len(p) > 1 else p[0] for p in zip(*backs))
-    d_act_one_part, g_mod_items = modulate_back(d_q, d_k, d_v, qkv_mine, token_all, tri_col, items)
-    d_act_one_part, g_mod_items, d_q, d_k, d_v, in_sum, patch_sum, out_sum = sync(
-        d_act_one_part, g_mod_items, d_q, d_k, d_v, in_sum, patch_sum, out_sum
-    )
-    line = LineSum(d_act_one_part, ns)
+    d_act_one, g_mod_items = modulate_back(d_q, d_k, d_v, qkv_mine, token_all, tri_col, items)
+    d_act_one, g_mod_items, d_q, d_k, d_v, in_sum, patch_line.moved, out_sum = sync(
+        d_act_one, g_mod_items, d_q, d_k, d_v, in_sum, patch_line.moved, out_sum
+    )
+
+    line = LineSum(d_act_one, ns)
     line.start()
     g_mod = lax.dot_general(
         g_mod_items, cameras.astype(F32), (((0,), (0,)), ((), ())), precision=lax.Precision.HIGHEST
     )
-    n_dev = nd * ns
     tail = jnp.concatenate(
         [g_mod.reshape(n_dev, -1)]
         + [v.reshape(n_dev, -1) for v in (g_gain_two, g_bias_two, g_gain_three, g_bias_three, g_out_bias, g_in_bias)],
         axis=1,
     )
-    tail_n = tail.shape[1]
-    tail = jnp.pad(tail, ((0, 0), (0, -tail_n % 1024))).reshape(nd, ns, -1, 128)
-    tail = sum_xor(tail, "dp", nd)
+    tail = jnp.pad(tail, ((0, 0), (0, extra * w_rows - length))).reshape(n_dev * w_rows, extra).astype(BF)
     g_qkv = weight_grads([(act_one, d_q), (act_one, d_k), (act_one, d_v)])
-    g_qkv, line.moved, tail, patch_sum, out_sum, in_sum = sync(g_qkv, line.moved, tail, patch_sum, out_sum, in_sum)
+    g_qkv = jnp.concatenate([g_qkv, tail], axis=1)
+    line.moved, g_qkv, in_sum, g_mid = sync(line.moved, g_qkv, in_sum, g_mid)
     g_qkv = to_dp(g_qkv)
-    for k in range(2, ns):
+    g_mid = over_seq(g_mid)
+    line.start()
+    patch_grad, g_w_out, g_w_in = patch_line.total(), add_all(out_sum), add_all(in_sum)
+    line.moved, patch_grad, g_w_out, g_w_in, g_mid = sync(line.moved, patch_grad, g_w_out, g_w_in, g_mid)
+    for _ in range(line.k, ns - 1):
         line.start()
-        if k == 2:
-            tail = sum_xor(add_all(*tail), "seq", ns)
-            patch_grad, g_w_out, g_w_in = add_all(*patch_sum), add_all(*out_sum), add_all(*in_sum)
-            line.moved, tail, patch_grad, g_w_out, g_w_in, g_mid = sync(
-                line.moved, tail, patch_grad, g_w_out, g_w_in, g_mid
-            )
-            g_mid = over_seq(g_mid)
-            tail = add_all(*tail).reshape(-1)
+    g_mid = add_all(g_mid)
     line.moved, g_mid, g_qkv = sync(line.moved, g_mid, g_qkv)
+    g_qkv = exchange_start(g_qkv.reshape(ns, w_rows, -1), seq)
     d_act_one = line.total()
+    unit_own, inv_own = norm_parts(resid_in)
+    scale_own = per_item(my_items.reshape(-1, 1), mod_items[:, width:])
+    input_grad = d_resid_two + norm_back(unit_own, inv_own, d_act_one * (1.0 + scale_own))
+    g_qkv = join([g[None] for g in g_qkv], seq).astype(F32)
+    tail = jnp.sum(g_qkv[:, :, 3 * cols_here :], axis=0).reshape(-1)
     g_mod = tail[:mod_n].reshape(mod_weight.shape)
-    cut = [tail[mod_n + n * own : mod_n + (n + 1) * own] for n in range(5)]
-    g_in_bias = tail[mod_n + 5 * own : tail_n]
-    g_qkv = join(exchange_start(g_qkv.reshape(ns, -1, g_qkv.shape[1]), ns), "seq", ns).astype(F32)
-    g_qkv = (
-        g_qkv.reshape(ns, qkv_weight.shape[0], 3, cols_here)
-        .transpose(1, 2, 0, 3)
-        .reshape(qkv_weight.shape)
-    )
-    g_mid = add_all(*g_mid)
-    unit_own, inv_own = norm_parts(resid_in)
-    scale_own = per_item(my_col, mod_items[:, width:])
-    input_grad = d_resid_two + norm_back(unit_own, inv_own, d_act_one * (1.0 + scale_own))
+    parts = [tail[mod_n + n * own : mod_n + (n + 1) * own] for n in range(5)]
+    g_in_bias = tail[mod_n + 5 * own : length]
+    g_qkv = g_qkv[:, :, : 3 * cols_here].reshape(ns, w_rows, 3, cols_here)
+    g_qkv = g_qkv.transpose(1, 2, 0, 3).reshape(qkv_weight.shape)
     return (
         block_out,
         input_grad,
@@ -721,17 +712,17 @@
         g_mod,
         g_qkv,
         g_mid[:, :width],
-        cut[0],
-        cut[1],
+        parts[0],
+        parts[1],
         g_mid[:, width : 2 * width],
         g_mid[:, 2 * width : 4 * width],
         g_mid[:, 4 * width :],
-        cut[2],
-        cut[3],
+        parts[2],
+        parts[3],
         g_w_in,
         g_in_bias,
         g_w_out,
-        cut[4],
+        parts[4],
     )
 
 

time: 705 us -> 677 us (0.960)
  Pallas kernels: 221 us -> 208 us
    ppermute x3, waiting for transfers between devices: 17.5 us -> 0.01 us  [line_step(): lax.ppermute(up, 'seq', [(r, r + 1) for r in range(ns - 1)])]
    ppermute x50 -> x27, starting transfers between devices: 73.9 us -> 57.7 us  [send(): lax.ppermute(value, self.name, [(r, r ^ self.flip(m)) for r in range(self...]
    ppermute x50 -> x27, waiting for transfers between devices: 122 us -> 138 us  [send(): lax.ppermute(value, self.name, [(r, r ^ self.flip(m)) for r in range(self...]
    ppermute x3 -> x6, waiting for transfers between devices: 14.8 us -> 0.57 us  [start(): lax.ppermute(above.astype(BF), 'seq', [(r, r + 1) for r in range(k)])]
    ppermute x3 -> x6, waiting for transfers between devices: 0.01 us -> 12.5 us  [start(): lax.ppermute(below.astype(BF), 'seq', [(ns - 1 - r, ns - 2 - r) for r in...]
    pallas_call x6, Pallas kernels: 146 us -> 136 us  [the longest x3 77.1 us: attend_back(): pl.pallas_call(functools.partial(attend_back_kernel, kb=kb), grid=(pairs,...]
    ppermute x3 -> x6, starting transfers between devices: 12.6 us -> 20.8 us  [start(): lax.ppermute(above.astype(BF), 'seq', [(r, r + 1) for r in range(k)])]
  transfers between devices with their start and end apart: 72 -> 55, of which waited for: 27 -> 15; matrix products, arithmetic and copies ran while one was open for 23% -> 23% of each run, Pallas kernels for 32% -> 31%
where the time goes in v3:
time: 677 us; the launch traced here: 670 us
  Pallas kernels  208 us (31%)
  waiting for transfers between devices  165 us (24%)
  starting transfers between devices  110 us (16%)
  matrix products  84.6 us (12%)
  other arithmetic  44.3 us (7%)
  local copies, waits for them, and re-layouts  42.2 us (6%)
  between operations  15.5 us (2%)
    ppermute x27, waiting for transfers between devices, send(): lax.ppermute(value, self.name, [(r, r ^ self.flip(m)) for r in range(self...  138 us
    pallas_call x3, Pallas kernels, attend_back(): pl.pallas_call(functools.partial(attend_back_kernel, kb=kb), grid=(pairs,...  77.1 us
    ppermute x27, starting transfers between devices, send(): lax.ppermute(value, self.name, [(r, r ^ self.flip(m)) for r in range(self...  57.7 us
    pallas_call x2, Pallas kernels, attend(): pl.pallas_call(functools.partial(attend_kernel, heads=step), grid=(heads...  46.1 us
    dot_general x6, matrix products, product(): return jnp.dot(a, b, preferred_element_type=F32)  33.8 us
    pallas_call x2, Pallas kernels, weight_grads(): pl.pallas_call(functools.partial(grads_kernel, spans=tuple(spans)), grid=...  33.1 us
    dot_general x7, matrix products, product_t(): lax.dot_general(a, b, (((1,), (1,)), ((), ())), preferred_element_type=F32)  31.8 us
    ppermute x6, starting transfers between devices, start(): lax.ppermute(above.astype(BF), 'seq', [(r, r + 1) for r in range(k)])  20.8 us
  transfers between devices with their start and end apart: 55, of which 15 were waited for; matrix products, arithmetic and copies ran while one was open for 23% of the time, Pallas kernels for 31%

profile of v3, /device:TPU:0, one launch (start us, length us, event | category | flops | bytes accessed | tf_op | source)
XLA Modules:
  0.0 670.1 jit_solution(13039747811519343460)
XLA Ops:
  8.5 5.6 collective-permute-start
  25.9 14.3 %collective-permute-done.4 = bf16[32,896]{1,0:T(8,128)(2,1)S(1)} collective-permute-done((bf16[32,896]{1,0:T(8,128)(2,1)S(1)}, bf16[32,896]{1,0:T(8,128)(2,1)S(1)}, u32[]{:S(2)}, u32[]{:S(2)}) %collective-permute-start.4) | collective-permute-done | bytes 57376 | tf_op jit(solution)/shard_map/ppermute | solution.py:425
  55.5 30.5 %collective-permute-done.7 = bf16[32,5120]{1,0:T(8,128)(2,1)S(1)} collective-permute-done((bf16[32,5120]{1,0:T(8,128)(2,1)S(1)}, bf16[32,5120]{1,0:T(8,128)(2,1)S(1)}, u32[]{:S(2)}, u32[]{:S(2)}) %collective-permute-start.7) | collective-permute-done | bytes 327712 | tf_op jit(solution)/shard_map/ppermute | solution.py:425
  91.5 30.4 %collective-permute-done.10 = bf16[32,5120]{1,0:T(8,128)(2,1)S(1)} collective-permute-done((bf16[32,5120]{1,0:T(8,128)(2,1)S(1)}, bf16[32,5120]{1,0:T(8,128)(2,1)S(1)}, u32[]{:S(2)}, u32[]{:S(2)}) %collective-permute-start.10) | collective-permute-done | bytes 327712 | tf_op jit(solution)/shard_map/ppermute | solution.py:425
  132.1 12.3 %modulate.1 = (bf16[2048,1024]{1,0:T(8,128)(2,1)}, bf16[2048,1024]{1,0:T(8,128)(2,1)}) custom-call(s32[1]{0:T(128)} %bitcast.me_ref, bf16[512,1024]{1,0:T(8,128)(2,1)} %refs_0_.1, bf16[512,1024]{1,0:T(8,128)(2,1)} %copy-done.28, bf16[512,1024]{1,0:T(8,128)(2,1)} %copy-done.29, bf16[512,1024]{1,0:T(8,128)(2,1)} %copy-done.30, bf16[512,1024]{1,0:T(8,128)(2,1)} %copy-done.27, ...), custom_call_target="tpu_custom_call" | custom-call | flops 1 | bytes 1 | tf_op jit(solution)/shard_map/modulate/pallas_call | solution.py:300
  146.5 7.3 %convolution_convert_fusion.2.q_ref.k_ref.v_ref = bf16[2048,768]{1,0:T(8,128)(2,1)} fusion(bf16[2048,1024]{1,0:T(8,128)(2,1)} %get-tuple-element.175.refs_0_.refs_1_.refs_2_, bf16[1024,896]{1,0:T(8,128)(2,1)S(1)} %copy-done.25), kind=kOutput, calls=%fused_computation.6 | convolution fusion | flops 3222798336 | bytes 8912896 | tf_op jit(solution)/shard_map/dot_general | solution.py:24
  164.6 29.2 %attend.2 = (bf16[2048,256]{1,0:T(8,128)(2,1)}, f32[2,2,2048]{2,1,0:T(2,128)}) custom-call(bf16[2048,768]{1,0:T(8,128)(2,1)} %convolution_convert_fusion.2.q_ref.k_ref.v_ref, bf16[2048,768]{1,0:T(8,128)(2,1)} %convolution_convert_fusion.2.q_ref.k_ref.v_ref, bf16[2048,768]{1,0:T(8,128)(2,1)} %convolution_convert_fusion.2.q_ref.k_ref.v_ref, ...), custom_call_target="tpu_custom_call" | custom-call | flops 1 | bytes 1 | tf_op jit(solution)/shard_map/attend/pallas_call | solution.py:94
  193.8 13.2 %collective-permute-done.16 = bf16[256,1024]{1,0:T(8,128)(2,1)S(1)} collective-permute-done((bf16[256,1024]{1,0:T(8,128)(2,1)S(1)}, bf16[256,1024]{1,0:T(8,128)(2,1)S(1)}, u32[]{:S(2)}, u32[]{:S(2)}) %collective-permute-start.16) | collective-permute-done | bytes 524320 | tf_op jit(solution)/shard_map/ppermute | solution.py:425
  221.2 10.2 %fusion.2.k_ref.v_ref = bf16[1024,2048]{1,0:T(8,128)(2,1)} fusion(bf16[1024,5120]{1,0:T(8,128)(2,1)} %all-gather.7.cloned.1.call-done, bf16[256,1024]{1,0:T(8,128)(2,1)S(1)} %get-tuple-element.374, bf16[256,1024]{1,0:T(8,128)(2,1)S(1)} %get-tuple-element.373, bf16[256,1024]{1,0:T(8,128)(2,1)S(1)} %get-tuple-element.372, ...), kind=kOutput, calls=%fused_computation.5 | convolution fusion | flops 4305453056 | bytes 10485760 | tf_op jit(solution)/shard_map/dot_general | solution.py:24
  231.4 9.1 %all-to-all-done = bf16[4,512,256]{2,1,0:T(8,128)(2,1)S(1)} async-done(((bf16[4,512,256]{2,1,0:T(8,128)(2,1)}), bf16[4,512,256]{2,1,0:T(8,128)(2,1)S(1)}, u32[]{:S(2)}, u32[]{:S(2)}) %all-to-all-start) | async-done | bytes 1048608 | tf_op jit(solution)/shard_map/all_to_all | solution.py:590
  254.2 16.9 %attend.3 = (bf16[512,1024]{1,0:T(8,128)(2,1)}, f32[8,2,512]{2,1,0:T(2,128)}) custom-call(bf16[512,1024]{1,0:T(8,128)(2,1)} %fusion.40.q_ref, bf16[1024,2048]{1,0:T(8,128)(2,1)} %fusion.2.k_ref.v_ref, bf16[1024,2048]{1,0:T(8,128)(2,1)} %fusion.2.k_ref.v_ref, bf16[512,128]{1,0:T(8,128)(2,1)} %select_convert_fusion.3.qtag_ref, ...), custom_call_target="tpu_custom_call" | custom-call | flops 1 | bytes 1 | tf_op jit(solution)/shard_map/attend/pallas_call | solution.py:94
  277.1 13.4 %mlp_up.1 = (bf16[512,4096]{1,0:T(8,128)(2,1)}, bf16[512,4096]{1,0:T(8,128)(2,1)}) custom-call(bf16[512,1024]{1,0:T(8,128)(2,1)} %add_convert_fusion.6.a_ref, bf16[1024,4096]{1,0:T(8,128)(2,1)} %all-gather.9.cloned.1.call-done.w_ref, f32[1,4096]{1,0:T(1,128)} %bitcast.124), custom_call_target="tpu_custom_call" | custom-call | flops 1 | bytes 1 | tf_op jit(solution)/shard_map/mlp_up/pallas_call | solution.py:213
  290.4 9.1 %convolution_convert_fusion.1 = bf16[4096,1024]{1,0:T(8,128)(2,1)} fusion(bf16[512,4096]{1,0:T(8,128)(2,1)} %get-tuple-element.205, bf16[512,1024]{1,0:T(8,128)(2,1)S(1)} %copy-done.7), kind=kOutput, calls=%fused_computation.1 | convolution fusion | flops 4299161600 | bytes 13631488 | tf_op jit(solution)/shard_map/dot_general | solution.py:32
  299.5 5.4 all-gather.11.cloned.1.call-done.w_ref
  305.2 12.2 %mlp_back.1 = (bf16[512,4096]{1,0:T(8,128)(2,1)}, f32[1,4096]{1,0:T(1,128)}) custom-call(bf16[512,1024]{1,0:T(8,128)(2,1)} %g_ref.1, bf16[4096,1024]{1,0:T(8,128)(2,1)} %all-gather.11.cloned.1.call-done.w_ref, bf16[512,4096]{1,0:T(8,128)(2,1)} %get-tuple-element.211.slope_ref), custom_call_target="tpu_custom_call" | custom-call | flops 1 | bytes 1 | tf_op jit(solution)/shard_map/mlp_back/pallas_call | solution.py:240
  317.4 9.7 %convolution_convert_fusion = bf16[1024,4096]{1,0:T(8,128)(2,1)} fusion(bf16[512,1024]{1,0:T(8,128)(2,1)S(1)} %copy-done.19, bf16[512,4096]{1,0:T(8,128)(2,1)} %get-tuple-element.213), kind=kOutput, calls=%fused_computation | convolution fusion | flops 4299161600 | bytes 13631488 | tf_op jit(solution)/shard_map/dot_general | solution.py:32
  330.4 9.4 %multiply_reduce_fusion = (bf16[1024]{0:T(1024)(128)(2,1)S(1)}, f32[512]{0:T(512)S(1)}, f32[512]{0:T(512)S(1)}, bf16[1024]{0:T(1024)(128)(2,1)S(1)}, f32[512,1024]{1,0:T(8,128)S(1)}) fusion(f32[512,1024]{1,0:T(8,128)S(1)} %copy-done.3, f32[512]{0:T(512)S(1)} %add_rsqrt_fusion.1, f32[512]{0:T(512)S(1)} %broadcast_multiply_fusion.7, f32[1024]{0:T(1024)S(1)} %reshape.279, ...), kind=kOutput, calls=%fused_computation.27 | convolution fusion | flops 4299682816 | bytes 16793600 | tf_op jit(solution)/shard_map/dot_general | solution.py:28
  344.9 25.7 %attend_back.3 = (bf16[512,1024]{1,0:T(8,128)(2,1)}, bf16[1024,1024]{1,0:T(8,128)(2,1)}, bf16[1024,1024]{1,0:T(8,128)(2,1)}) custom-call(bf16[512,1024]{1,0:T(8,128)(2,1)} %fusion.40.q_ref, bf16[1024,2048]{1,0:T(8,128)(2,1)} %fusion.2.k_ref.v_ref, bf16[1024,2048]{1,0:T(8,128)(2,1)} %fusion.2.k_ref.v_ref, bf16[512,1024]{1,0:T(8,128)(2,1)} %fusion.43.do_ref, ...), custom_call_target="tpu_custom_call" | custom-call | flops 1 | bytes 1 | tf_op jit(solution)/shard_map/attend_back/pallas_call | solution.py:166
  385.1 18.6 %weight_grads.2 = bf16[1024,5120]{1,0:T(8,128)(2,1)} custom-call(bf16[512,1024]{1,0:T(8,128)(2,1)} %bitcast.114, bf16[512,1024]{1,0:T(8,128)(2,1)} %copy-done.18, bf16[1024,1024]{1,0:T(8,128)(2,1)} %pad_maximum_fusion.refs_2_.refs_3_, bf16[1024,1024]{1,0:T(8,128)(2,1)} %pad_maximum_fusion.refs_2_.refs_3_, ...), custom_call_target="tpu_custom_call" | custom-call | flops 1 | bytes 1 | tf_op jit(solution)/shard_map/weight_grads/pallas_call | solution.py:403
  408.5 5.5 add_convert_fusion
  414.1 5.5 add_convert_fusion.5
  424.6 4.8 collective-permute-start.21
  432.7 25.4 %attend_back.4 = (bf16[2048,128]{1,0:T(8,128)(2,1)}, bf16[2048,128]{1,0:T(8,128)(2,1)}, bf16[2048,128]{1,0:T(8,128)(2,1)}) custom-call(bf16[2048,768]{1,0:T(8,128)(2,1)} %convolution_convert_fusion.2.q_ref.k_ref.v_ref, bf16[2048,768]{1,0:T(8,128)(2,1)} %convolution_convert_fusion.2.q_ref.k_ref.v_ref, ...), custom_call_target="tpu_custom_call" | custom-call | flops 1 | bytes 1 | tf_op jit(solution)/shard_map/attend_back/pallas_call | solution.py:166
  467.1 25.9 %attend_back.5 = (bf16[2048,128]{1,0:T(8,128)(2,1)}, bf16[2048,128]{1,0:T(8,128)(2,1)}, bf16[2048,128]{1,0:T(8,128)(2,1)}) custom-call(bf16[2048,768]{1,0:T(8,128)(2,1)} %convolution_convert_fusion.2.q_ref.k_ref.v_ref, bf16[2048,768]{1,0:T(8,128)(2,1)} %convolution_convert_fusion.2.q_ref.k_ref.v_ref, ...), custom_call_target="tpu_custom_call" | custom-call | flops 1 | bytes 1 | tf_op jit(solution)/shard_map/attend_back/pallas_call | solution.py:166
  497.0 16.8 %collective-permute-start.28 = (bf16[32,4096]{1,0:T(8,128)(2,1)S(1)}, bf16[32,4096]{1,0:T(8,128)(2,1)}, u32[]{:S(2)}, u32[]{:S(2)}) collective-permute-start(bf16[32,4096]{1,0:T(8,128)(2,1)S(1)} %get-tuple-element.385), channel_id=1, source_target_pairs={{0,1},{1,0},{2,3},{3,2},{4,5},{5,4},{6,7},{7,6},{8,9},{9,8},{10,11... | collective-permute-start | bytes 786440 | tf_op jit(solution)/shard_map/ppermute | solution.py:425
  516.6 5.5 collective-permute-start.31
  524.6 13.9 %modulate_back.1 = (bf16[2048,1024]{1,0:T(8,128)(2,1)}, f32[4,2048]{1,0:T(4,128)}) custom-call(bf16[2048,256]{1,0:T(8,128)(2,1)} %copy-done.13, bf16[2048,256]{1,0:T(8,128)(2,1)} %copy-done.12, bf16[2048,256]{1,0:T(8,128)(2,1)} %copy-done.11, bf16[1024,768]{1,0:T(8,128)(2,1)} %slice.106.w_ref, bf16[2048,1024]{1,0:T(8,128)(2,1)} %get-tuple-element.243.x_ref, ...), custom_call_target="tpu_custom_call" | custom-call | flops 1 | bytes 1 | tf_op jit(solution)/shard_map/modulate_back/pallas_call | solution.py:352
  546.1 14.4 %weight_grads.3 = bf16[1024,768]{1,0:T(8,128)(2,1)} custom-call(bf16[2048,1024]{1,0:T(8,128)(2,1)} %get-tuple-element.175.refs_0_.refs_1_.refs_2_, bf16[2048,1024]{1,0:T(8,128)(2,1)} %get-tuple-element.175.refs_0_.refs_1_.refs_2_, bf16[2048,1024]{1,0:T(8,128)(2,1)} %get-tuple-element.175.refs_0_.refs_1_.refs_2_, bf16[2048,256]{1,0:T(8,128)(2,1)} %copy-done.13, ...), custom_call_target="tpu_custom_call" | custom-call | flops 1 | bytes 1 | tf_op jit(solution)/shard_map/weight_grads/pallas_call | solution.py:403
  585.0 24.0 %collective-permute-done.39 = bf16[32,5120]{1,0:T(8,128)(2,1)S(1)} collective-permute-done((bf16[32,5120]{1,0:T(8,128)(2,1)S(1)}, bf16[32,5120]{1,0:T(8,128)(2,1)S(1)}, u32[]{:S(2)}, u32[]{:S(2)}) %collective-permute-start.39) | collective-permute-done | bytes 327712 | tf_op jit(solution)/shard_map/ppermute | solution.py:425
  609.0 14.5 %collective-permute-done.38 = bf16[32,5120]{1,0:T(8,128)(2,1)S(1)} collective-permute-done((bf16[32,5120]{1,0:T(8,128)(2,1)S(1)}, bf16[32,5120]{1,0:T(8,128)(2,1)S(1)}, u32[]{:S(2)}, u32[]{:S(2)}) %collective-permute-start.38) | collective-permute-done | bytes 327712 | tf_op jit(solution)/shard_map/ppermute | solution.py:425
  625.9 5.5 collective-permute-start.40
  631.5 12.5 %collective-permute-done.41 = bf16[512,1024]{1,0:T(8,128)(2,1)S(1)} collective-permute-done((bf16[512,1024]{1,0:T(8,128)(2,1)S(1)}, bf16[512,1024]{1,0:T(8,128)(2,1)S(1)}, u32[]{:S(2)}, u32[]{:S(2)}) %collective-permute-start.41) | collective-permute-done | bytes 1048608 | tf_op jit(solution)/shard_map/ppermute | solution.py:487
  (348 shorter events, 197.8 us)
Async XLA Ops:
  7.2 120.9 %all-gather.5.cloned.1.call-start = ((), (), s32[]{:S(2)}) async-start(), calls=%async_computation.6 | async-start | bytes 2064384 | tf_op jit(solution)/shard_map/all_gather | solution.py:544
  7.2 34.4 %collective-permute-start.1 = (bf16[512,1024]{1,0:T(8,128)(2,1)}, bf16[512,1024]{1,0:T(8,128)(2,1)S(1)}, u32[]{:S(2)}, u32[]{:S(2)}) collective-permute-start(bf16[512,1024]{1,0:T(8,128)(2,1)} %refs_0_.1), channel_id=1, source_target_pairs={{1,0},{2,1},{3,2},{5,4},{6,5},{7,6},{9,8},{10,9},{11,10},{13,12},{... | collective-permute-start | bytes 3145736 | tf_op jit(solution)/shard_map/ppermute | solution.py:497
  42.3 43.8 %collective-permute-start.5 = (bf16[512,1024]{1,0:T(8,128)(2,1)S(1)}, bf16[512,1024]{1,0:T(8,128)(2,1)S(1)}, u32[]{:S(2)}, u32[]{:S(2)}) collective-permute-start(bf16[512,1024]{1,0:T(8,128)(2,1)S(1)} %collective-permute-done.refs_1_), channel_id=1, source_target_pairs={{0,1},{1,2},{2,3},{4,5},{5,6},{6,7},{8,9},{9,10},{10,11},{12,13},{... | collective-permute-start | bytes 3145736 | tf_op jit(solution)/shard_map/ppermute | solution.py:496
  46.0 40.1 %collective-permute-start.6 = (bf16[512,1024]{1,0:T(8,128)(2,1)S(1)}, bf16[512,1024]{1,0:T(8,128)(2,1)}, u32[]{:S(2)}, u32[]{:S(2)}) collective-permute-start(bf16[512,1024]{1,0:T(8,128)(2,1)S(1)} %collective-permute-done.1.refs_4_), channel_id=1, source_target_pairs={{1,0},{2,1},{3,2},{5,4},{6,5},{7,6},{9,8},{10,9},{11,10},{13,12},{... | collective-permute-start | bytes 3145736 | tf_op jit(solution)/shard_map/ppermute | solution.py:497
  50.7 160.0 %all-gather.7.cloned.1.call-start = ((), (), s32[]{:S(2)}) async-start(), calls=%async_computation.7 | async-start | bytes 11796480 | tf_op jit(solution)/shard_map/all_gather | solution.py:522
  51.6 34.4 %collective-permute-start.7 = (bf16[32,5120]{1,0:T(8,128)(2,1)S(1)}, bf16[32,5120]{1,0:T(8,128)(2,1)S(1)}, u32[]{:S(2)}, u32[]{:S(2)}) collective-permute-start(bf16[32,5120]{1,0:T(8,128)(2,1)S(1)} %constant_dynamic-update-slice_fusion), channel_id=1, source_target_pairs={{0,2},{1,3},{2,0},{3,1},{4,6},{5,7},{6,4},{7,5},{8,10},{9,11},{10,... | collective-permute-start | bytes 983048 | tf_op jit(solution)/shard_map/ppermute | solution.py:425
  86.0 39.4 %collective-permute-start.8 = (bf16[512,1024]{1,0:T(8,128)(2,1)S(1)}, bf16[512,1024]{1,0:T(8,128)(2,1)S(1)}, u32[]{:S(2)}, u32[]{:S(2)}) collective-permute-start(bf16[512,1024]{1,0:T(8,128)(2,1)S(1)} %collective-permute-done.5.refs_2_), channel_id=1, source_target_pairs={{0,1},{1,2},{2,3},{4,5},{5,6},{6,7},{8,9},{9,10},{10,11},{12,13},{... | collective-permute-start | bytes 3145736 | tf_op jit(solution)/shard_map/ppermute | solution.py:496
  87.4 39.0 %collective-permute-start.9 = (bf16[512,1024]{1,0:T(8,128)(2,1)}, bf16[512,1024]{1,0:T(8,128)(2,1)}, u32[]{:S(2)}, u32[]{:S(2)}) collective-permute-start(bf16[512,1024]{1,0:T(8,128)(2,1)} %collective-permute-done.6.refs_5_), channel_id=1, source_target_pairs={{1,0},{2,1},{3,2},{5,4},{6,5},{7,6},{9,8},{10,9},{11,10},{13,12},{... | collective-permute-start | bytes 3145736 | tf_op jit(solution)/shard_map/ppermute | solution.py:497
  88.7 33.2 %collective-permute-start.10 = (bf16[32,5120]{1,0:T(8,128)(2,1)S(1)}, bf16[32,5120]{1,0:T(8,128)(2,1)S(1)}, u32[]{:S(2)}, u32[]{:S(2)}) collective-permute-start(bf16[32,5120]{1,0:T(8,128)(2,1)S(1)} %constant_dynamic-update-slice_fusion), channel_id=1, source_target_pairs={{0,1},{1,0},{2,3},{3,2},{4,5},{5,4},{6,7},{7,6},{8,9},{9,8},{10,11... | collective-permute-start | bytes 983048 | tf_op jit(solution)/shard_map/ppermute | solution.py:425
  91.4 34.0 %collective-permute-start.11 = (bf16[32,5120]{1,0:T(8,128)(2,1)S(1)}, bf16[32,5120]{1,0:T(8,128)(2,1)S(1)}, u32[]{:S(2)}, u32[]{:S(2)}) collective-permute-start(bf16[32,5120]{1,0:T(8,128)(2,1)S(1)} %collective-permute-done.7), channel_id=1, source_target_pairs={{0,1},{1,0},{2,3},{3,2},{4,5},{5,4},{6,7},{7,6},{8,9},{9,8},{10,11... | collective-permute-start | bytes 983048 | tf_op jit(solution)/shard_map/ppermute | solution.py:425
  127.7 149.3 %all-gather.9.cloned.1.call-start = ((), (), s32[]{:S(2)}) async-start(), calls=%async_computation.8 | async-start | bytes 9437184 | tf_op jit(solution)/shard_map/all_gather | solution.py:522
  156.2 37.6 %collective-permute-start.17 = (bf16[256,1024]{1,0:T(8,128)(2,1)S(1)}, bf16[256,1024]{1,0:T(8,128)(2,1)S(1)}, u32[]{:S(2)}, u32[]{:S(2)}) collective-permute-start(bf16[256,1024]{1,0:T(8,128)(2,1)S(1)} %copy-done.34), channel_id=1, source_target_pairs={{0,3},{1,2},{2,1},{3,0},{4,7},{5,6},{6,5},{7,4},{8,11},{9,10},{10,... | collective-permute-start | bytes 1572872 | tf_op jit(solution)/shard_map/ppermute | solution.py:425
  158.8 48.1 %collective-permute-start.16 = (bf16[256,1024]{1,0:T(8,128)(2,1)S(1)}, bf16[256,1024]{1,0:T(8,128)(2,1)S(1)}, u32[]{:S(2)}, u32[]{:S(2)}) collective-permute-start(bf16[256,1024]{1,0:T(8,128)(2,1)S(1)} %copy-done.34), channel_id=1, source_target_pairs={{0,2},{1,3},{2,0},{3,1},{4,6},{5,7},{6,4},{7,5},{8,10},{9,11},{10,... | collective-permute-start | bytes 1572872 | tf_op jit(solution)/shard_map/ppermute | solution.py:425
  159.9 47.0 %collective-permute-start.15 = (bf16[256,1024]{1,0:T(8,128)(2,1)S(1)}, bf16[256,1024]{1,0:T(8,128)(2,1)S(1)}, u32[]{:S(2)}, u32[]{:S(2)}) collective-permute-start(bf16[256,1024]{1,0:T(8,128)(2,1)S(1)} %copy-done.34), channel_id=1, source_target_pairs={{0,1},{1,0},{2,3},{3,2},{4,5},{5,4},{6,7},{7,6},{8,9},{9,8},{10,11... | collective-permute-start | bytes 1572872 | tf_op jit(solution)/shard_map/ppermute | solution.py:425
  160.7 50.0 %collective-permute-start.18 = (bf16[128,1024]{1,0:T(8,128)(2,1)S(1)}, bf16[128,1024]{1,0:T(8,128)(2,1)S(1)}, u32[]{:S(2)}, u32[]{:S(2)}) collective-permute-start(bf16[128,1024]{1,0:T(8,128)(2,1)S(1)} %copy-done.44), channel_id=1, source_target_pairs={{0,2},{1,3},{2,0},{3,1},{4,6},{5,7},{6,4},{7,5},{8,10},{9,11},{10,... | collective-permute-start | bytes 786440 | tf_op jit(solution)/shard_map/ppermute | solution.py:425
  215.3 89.6 %all-gather.11.cloned.1.call-start = ((), (), s32[]{:S(2)}) async-start(), calls=%async_computation.9 | async-start | bytes 9437184 | tf_op jit(solution)/shard_map/all_gather | solution.py:522
  251.3 168.2 %reduce-scatter.5.cloned.1.call-start = ((), (), s32[]{:S(2)}) async-start(), calls=%async_computation.10 | async-start | bytes 9437184 | tf_op jit(solution)/shard_map/reduce_scatter | solution.py:509
  305.0 153.1 %reduce-scatter.7.cloned.1.call-start = ((), (), s32[]{:S(2)}) async-start(), calls=%async_computation.11 | async-start | bytes 9437184 | tf_op jit(solution)/shard_map/reduce_scatter | solution.py:509
  380.8 38.7 %all-to-all-start.1 = ((bf16[512,4,256]{2,0,1:T(8,128)(2,1)}), bf16[512,4,256]{2,0,1:T(8,128)(2,1)S(1)}, u32[]{:S(2)}, u32[]{:S(2)}) async-start(bf16[512,4,256]{2,0,1:T(8,128)(2,1)} %bitcast.106), calls=%async_computation.1 | async-start | bytes 2097152 | tf_op jit(solution)/shard_map/all_to_all | solution.py:639
  385.1 187.8 %reduce-scatter.9.cloned.1.call-start = ((), (), s32[]{:S(2)}) async-start(), calls=%async_computation.12 | async-start | bytes 11796480 | tf_op jit(solution)/shard_map/reduce_scatter | solution.py:509
  420.5 224.0 %reduce-scatter.11.cloned.1.call-start = ((), (), s32[]{:S(2)}) async-start(), calls=%async_computation.13 | async-start | bytes 2064384 | tf_op jit(solution)/shard_map/reduce_scatter | solution.py:509
  423.1 35.0 %collective-permute-start.22 = (bf16[256,1024]{1,0:T(8,128)(2,1)}, bf16[256,1024]{1,0:T(8,128)(2,1)}, u32[]{:S(2)}, u32[]{:S(2)}) collective-permute-start(bf16[256,1024]{1,0:T(8,128)(2,1)} %get-tuple-element.369), channel_id=1, source_target_pairs={{3,2},{7,6},{11,10},{15,14},{19,18},{23,22},{27,26},{31,30}} | collective-permute-start | bytes 1572872 | tf_op jit(solution)/shard_map/ppermute | solution.py:487
  424.6 33.6 %collective-permute-start.21 = (bf16[256,1024]{1,0:T(8,128)(2,1)}, bf16[256,1024]{1,0:T(8,128)(2,1)}, u32[]{:S(2)}, u32[]{:S(2)}) collective-permute-start(bf16[256,1024]{1,0:T(8,128)(2,1)} %get-tuple-element.370), channel_id=1, source_target_pairs={{0,1},{4,5},{8,9},{12,13},{16,17},{20,21},{24,25},{28,29}} | collective-permute-start | bytes 1572872 | tf_op jit(solution)/shard_map/ppermute | solution.py:486
  459.9 53.9 %collective-permute-start.24 = (bf16[256,1024]{1,0:T(8,128)(2,1)S(1)}, bf16[256,1024]{1,0:T(8,128)(2,1)S(1)}, u32[]{:S(2)}, u32[]{:S(2)}) collective-permute-start(bf16[256,1024]{1,0:T(8,128)(2,1)S(1)} %get-tuple-element.367), channel_id=1, source_target_pairs={{3,2},{2,1},{7,6},{6,5},{11,10},{10,9},{15,14},{14,13},{19,18},{18... | collective-permute-start | bytes 1572872 | tf_op jit(solution)/shard_map/ppermute | solution.py:487
  460.6 53.2 %collective-permute-start.23 = (bf16[256,1024]{1,0:T(8,128)(2,1)S(1)}, bf16[256,1024]{1,0:T(8,128)(2,1)S(1)}, u32[]{:S(2)}, u32[]{:S(2)}) collective-permute-start(bf16[256,1024]{1,0:T(8,128)(2,1)S(1)} %get-tuple-element.368), channel_id=1, source_target_pairs={{0,1},{1,2},{4,5},{5,6},{8,9},{9,10},{12,13},{13,14},{16,17},{17,1... | collective-permute-start | bytes 1572872 | tf_op jit(solution)/shard_map/ppermute | solution.py:486
  494.0 44.5 %collective-permute-start.30 = (bf16[32,4096]{1,0:T(8,128)(2,1)}, bf16[32,4096]{1,0:T(8,128)(2,1)}, u32[]{:S(2)}, u32[]{:S(2)}) collective-permute-start(bf16[32,4096]{1,0:T(8,128)(2,1)} %get-tuple-element.383), channel_id=1, source_target_pairs={{0,3},{1,2},{2,1},{3,0},{4,7},{5,6},{6,5},{7,4},{8,11},{9,10},{10,... | collective-permute-start | bytes 786440 | tf_op jit(solution)/shard_map/ppermute | solution.py:425
  496.4 42.1 %collective-permute-start.29 = (bf16[32,4096]{1,0:T(8,128)(2,1)}, bf16[32,4096]{1,0:T(8,128)(2,1)}, u32[]{:S(2)}, u32[]{:S(2)}) collective-permute-start(bf16[32,4096]{1,0:T(8,128)(2,1)} %get-tuple-element.384), channel_id=1, source_target_pairs={{0,2},{1,3},{2,0},{3,1},{4,6},{5,7},{6,4},{7,5},{8,10},{9,11},{10,... | collective-permute-start | bytes 786440 | tf_op jit(solution)/shard_map/ppermute | solution.py:425
  497.0 41.6 %collective-permute-start.28 = (bf16[32,4096]{1,0:T(8,128)(2,1)S(1)}, bf16[32,4096]{1,0:T(8,128)(2,1)}, u32[]{:S(2)}, u32[]{:S(2)}) collective-permute-start(bf16[32,4096]{1,0:T(8,128)(2,1)S(1)} %get-tuple-element.385), channel_id=1, source_target_pairs={{0,1},{1,0},{2,3},{3,2},{4,5},{5,4},{6,7},{7,6},{8,9},{9,8},{10,11... | collective-permute-start | bytes 786440 | tf_op jit(solution)/shard_map/ppermute | solution.py:425
  576.2 47.3 %collective-permute-start.36 = (bf16[512,1024]{1,0:T(8,128)(2,1)S(1)}, bf16[512,1024]{1,0:T(8,128)(2,1)S(1)}, u32[]{:S(2)}, u32[]{:S(2)}) collective-permute-start(bf16[512,1024]{1,0:T(8,128)(2,1)S(1)} %get-tuple-element.361), channel_id=1, source_target_pairs={{3,2},{2,1},{7,6},{6,5},{11,10},{10,9},{15,14},{14,13},{19,18},{18... | collective-permute-start | bytes 3145736 | tf_op jit(solution)/shard_map/ppermute | solution.py:487
  576.9 46.6 %collective-permute-start.35 = (bf16[512,1024]{1,0:T(8,128)(2,1)S(1)}, bf16[512,1024]{1,0:T(8,128)(2,1)S(1)}, u32[]{:S(2)}, u32[]{:S(2)}) collective-permute-start(bf16[512,1024]{1,0:T(8,128)(2,1)S(1)} %get-tuple-element.362), channel_id=1, source_target_pairs={{0,1},{1,2},{4,5},{5,6},{8,9},{9,10},{12,13},{13,14},{16,17},{17,1... | collective-permute-start | bytes 3145736 | tf_op jit(solution)/shard_map/ppermute | solution.py:486
  580.7 42.8 %collective-permute-start.38 = (bf16[32,5120]{1,0:T(8,128)(2,1)S(1)}, bf16[32,5120]{1,0:T(8,128)(2,1)S(1)}, u32[]{:S(2)}, u32[]{:S(2)}) collective-permute-start(bf16[32,5120]{1,0:T(8,128)(2,1)S(1)} %get-tuple-element.376), channel_id=1, source_target_pairs={{0,2},{1,3},{2,0},{3,1},{4,6},{5,7},{6,4},{7,5},{8,10},{9,11},{10,... | collective-permute-start | bytes 983048 | tf_op jit(solution)/shard_map/ppermute | solution.py:425
  582.1 41.4 %collective-permute-start.37 = (bf16[32,5120]{1,0:T(8,128)(2,1)S(1)}, bf16[32,5120]{1,0:T(8,128)(2,1)S(1)}, u32[]{:S(2)}, u32[]{:S(2)}) collective-permute-start(bf16[32,5120]{1,0:T(8,128)(2,1)S(1)} %get-tuple-element.377), channel_id=1, source_target_pairs={{0,1},{1,0},{2,3},{3,2},{4,5},{5,4},{6,7},{7,6},{8,9},{9,8},{10,11... | collective-permute-start | bytes 983048 | tf_op jit(solution)/shard_map/ppermute | solution.py:425
  (83 other events, 1253.5 us)
Sparse Core Ops, SparseCore 0:
  50.8 30.8 all-gather.4
  127.9 61.4 all-gather.6
  191.3 54.3 all-gather.8
  251.5 53.4 all-gather.10
  308.3 71.2 reduce-scatter.4
  383.3 71.2 reduce-scatter.6
  458.1 81.5 reduce-scatter.8
  573.0 39.3 reduce-scatter.10

commit v4 on v3

--- a/solution.py
+++ b/solution.py
@@ -208,7 +208,7 @@
 
 def mlp_up(act, w, bias):
     rows, ff = act.shape[0], w.shape[1]
-    cb = 512
+    cb = 1024
     block = pl.BlockSpec((rows, cb), lambda g: (0, g))
     return pl.pallas_call(
         mlp_up_kernel,
@@ -235,7 +235,7 @@
 
 def mlp_back(grad, w, slope):
     rows, ff = slope.shape
-    cb = 512
+    cb = 1024
     block = pl.BlockSpec((rows, cb), lambda g: (0, g))
     return pl.pallas_call(
         mlp_back_kernel,
@@ -293,7 +293,7 @@
 
 def modulate(pieces, offsets, me, ids, mod_items):
     rows, width = pieces[0].shape
-    rb = min(256, rows)
+    rb = min(512, rows)
     per = rows // rb
     total = ids.shape[0]
     block = pl.BlockSpec((rb, width), lambda i, me: (i, 0))
@@ -346,7 +346,7 @@
 
 def modulate_back(d_q, d_k, d_v, w, x, ids, items):
     rows, width = x.shape
-    rb = 256
+    rb = 512
     c = d_q.shape[1]
     part = pl.BlockSpec((rb, c), lambda i: (i, 0))
     return pl.pallas_call(
@@ -371,16 +371,15 @@
     )(d_q, d_k, d_v, w, x, ids)
 
 
-def grads_kernel(*refs, spans):
-    n = len(spans)
+def grads_kernel(*refs, spans, sources, count):
     g = pl.program_id(0)
-    x_refs, y_refs, out_ref, xt_ref = refs[:n], refs[n : 2 * n], refs[-2], refs[-1]
+    x_refs, y_refs, out_ref, xt_ref = refs[:count], refs[count:-2], refs[-2], refs[-1]
     for i, (start, stop) in enumerate(spans):
         rows = y_refs[i].shape[0]
-
-        @pl.when(g == start)
-        def _():
-            xt_ref[:, :rows] = x_refs[i][...].T
+        if i == 0 or sources[i] != sources[i - 1]:
+            @pl.when(g == start)
+            def _():
+                xt_ref[:, :rows] = x_refs[sources[i]][...].T
 
         @pl.when((g >= start) & (g < stop))
         def _():
@@ -388,20 +387,21 @@
 
 
 def weight_grads(pairs):
+    flat = [(n, y) for n, (_, ys) in enumerate(pairs) for y in ys]
     width = pairs[0][0].shape[1]
-    cb = min(1024, min(y.shape[1] for _, y in pairs))
+    cb = min(1024, min(y.shape[1] for _, y in flat))
     spans, at = [], 0
-    for _, y in pairs:
+    for _, y in flat:
         spans.append((at, at + y.shape[1] // cb))
         at = spans[-1][1]
     in_specs = [pl.BlockSpec(x.shape, lambda g: (0, 0), pipeline_mode=pl.Buffered(1)) for x, _ in pairs]
-    for (_, y), (start, stop) in zip(pairs, spans):
+    for (_, y), (start, stop) in zip(flat, spans):
         in_specs.append(
             pl.BlockSpec((y.shape[0], cb), lambda g, start=start, stop=stop: (0, jnp.clip(g - start, 0, stop - start - 1)))
         )
     longest = max(x.shape[0] for x, _ in pairs)
     return pl.pallas_call(
-        functools.partial(grads_kernel, spans=tuple(spans)),
+        functools.partial(grads_kernel, spans=tuple(spans), sources=tuple(n for n, _ in flat), count=len(pairs)),
         grid=(at,),
         in_specs=in_specs,
         out_specs=pl.BlockSpec((width, cb), lambda g: (0, g)),
@@ -410,7 +410,7 @@
         compiler_params=kernel_params(),
         cost_estimate=SHORT,
         name="weight_grads",
-    )(*[x for x, _ in pairs], *[y for _, y in pairs])
+    )(*[x for x, _ in pairs], *[y for _, y in flat])
 
 
 def bits_of(size):
@@ -498,6 +498,13 @@
     )
 
 
+def line_join(ups, downs, ns):
+    ring = [ups[0]] + [downs[r] + ups[ns - r] for r in range(1, ns)]
+    rows = ups[0].shape[0]
+    first = (ns - lax.axis_index("seq")) % ns
+    return lax.dynamic_slice_in_dim(jnp.concatenate(ring + ring[:-1], axis=0), first * rows, ns * rows)
+
+
 def add_all(pieces, dtype=F32):
     total = pieces[0].astype(F32)
     for value in pieces[1:]:
@@ -545,15 +552,20 @@
         else:
             if todo:
                 bundle = double_start(bundle, todo.pop(0), seq)
-            up, down, bundle = sync(up, down, bundle)
+                up, down, bundle = sync(up, down, bundle)
+                if not todo:
+                    bundle = over_dp(bundle)
+            else:
+                up, down = sync(up, down)
         ups.append(up)
         downs.append(down)
-    while todo:
-        bundle = double_start(bundle, todo.pop(0), seq)
+    if len(todo) or ns == 2:
+        while todo:
+            bundle = double_start(bundle, todo.pop(0), seq)
+        bundle = over_dp(bundle)
     ups, downs, cut, patches, mlp_in_weight = sync(ups, downs, cut, patches, mlp_in_weight)
     qkv_mine = cut[:, : 3 * cols_here]
     small = cut[:, 3 * cols_here :].reshape(n_dev, -1)
-    bundle = over_dp(bundle)
     mod_n = mod_weight.size
     own = norm2_gain.shape[0]
     mod_full = small[:, :mod_n].reshape(-1, mod_weight.shape[1])
@@ -567,28 +579,41 @@
     my_query, patch_key = query_tags(my_items, items), key_tags(patch_items)
 
     mod_items = product_t(cameras, mod_full)
-    patch_all = xor_start(patches, seq)
+    patch_ups, patch_downs = [patches], [patches]
+
+    def patch_step():
+        if len(patch_ups) < ns:
+            up, down = line_step(patch_ups[-1], patch_downs[-1], ns)
+            patch_ups.append(up)
+            patch_downs.append(down)
+
+    patch_step()
     w_in = double_start({0: mlp_in_weight}, down_bits[0], seq)
     steps = range(1, ns)
     act_one, token_all = modulate(
         [tokens] + ups[1:] + downs[1:], [0] + [-k for k in steps] + list(steps), seq.me, tri_col, mod_items
     )
-    act_one, w_in = sync(act_one, w_in)
+    act_one, w_in, patch_ups[-1], patch_downs[-1] = sync(act_one, w_in, patch_ups[-1], patch_downs[-1])
     for bit in down_bits[1:]:
         w_in = double_start(w_in, bit, seq)
+    patch_step()
     qkv = product(act_one, qkv_mine).astype(BF)
-    qkv, w_in, mlp_out_weight = sync(qkv, w_in, mlp_out_weight)
+    qkv, w_in, mlp_out_weight, patch_ups[-1], patch_downs[-1] = sync(
+        qkv, w_in, mlp_out_weight, patch_ups[-1], patch_downs[-1]
+    )
     w_in = over_dp(w_in)
+    while len(patch_ups) < ns:
+        patch_step()
     w_out = double_start({0: mlp_out_weight}, down_bits[0], seq)
     self_at = (0, cols_here, 2 * cols_here)
     self_mine, self_lse = attend(qkv, qkv, qkv, self_at, heads_here, tri_query, tri_key)
-    self_mine, bundle, patch_all, w_out = sync(self_mine, bundle, patch_all, w_out)
+    self_mine, bundle, patch_ups, patch_downs, w_out = sync(self_mine, bundle, patch_ups, patch_downs, w_out)
     w_self_out = bundle[:, :width]
     w_cross_q = bundle[:, width : 2 * width]
     w_cross_kv = bundle[:, 2 * width : 4 * width]
     w_cross_out = bundle[:, 4 * width :]
     self_att = lax.all_to_all(self_mine, "seq", 0, 1, tiled=True)
-    patch_all = join(patch_all, seq)
+    patch_all = line_join(patch_ups, patch_downs, ns)
     cross_kv = product(patch_all, w_cross_kv).astype(BF)
     self_att, cross_kv = sync(self_att, cross_kv)
     for bit in down_bits[1:]:
@@ -637,16 +662,16 @@
     d_self_out = d_resid_two.astype(BF)
     d_self = product_t(d_self_out, w_self_out).astype(BF)
     d_self_mine = lax.all_to_all(d_self, "seq", 1, 0, tiled=True)
+
+    def over_seq(value):
+        return exchange_start(value.reshape((ns, -1) + value.shape[1:]), seq)
+
     g_mid = weight_grads(
-        [(self_att, d_self_out), (act_two, d_cq), (patch_all, d_ck), (patch_all, d_cv), (cross_att, d_cross_out)]
+        [(self_att, [d_self_out]), (act_two, [d_cq]), (patch_all, [d_ck, d_cv]), (cross_att, [d_cross_out])]
     )
     patch_part = (product_t(d_ck, w_cross_kv[:, :width]) + product_t(d_cv, w_cross_kv[:, width:])).astype(BF)
     block_out = (resid_three + product(hid, w_out) + out_bias).astype(BF)
     d_self_mine, g_mid, patch_part, block_out, g_w_out = sync(d_self_mine, g_mid, patch_part, block_out, g_w_out)
-
-    def over_seq(value):
-        return exchange_start(value.reshape((ns, -1) + value.shape[1:]), seq)
-
     g_mid = to_dp(g_mid)
     out_sum, in_sum = over_seq(g_w_out), None
     patch_line = LineSum(patch_part, ns)
@@ -661,7 +686,7 @@
             in_sum = over_seq(g_w_in)
             patch_line.start()
         backs.append(back)
-    backs, patch_line.moved, out_sum = sync(backs, patch_line.moved, out_sum)
+    backs, patch_line.moved, out_sum, in_sum = sync(backs, patch_line.moved, out_sum, in_sum)
     for _ in range(patch_line.k, ns - 1):
         patch_line.start()
     d_q, d_k, d_v = (jnp.concatenate(p, axis=1) if len(p) > 1 else p[0] for p in zip(*backs))
@@ -681,12 +706,13 @@
         axis=1,
     )
     tail = jnp.pad(tail, ((0, 0), (0, extra * w_rows - length))).reshape(n_dev * w_rows, extra).astype(BF)
-    g_qkv = weight_grads([(act_one, d_q), (act_one, d_k), (act_one, d_v)])
+    g_qkv = weight_grads([(act_one, [d_q, d_k, d_v])])
     g_qkv = jnp.concatenate([g_qkv, tail], axis=1)
     line.moved, g_qkv, in_sum, g_mid = sync(line.moved, g_qkv, in_sum, g_mid)
     g_qkv = to_dp(g_qkv)
     g_mid = over_seq(g_mid)
     line.start()
+    g_mid[1], patch_line.moved, out_sum, in_sum = sync(g_mid[1], patch_line.moved, out_sum, in_sum)
     patch_grad, g_w_out, g_w_in = patch_line.total(), add_all(out_sum), add_all(in_sum)
     line.moved, patch_grad, g_w_out, g_w_in, g_mid = sync(line.moved, patch_grad, g_w_out, g_w_in, g_mid)
     for _ in range(line.k, ns - 1):

time: 677 us -> 664 us (0.981)
  Pallas kernels: 208 us -> 197 us
    ppermute x27 -> x24, starting transfers between devices: 57.7 us -> 39.2 us  [send(): lax.ppermute(value, self.name, [(r, r ^ self.flip(m)) for r in range(self...]
    ppermute x27 -> x24, waiting for transfers between devices: 138 us -> 121 us  [send(): lax.ppermute(value, self.name, [(r, r ^ self.flip(m)) for r in range(self...]
    ppermute x3 -> x6, starting transfers between devices: 10.7 us -> 23.5 us  [line_step(): lax.ppermute(up, 'seq', [(r, r + 1) for r in range(ns - 1)])]
    pallas_call x2, Pallas kernels: 33.1 us -> 26.1 us  [weight_grads(): pl.pallas_call(functools.partial(grads_kernel, spans=tuple(spans), source...]
  transfers between devices with their start and end apart: 55 -> 58, of which waited for: 15 -> 17; matrix products, arithmetic and copies ran while one was open for 23% -> 23% of each run, Pallas kernels for 31% -> 30%
where the time goes in v4:
time: 664 us; the launch traced here: 655 us
  Pallas kernels  197 us (30%)
  waiting for transfers between devices  162 us (24%)
  starting transfers between devices  114 us (17%)
  matrix products  84.3 us (13%)
  other arithmetic  41.9 us (6%)
  local copies, waits for them, and re-layouts  40.6 us (6%)
  between operations  15.9 us (2%)
    ppermute x24, waiting for transfers between devices, send(): lax.ppermute(value, self.name, [(r, r ^ self.flip(m)) for r in range(self...  121 us
    pallas_call x3, Pallas kernels, attend_back(): pl.pallas_call(functools.partial(attend_back_kernel, kb=kb), grid=(pairs,...  76.9 us
    pallas_call x2, Pallas kernels, attend(): pl.pallas_call(functools.partial(attend_kernel, heads=step), grid=(heads...  46.2 us
    ppermute x24, starting transfers between devices, send(): lax.ppermute(value, self.name, [(r, r ^ self.flip(m)) for r in range(self...  39.2 us
    dot_general x7, matrix products, product_t(): lax.dot_general(a, b, (((1,), (1,)), ((), ())), preferred_element_type=F32)  32.9 us
    dot_general x6, matrix products, product(): return jnp.dot(a, b, preferred_element_type=F32)  32 us
    pallas_call x2, Pallas kernels, weight_grads(): pl.pallas_call(functools.partial(grads_kernel, spans=tuple(spans), source...  26.1 us
    ppermute x6, starting transfers between devices, start(): lax.ppermute(above.astype(BF), 'seq', [(r, r + 1) for r in range(k)])  26 us
  transfers between devices with their start and end apart: 58, of which 17 were waited for; matrix products, arithmetic and copies ran while one was open for 23% of the time, Pallas kernels for 30%

profile of v4, /device:TPU:0, one launch (start us, length us, event | category | flops | bytes accessed | tf_op | source)
XLA Modules:
  0.0 654.8 jit_solution(4218419173389308567)
XLA Ops:
  8.5 5.6 collective-permute-start
  25.9 14.3 %collective-permute-done.4 = bf16[32,896]{1,0:T(8,128)(2,1)S(1)} collective-permute-done((bf16[32,896]{1,0:T(8,128)(2,1)S(1)}, bf16[32,896]{1,0:T(8,128)(2,1)S(1)}, u32[]{:S(2)}, u32[]{:S(2)}) %collective-permute-start.4) | collective-permute-done | bytes 57376 | tf_op jit(solution)/shard_map/ppermute | solution.py:425
  55.5 30.5 %collective-permute-done.7 = bf16[32,5120]{1,0:T(8,128)(2,1)S(1)} collective-permute-done((bf16[32,5120]{1,0:T(8,128)(2,1)S(1)}, bf16[32,5120]{1,0:T(8,128)(2,1)S(1)}, u32[]{:S(2)}, u32[]{:S(2)}) %collective-permute-start.7) | collective-permute-done | bytes 327712 | tf_op jit(solution)/shard_map/ppermute | solution.py:425
  91.5 30.4 %collective-permute-done.10 = bf16[32,5120]{1,0:T(8,128)(2,1)S(1)} collective-permute-done((bf16[32,5120]{1,0:T(8,128)(2,1)S(1)}, bf16[32,5120]{1,0:T(8,128)(2,1)S(1)}, u32[]{:S(2)}, u32[]{:S(2)}) %collective-permute-start.10) | collective-permute-done | bytes 327712 | tf_op jit(solution)/shard_map/ppermute | solution.py:425
  137.7 11.3 %modulate.1 = (bf16[2048,1024]{1,0:T(8,128)(2,1)}, bf16[2048,1024]{1,0:T(8,128)(2,1)}) custom-call(s32[1]{0:T(128)} %bitcast.me_ref, bf16[512,1024]{1,0:T(8,128)(2,1)} %refs_0_.1, bf16[512,1024]{1,0:T(8,128)(2,1)} %copy-done.28, bf16[512,1024]{1,0:T(8,128)(2,1)} %copy-done.29, bf16[512,1024]{1,0:T(8,128)(2,1)} %copy-done.30, bf16[512,1024]{1,0:T(8,128)(2,1)} %copy-done.27, ...), custom_call_target="tpu_custom_call" | custom-call | flops 1 | bytes 1 | tf_op jit(solution)/shard_map/modulate/pallas_call | solution.py:300
  157.9 7.4 %convolution_convert_fusion.2.q_ref.k_ref.v_ref = bf16[2048,768]{1,0:T(8,128)(2,1)} fusion(bf16[2048,1024]{1,0:T(8,128)(2,1)} %get-tuple-element.198.refs_0_, bf16[1024,896]{1,0:T(8,128)(2,1)S(1)} %copy-done.25), kind=kOutput, calls=%fused_computation.6 | convolution fusion | flops 3222798336 | bytes 8912896 | tf_op jit(solution)/shard_map/dot_general | solution.py:24
  183.8 29.3 %attend.2 = (bf16[2048,256]{1,0:T(8,128)(2,1)}, f32[2,2,2048]{2,1,0:T(2,128)}) custom-call(bf16[2048,768]{1,0:T(8,128)(2,1)} %convolution_convert_fusion.2.q_ref.k_ref.v_ref, bf16[2048,768]{1,0:T(8,128)(2,1)} %convolution_convert_fusion.2.q_ref.k_ref.v_ref, bf16[2048,768]{1,0:T(8,128)(2,1)} %convolution_convert_fusion.2.q_ref.k_ref.v_ref, ...), custom_call_target="tpu_custom_call" | custom-call | flops 1 | bytes 1 | tf_op jit(solution)/shard_map/attend/pallas_call | solution.py:94
  223.2 8.2 %fusion.2.k_ref.v_ref = bf16[1024,2048]{1,0:T(8,128)(2,1)} fusion(bf16[1024,1024]{1,0:T(8,128)(2,1)S(1)} %constant_dynamic-slice_fusion.4.refs_2_, bf16[1024,5120]{1,0:T(8,128)(2,1)} %all-gather.7.cloned.1.call-done), kind=kOutput, calls=%fused_computation.5 | convolution fusion | flops 4297064448 | bytes 10485760 | tf_op jit(solution)/shard_map/dot_general | solution.py:24
  248.0 16.9 %attend.3 = (bf16[512,1024]{1,0:T(8,128)(2,1)}, f32[8,2,512]{2,1,0:T(2,128)}) custom-call(bf16[512,1024]{1,0:T(8,128)(2,1)} %fusion.40.q_ref, bf16[1024,2048]{1,0:T(8,128)(2,1)} %fusion.2.k_ref.v_ref, bf16[1024,2048]{1,0:T(8,128)(2,1)} %fusion.2.k_ref.v_ref, bf16[512,128]{1,0:T(8,128)(2,1)} %select_convert_fusion.3.qtag_ref, ...), custom_call_target="tpu_custom_call" | custom-call | flops 1 | bytes 1 | tf_op jit(solution)/shard_map/attend/pallas_call | solution.py:94
  271.0 12.4 %mlp_up.1 = (bf16[512,4096]{1,0:T(8,128)(2,1)}, bf16[512,4096]{1,0:T(8,128)(2,1)}) custom-call(bf16[512,1024]{1,0:T(8,128)(2,1)} %add_convert_fusion.6.a_ref, bf16[1024,4096]{1,0:T(8,128)(2,1)} %all-gather.9.cloned.1.call-done.w_ref, f32[1,4096]{1,0:T(1,128)} %bitcast.125), custom_call_target="tpu_custom_call" | custom-call | flops 1 | bytes 1 | tf_op jit(solution)/shard_map/mlp_up/pallas_call | solution.py:213
  283.4 9.2 %convolution_convert_fusion.1 = bf16[4096,1024]{1,0:T(8,128)(2,1)} fusion(bf16[512,4096]{1,0:T(8,128)(2,1)} %get-tuple-element.234, bf16[512,1024]{1,0:T(8,128)(2,1)S(1)} %copy-done.7), kind=kOutput, calls=%fused_computation.1 | convolution fusion | flops 4299161600 | bytes 13631488 | tf_op jit(solution)/shard_map/dot_general | solution.py:32
  292.5 9.3 %all-gather.11.cloned.1.call-done.w_ref = bf16[4096,1024]{1,0:T(8,128)(2,1)} async-done(((bf16[512,1024]{1,0:T(8,128)(2,1)}), bf16[4096,1024]{1,0:T(8,128)(2,1)}) %all-gather.11.cloned.1.call-update) | async-done | bytes 8388624 | tf_op jit(solution)/shard_map/all_gather | solution.py:529
  302.1 10.5 %mlp_back.1 = (bf16[512,4096]{1,0:T(8,128)(2,1)}, f32[1,4096]{1,0:T(1,128)}) custom-call(bf16[512,1024]{1,0:T(8,128)(2,1)} %g_ref.1, bf16[4096,1024]{1,0:T(8,128)(2,1)} %all-gather.11.cloned.1.call-done.w_ref, bf16[512,4096]{1,0:T(8,128)(2,1)} %get-tuple-element.240.slope_ref), custom_call_target="tpu_custom_call" | custom-call | flops 1 | bytes 1 | tf_op jit(solution)/shard_map/mlp_back/pallas_call | solution.py:240
  312.7 9.9 %convolution_convert_fusion = bf16[1024,4096]{1,0:T(8,128)(2,1)} fusion(bf16[512,1024]{1,0:T(8,128)(2,1)S(1)} %copy-done.22, bf16[512,4096]{1,0:T(8,128)(2,1)} %get-tuple-element.242), kind=kOutput, calls=%fused_computation | convolution fusion | flops 4299161600 | bytes 13631488 | tf_op jit(solution)/shard_map/dot_general | solution.py:32
  322.7 10.3 %multiply_reduce_fusion = (bf16[1024]{0:T(1024)(128)(2,1)S(1)}, f32[512]{0:T(512)S(1)}, f32[512]{0:T(512)S(1)}, bf16[1024]{0:T(1024)(128)(2,1)S(1)}, f32[512,1024]{1,0:T(8,128)S(1)}) fusion(f32[512,1024]{1,0:T(8,128)} %copy-done.2, f32[512]{0:T(512)S(1)} %add_rsqrt_fusion.1, f32[512]{0:T(512)S(1)} %broadcast_multiply_fusion.7, f32[1024]{0:T(1024)S(1)} %reshape.279, ...), kind=kOutput, calls=%fused_computation.26 | convolution fusion | flops 4299682816 | bytes 16793600 | tf_op jit(solution)/shard_map/dot_general | solution.py:28
  338.2 25.3 %attend_back.3 = (bf16[512,1024]{1,0:T(8,128)(2,1)}, bf16[1024,1024]{1,0:T(8,128)(2,1)}, bf16[1024,1024]{1,0:T(8,128)(2,1)}) custom-call(bf16[512,1024]{1,0:T(8,128)(2,1)} %fusion.40.q_ref, bf16[1024,2048]{1,0:T(8,128)(2,1)} %fusion.2.k_ref.v_ref, bf16[1024,2048]{1,0:T(8,128)(2,1)} %fusion.2.k_ref.v_ref, bf16[512,1024]{1,0:T(8,128)(2,1)} %fusion.43.do_ref, ...), custom_call_target="tpu_custom_call" | custom-call | flops 1 | bytes 1 | tf_op jit(solution)/shard_map/attend_back/pallas_call | solution.py:166
  373.7 4.7 all-to-all-start.1
  378.4 16.8 %weight_grads.2 = bf16[1024,5120]{1,0:T(8,128)(2,1)} custom-call(bf16[512,1024]{1,0:T(8,128)(2,1)} %bitcast.115, bf16[512,1024]{1,0:T(8,128)(2,1)} %copy-done.21, bf16[1024,1024]{1,0:T(8,128)(2,1)} %copy-done.11, bf16[512,1024]{1,0:T(8,128)(2,1)} %get-tuple-element.226.o_ref.refs_3_, bf16[512,1024]{1,0:T(8,128)(2,1)} %copy-done.19, ...), custom_call_target="tpu_custom_call" | custom-call | flops 1 | bytes 1 | tf_op jit(solution)/shard_map/weight_grads/pallas_call | solution.py:403
  395.2 5.0 fusion.14
  400.2 5.5 add_convert_fusion
  405.7 5.5 add_convert_fusion.5
  416.0 4.7 collective-permute-start.24
  426.6 25.3 %attend_back.4 = (bf16[2048,128]{1,0:T(8,128)(2,1)}, bf16[2048,128]{1,0:T(8,128)(2,1)}, bf16[2048,128]{1,0:T(8,128)(2,1)}) custom-call(bf16[2048,768]{1,0:T(8,128)(2,1)} %convolution_convert_fusion.2.q_ref.k_ref.v_ref, bf16[2048,768]{1,0:T(8,128)(2,1)} %convolution_convert_fusion.2.q_ref.k_ref.v_ref, ...), custom_call_target="tpu_custom_call" | custom-call | flops 1 | bytes 1 | tf_op jit(solution)/shard_map/attend_back/pallas_call | solution.py:166
  468.0 26.3 %attend_back.5 = (bf16[2048,128]{1,0:T(8,128)(2,1)}, bf16[2048,128]{1,0:T(8,128)(2,1)}, bf16[2048,128]{1,0:T(8,128)(2,1)}) custom-call(bf16[2048,768]{1,0:T(8,128)(2,1)} %convolution_convert_fusion.2.q_ref.k_ref.v_ref, bf16[2048,768]{1,0:T(8,128)(2,1)} %convolution_convert_fusion.2.q_ref.k_ref.v_ref, ...), custom_call_target="tpu_custom_call" | custom-call | flops 1 | bytes 1 | tf_op jit(solution)/shard_map/attend_back/pallas_call | solution.py:166
  497.1 5.5 collective-permute-start.34
  505.2 13.5 %modulate_back.1 = (bf16[2048,1024]{1,0:T(8,128)(2,1)}, f32[4,2048]{1,0:T(4,128)}) custom-call(bf16[2048,256]{1,0:T(8,128)(2,1)} %copy-done.14, bf16[2048,256]{1,0:T(8,128)(2,1)} %copy-done.13, bf16[2048,256]{1,0:T(8,128)(2,1)} %copy-done.12, bf16[1024,768]{1,0:T(8,128)(2,1)} %slice.106.w_ref, bf16[2048,1024]{1,0:T(8,128)(2,1)} %get-tuple-element.273.x_ref, ...), custom_call_target="tpu_custom_call" | custom-call | flops 1 | bytes 1 | tf_op jit(solution)/shard_map/modulate_back/pallas_call | solution.py:352
  528.8 9.3 %weight_grads.3 = bf16[1024,768]{1,0:T(8,128)(2,1)} custom-call(bf16[2048,1024]{1,0:T(8,128)(2,1)} %get-tuple-element.198.refs_0_, bf16[2048,256]{1,0:T(8,128)(2,1)} %copy-done.14, bf16[2048,256]{1,0:T(8,128)(2,1)} %copy-done.13, bf16[2048,256]{1,0:T(8,128)(2,1)} %copy-done.12), custom_call_target="tpu_custom_call" | custom-call | flops 1 | bytes 1 | tf_op jit(solution)/shard_map/weight_grads/pallas_call | solution.py:403
  541.1 6.1 collective-permute-done.36
  568.6 19.7 %collective-permute-done.42 = bf16[32,5120]{1,0:T(8,128)(2,1)S(1)} collective-permute-done((bf16[32,5120]{1,0:T(8,128)(2,1)S(1)}, bf16[32,5120]{1,0:T(8,128)(2,1)S(1)}, u32[]{:S(2)}, u32[]{:S(2)}) %collective-permute-start.42) | collective-permute-done | bytes 327712 | tf_op jit(solution)/shard_map/ppermute | solution.py:425
  588.3 17.0 %collective-permute-done.41 = bf16[32,5120]{1,0:T(8,128)(2,1)S(1)} collective-permute-done((bf16[32,5120]{1,0:T(8,128)(2,1)S(1)}, bf16[32,5120]{1,0:T(8,128)(2,1)S(1)}, u32[]{:S(2)}, u32[]{:S(2)}) %collective-permute-start.41) | collective-permute-done | bytes 327712 | tf_op jit(solution)/shard_map/ppermute | solution.py:425
  607.7 5.6 collective-permute-start.43
  613.4 15.2 %collective-permute-done.44 = bf16[512,1024]{1,0:T(8,128)(2,1)S(1)} collective-permute-done((bf16[512,1024]{1,0:T(8,128)(2,1)S(1)}, bf16[512,1024]{1,0:T(8,128)(2,1)S(1)}, u32[]{:S(2)}, u32[]{:S(2)}) %collective-permute-start.44) | collective-permute-done | bytes 1048608 | tf_op jit(solution)/shard_map/ppermute | solution.py:487
  (364 shorter events, 212.3 us)
Async XLA Ops:
  7.2 120.6 %all-gather.5.cloned.1.call-start = ((), (), s32[]{:S(2)}) async-start(), calls=%async_computation.6 | async-start | bytes 2064384 | tf_op jit(solution)/shard_map/all_gather | solution.py:551
  7.2 34.4 %collective-permute-start.1 = (bf16[512,1024]{1,0:T(8,128)(2,1)}, bf16[512,1024]{1,0:T(8,128)(2,1)S(1)}, u32[]{:S(2)}, u32[]{:S(2)}) collective-permute-start(bf16[512,1024]{1,0:T(8,128)(2,1)} %refs_0_.1), channel_id=1, source_target_pairs={{1,0},{2,1},{3,2},{5,4},{6,5},{7,6},{9,8},{10,9},{11,10},{13,12},{... | collective-permute-start | bytes 3145736 | tf_op jit(solution)/shard_map/ppermute | solution.py:497
  8.5 33.1 %collective-permute-start = (bf16[512,1024]{1,0:T(8,128)(2,1)}, bf16[512,1024]{1,0:T(8,128)(2,1)S(1)}, u32[]{:S(2)}, u32[]{:S(2)}) collective-permute-start(bf16[512,1024]{1,0:T(8,128)(2,1)} %refs_0_.1), channel_id=1, source_target_pairs={{0,1},{1,2},{2,3},{4,5},{5,6},{6,7},{8,9},{9,10},{10,11},{12,13},{... | collective-permute-start | bytes 3145736 | tf_op jit(solution)/shard_map/ppermute | solution.py:496
  42.3 43.8 %collective-permute-start.5 = (bf16[512,1024]{1,0:T(8,128)(2,1)S(1)}, bf16[512,1024]{1,0:T(8,128)(2,1)S(1)}, u32[]{:S(2)}, u32[]{:S(2)}) collective-permute-start(bf16[512,1024]{1,0:T(8,128)(2,1)S(1)} %collective-permute-done.refs_1_), channel_id=1, source_target_pairs={{0,1},{1,2},{2,3},{4,5},{5,6},{6,7},{8,9},{9,10},{10,11},{12,13},{... | collective-permute-start | bytes 3145736 | tf_op jit(solution)/shard_map/ppermute | solution.py:496
  46.0 40.1 %collective-permute-start.6 = (bf16[512,1024]{1,0:T(8,128)(2,1)S(1)}, bf16[512,1024]{1,0:T(8,128)(2,1)}, u32[]{:S(2)}, u32[]{:S(2)}) collective-permute-start(bf16[512,1024]{1,0:T(8,128)(2,1)S(1)} %collective-permute-done.1.refs_4_), channel_id=1, source_target_pairs={{1,0},{2,1},{3,2},{5,4},{6,5},{7,6},{9,8},{10,9},{11,10},{13,12},{... | collective-permute-start | bytes 3145736 | tf_op jit(solution)/shard_map/ppermute | solution.py:497
  50.7 162.5 %all-gather.7.cloned.1.call-start = ((), (), s32[]{:S(2)}) async-start(), calls=%async_computation.7 | async-start | bytes 11796480 | tf_op jit(solution)/shard_map/all_gather | solution.py:529
  51.6 34.4 %collective-permute-start.7 = (bf16[32,5120]{1,0:T(8,128)(2,1)S(1)}, bf16[32,5120]{1,0:T(8,128)(2,1)S(1)}, u32[]{:S(2)}, u32[]{:S(2)}) collective-permute-start(bf16[32,5120]{1,0:T(8,128)(2,1)S(1)} %constant_dynamic-update-slice_fusion), channel_id=1, source_target_pairs={{0,2},{1,3},{2,0},{3,1},{4,6},{5,7},{6,4},{7,5},{8,10},{9,11},{10,... | collective-permute-start | bytes 983048 | tf_op jit(solution)/shard_map/ppermute | solution.py:425
  86.0 39.4 %collective-permute-start.8 = (bf16[512,1024]{1,0:T(8,128)(2,1)S(1)}, bf16[512,1024]{1,0:T(8,128)(2,1)S(1)}, u32[]{:S(2)}, u32[]{:S(2)}) collective-permute-start(bf16[512,1024]{1,0:T(8,128)(2,1)S(1)} %collective-permute-done.5.refs_2_), channel_id=1, source_target_pairs={{0,1},{1,2},{2,3},{4,5},{5,6},{6,7},{8,9},{9,10},{10,11},{12,13},{... | collective-permute-start | bytes 3145736 | tf_op jit(solution)/shard_map/ppermute | solution.py:496
  87.4 39.0 %collective-permute-start.9 = (bf16[512,1024]{1,0:T(8,128)(2,1)}, bf16[512,1024]{1,0:T(8,128)(2,1)}, u32[]{:S(2)}, u32[]{:S(2)}) collective-permute-start(bf16[512,1024]{1,0:T(8,128)(2,1)} %collective-permute-done.6.refs_5_), channel_id=1, source_target_pairs={{1,0},{2,1},{3,2},{5,4},{6,5},{7,6},{9,8},{10,9},{11,10},{13,12},{... | collective-permute-start | bytes 3145736 | tf_op jit(solution)/shard_map/ppermute | solution.py:497
  88.7 33.2 %collective-permute-start.10 = (bf16[32,5120]{1,0:T(8,128)(2,1)S(1)}, bf16[32,5120]{1,0:T(8,128)(2,1)S(1)}, u32[]{:S(2)}, u32[]{:S(2)}) collective-permute-start(bf16[32,5120]{1,0:T(8,128)(2,1)S(1)} %constant_dynamic-update-slice_fusion), channel_id=1, source_target_pairs={{0,1},{1,0},{2,3},{3,2},{4,5},{5,4},{6,7},{7,6},{8,9},{9,8},{10,11... | collective-permute-start | bytes 983048 | tf_op jit(solution)/shard_map/ppermute | solution.py:425
  91.4 34.0 %collective-permute-start.11 = (bf16[32,5120]{1,0:T(8,128)(2,1)S(1)}, bf16[32,5120]{1,0:T(8,128)(2,1)S(1)}, u32[]{:S(2)}, u32[]{:S(2)}) collective-permute-start(bf16[32,5120]{1,0:T(8,128)(2,1)S(1)} %collective-permute-done.7), channel_id=1, source_target_pairs={{0,1},{1,0},{2,3},{3,2},{4,5},{5,4},{6,7},{7,6},{8,9},{9,8},{10,11... | collective-permute-start | bytes 983048 | tf_op jit(solution)/shard_map/ppermute | solution.py:425
  127.7 143.2 %all-gather.9.cloned.1.call-start = ((), (), s32[]{:S(2)}) async-start(), calls=%async_computation.8 | async-start | bytes 9437184 | tf_op jit(solution)/shard_map/all_gather | solution.py:529
  174.6 38.6 %collective-permute-start.21 = (bf16[128,1024]{1,0:T(8,128)(2,1)}, bf16[128,1024]{1,0:T(8,128)(2,1)}, u32[]{:S(2)}, u32[]{:S(2)}) collective-permute-start(bf16[128,1024]{1,0:T(8,128)(2,1)} %param.37), channel_id=1, source_target_pairs={{0,2},{1,3},{2,0},{3,1},{4,6},{5,7},{6,4},{7,5},{8,10},{9,11},{10,... | collective-permute-start | bytes 786440 | tf_op jit(solution)/shard_map/ppermute | solution.py:425
  176.4 36.7 %collective-permute-start.19 = (bf16[256,1024]{1,0:T(8,128)(2,1)S(1)}, bf16[256,1024]{1,0:T(8,128)(2,1)S(1)}, u32[]{:S(2)}, u32[]{:S(2)}) collective-permute-start(bf16[256,1024]{1,0:T(8,128)(2,1)S(1)} %collective-permute-done.17), channel_id=1, source_target_pairs={{0,1},{1,2},{2,3},{4,5},{5,6},{6,7},{8,9},{9,10},{10,11},{12,13},{... | collective-permute-start | bytes 1572872 | tf_op jit(solution)/shard_map/ppermute | solution.py:496
  217.0 84.9 %all-gather.11.cloned.1.call-start = ((), (), s32[]{:S(2)}) async-start(), calls=%async_computation.9 | async-start | bytes 9437184 | tf_op jit(solution)/shard_map/all_gather | solution.py:529
  245.0 166.2 %reduce-scatter.5.cloned.1.call-start = ((), (), s32[]{:S(2)}) async-start(), calls=%async_computation.10 | async-start | bytes 9437184 | tf_op jit(solution)/shard_map/reduce_scatter | solution.py:516
  301.9 150.0 %reduce-scatter.7.cloned.1.call-start = ((), (), s32[]{:S(2)}) async-start(), calls=%async_computation.11 | async-start | bytes 9437184 | tf_op jit(solution)/shard_map/reduce_scatter | solution.py:516
  373.7 37.5 %all-to-all-start.1 = ((bf16[512,4,256]{2,0,1:T(8,128)(2,1)}), bf16[512,4,256]{2,0,1:T(8,128)(2,1)S(1)}, u32[]{:S(2)}, u32[]{:S(2)}) async-start(bf16[512,4,256]{2,0,1:T(8,128)(2,1)} %bitcast.107), calls=%async_computation.1 | async-start | bytes 2097152 | tf_op jit(solution)/shard_map/all_to_all | solution.py:664
  378.4 168.8 %reduce-scatter.9.cloned.1.call-start = ((), (), s32[]{:S(2)}) async-start(), calls=%async_computation.12 | async-start | bytes 11796480 | tf_op jit(solution)/shard_map/reduce_scatter | solution.py:516
  412.2 217.6 %reduce-scatter.11.cloned.1.call-start = ((), (), s32[]{:S(2)}) async-start(), calls=%async_computation.13 | async-start | bytes 2064384 | tf_op jit(solution)/shard_map/reduce_scatter | solution.py:516
  414.5 37.4 %collective-permute-start.25 = (bf16[256,1024]{1,0:T(8,128)(2,1)}, bf16[256,1024]{1,0:T(8,128)(2,1)}, u32[]{:S(2)}, u32[]{:S(2)}) collective-permute-start(bf16[256,1024]{1,0:T(8,128)(2,1)} %get-tuple-element.417), channel_id=1, source_target_pairs={{3,2},{7,6},{11,10},{15,14},{19,18},{23,22},{27,26},{31,30}} | collective-permute-start | bytes 1572872 | tf_op jit(solution)/shard_map/ppermute | solution.py:487
  416.0 36.0 %collective-permute-start.24 = (bf16[256,1024]{1,0:T(8,128)(2,1)}, bf16[256,1024]{1,0:T(8,128)(2,1)}, u32[]{:S(2)}, u32[]{:S(2)}) collective-permute-start(bf16[256,1024]{1,0:T(8,128)(2,1)} %get-tuple-element.418), channel_id=1, source_target_pairs={{0,1},{4,5},{8,9},{12,13},{16,17},{20,21},{24,25},{28,29}} | collective-permute-start | bytes 1572872 | tf_op jit(solution)/shard_map/ppermute | solution.py:486
  422.2 37.9 %collective-permute-start.30 = (bf16[128,1024]{1,0:T(8,128)(2,1)}, bf16[128,1024]{1,0:T(8,128)(2,1)}, u32[]{:S(2)}, u32[]{:S(2)}) collective-permute-start(bf16[128,1024]{1,0:T(8,128)(2,1)} %get-tuple-element.431), channel_id=1, source_target_pairs={{0,3},{1,2},{2,1},{3,0},{4,7},{5,6},{6,5},{7,4},{8,11},{9,10},{10,... | collective-permute-start | bytes 786440 | tf_op jit(solution)/shard_map/ppermute | solution.py:425
  424.6 37.3 %collective-permute-start.29 = (bf16[128,1024]{1,0:T(8,128)(2,1)}, bf16[128,1024]{1,0:T(8,128)(2,1)}, u32[]{:S(2)}, u32[]{:S(2)}) collective-permute-start(bf16[128,1024]{1,0:T(8,128)(2,1)} %get-tuple-element.432), channel_id=1, source_target_pairs={{0,2},{1,3},{2,0},{3,1},{4,6},{5,7},{6,4},{7,5},{8,10},{9,11},{10,... | collective-permute-start | bytes 786440 | tf_op jit(solution)/shard_map/ppermute | solution.py:425
  424.6 39.6 %collective-permute-start.28 = (bf16[128,1024]{1,0:T(8,128)(2,1)}, bf16[128,1024]{1,0:T(8,128)(2,1)}, u32[]{:S(2)}, u32[]{:S(2)}) collective-permute-start(bf16[128,1024]{1,0:T(8,128)(2,1)} %get-tuple-element.433), channel_id=1, source_target_pairs={{0,1},{1,0},{2,3},{3,2},{4,5},{5,4},{6,7},{7,6},{8,9},{9,8},{10,11... | collective-permute-start | bytes 786440 | tf_op jit(solution)/shard_map/ppermute | solution.py:425
  454.7 39.6 %collective-permute-start.27 = (bf16[256,1024]{1,0:T(8,128)(2,1)}, bf16[256,1024]{1,0:T(8,128)(2,1)S(1)}, u32[]{:S(2)}, u32[]{:S(2)}) collective-permute-start(bf16[256,1024]{1,0:T(8,128)(2,1)} %get-tuple-element.415), channel_id=1, source_target_pairs={{3,2},{2,1},{7,6},{6,5},{11,10},{10,9},{15,14},{14,13},{19,18},{18... | collective-permute-start | bytes 1572872 | tf_op jit(solution)/shard_map/ppermute | solution.py:487
  455.5 38.8 %collective-permute-start.26 = (bf16[256,1024]{1,0:T(8,128)(2,1)}, bf16[256,1024]{1,0:T(8,128)(2,1)S(1)}, u32[]{:S(2)}, u32[]{:S(2)}) collective-permute-start(bf16[256,1024]{1,0:T(8,128)(2,1)} %get-tuple-element.416), channel_id=1, source_target_pairs={{0,1},{1,2},{4,5},{5,6},{8,9},{9,10},{12,13},{13,14},{16,17},{17,1... | collective-permute-start | bytes 1572872 | tf_op jit(solution)/shard_map/ppermute | solution.py:486
  460.1 34.2 %collective-permute-start.33 = (bf16[32,4096]{1,0:T(8,128)(2,1)}, bf16[32,4096]{1,0:T(8,128)(2,1)}, u32[]{:S(2)}, u32[]{:S(2)}) collective-permute-start(bf16[32,4096]{1,0:T(8,128)(2,1)} %get-tuple-element.427), channel_id=1, source_target_pairs={{0,3},{1,2},{2,1},{3,0},{4,7},{5,6},{6,5},{7,4},{8,11},{9,10},{10,... | collective-permute-start | bytes 786440 | tf_op jit(solution)/shard_map/ppermute | solution.py:425
  461.9 32.4 %collective-permute-start.32 = (bf16[32,4096]{1,0:T(8,128)(2,1)}, bf16[32,4096]{1,0:T(8,128)(2,1)}, u32[]{:S(2)}, u32[]{:S(2)}) collective-permute-start(bf16[32,4096]{1,0:T(8,128)(2,1)} %get-tuple-element.428), channel_id=1, source_target_pairs={{0,2},{1,3},{2,0},{3,1},{4,6},{5,7},{6,4},{7,5},{8,10},{9,11},{10,... | collective-permute-start | bytes 786440 | tf_op jit(solution)/shard_map/ppermute | solution.py:425
  554.4 51.0 %collective-permute-start.39 = (bf16[512,1024]{1,0:T(8,128)(2,1)S(1)}, bf16[512,1024]{1,0:T(8,128)(2,1)S(1)}, u32[]{:S(2)}, u32[]{:S(2)}) collective-permute-start(bf16[512,1024]{1,0:T(8,128)(2,1)S(1)} %get-tuple-element.409), channel_id=1, source_target_pairs={{3,2},{2,1},{7,6},{6,5},{11,10},{10,9},{15,14},{14,13},{19,18},{18... | collective-permute-start | bytes 3145736 | tf_op jit(solution)/shard_map/ppermute | solution.py:487
  555.2 50.1 %collective-permute-start.38 = (bf16[512,1024]{1,0:T(8,128)(2,1)S(1)}, bf16[512,1024]{1,0:T(8,128)(2,1)S(1)}, u32[]{:S(2)}, u32[]{:S(2)}) collective-permute-start(bf16[512,1024]{1,0:T(8,128)(2,1)S(1)} %get-tuple-element.410), channel_id=1, source_target_pairs={{0,1},{1,2},{4,5},{5,6},{8,9},{9,10},{12,13},{13,14},{16,17},{17,1... | collective-permute-start | bytes 3145736 | tf_op jit(solution)/shard_map/ppermute | solution.py:486
  557.8 47.6 %collective-permute-start.41 = (bf16[32,5120]{1,0:T(8,128)(2,1)S(1)}, bf16[32,5120]{1,0:T(8,128)(2,1)S(1)}, u32[]{:S(2)}, u32[]{:S(2)}) collective-permute-start(bf16[32,5120]{1,0:T(8,128)(2,1)S(1)} %get-tuple-element.420), channel_id=1, source_target_pairs={{0,2},{1,3},{2,0},{3,1},{4,6},{5,7},{6,4},{7,5},{8,10},{9,11},{10,... | collective-permute-start | bytes 983048 | tf_op jit(solution)/shard_map/ppermute | solution.py:425
  (88 other events, 1302.1 us)
Sparse Core Ops, SparseCore 0:
  50.8 30.7 all-gather.4
  127.8 61.4 all-gather.6
  191.2 54.4 all-gather.8
  247.5 54.3 all-gather.10
  305.2 71.2 reduce-scatter.4
  380.2 71.2 reduce-scatter.6
  455.0 81.5 reduce-scatter.8
  547.3 38.8 reduce-scatter.10

commit v5 on v4

--- a/solution.py
+++ b/solution.py
@@ -670,8 +670,7 @@
         [(self_att, [d_self_out]), (act_two, [d_cq]), (patch_all, [d_ck, d_cv]), (cross_att, [d_cross_out])]
     )
     patch_part = (product_t(d_ck, w_cross_kv[:, :width]) + product_t(d_cv, w_cross_kv[:, width:])).astype(BF)
-    block_out = (resid_three + product(hid, w_out) + out_bias).astype(BF)
-    d_self_mine, g_mid, patch_part, block_out, g_w_out = sync(d_self_mine, g_mid, patch_part, block_out, g_w_out)
+    d_self_mine, g_mid, patch_part, g_w_out = sync(d_self_mine, g_mid, patch_part, g_w_out)
     g_mid = to_dp(g_mid)
     out_sum, in_sum = over_seq(g_w_out), None
     patch_line = LineSum(patch_part, ns)
@@ -708,13 +707,17 @@
     tail = jnp.pad(tail, ((0, 0), (0, extra * w_rows - length))).reshape(n_dev * w_rows, extra).astype(BF)
     g_qkv = weight_grads([(act_one, [d_q, d_k, d_v])])
     g_qkv = jnp.concatenate([g_qkv, tail], axis=1)
-    line.moved, g_qkv, in_sum, g_mid = sync(line.moved, g_qkv, in_sum, g_mid)
+    g_qkv, in_sum, g_mid = sync(g_qkv, in_sum, g_mid)
+    g_mid = over_seq(g_mid)
+    line.moved, g_qkv, g_mid[1], hid = sync(line.moved, g_qkv, g_mid[1], hid)
     g_qkv = to_dp(g_qkv)
-    g_mid = over_seq(g_mid)
     line.start()
-    g_mid[1], patch_line.moved, out_sum, in_sum = sync(g_mid[1], patch_line.moved, out_sum, in_sum)
+    g_mid[2], hid, patch_line.moved, out_sum, in_sum = sync(g_mid[2], hid, patch_line.moved, out_sum, in_sum)
+    block_out = (resid_three + product(hid, w_out) + out_bias).astype(BF)
     patch_grad, g_w_out, g_w_in = patch_line.total(), add_all(out_sum), add_all(in_sum)
-    line.moved, patch_grad, g_w_out, g_w_in, g_mid = sync(line.moved, patch_grad, g_w_out, g_w_in, g_mid)
+    line.moved, patch_grad, g_w_out, g_w_in, g_mid, block_out = sync(
+        line.moved, patch_grad, g_w_out, g_w_in, g_mid, block_out
+    )
     for _ in range(line.k, ns - 1):
         line.start()
     g_mid = add_all(g_mid)

time: 664 us -> 662 us (level)
  waiting for transfers between devices: 162 us -> 145 us
    ppermute x24, waiting for transfers between devices: 121 us -> 102 us  [send(): lax.ppermute(value, self.name, [(r, r ^ self.flip(m)) for r in range(self...]
  transfers between devices with their start and end apart: 58 -> 58, of which waited for: 17 -> 18; matrix products, arithmetic and copies ran while one was open for 23% -> 25% of each run, Pallas kernels for 30% -> 30%
where the time goes in v5:
time: 662 us; the launch traced here: 652 us
  Pallas kernels  197 us (30%)
  waiting for transfers between devices  145 us (22%)
  starting transfers between devices  118 us (18%)
  matrix products  86.8 us (13%)
  other arithmetic  47 us (7%)
  local copies, waits for them, and re-layouts  42 us (6%)
  between operations  15.8 us (2%)
    ppermute x24, waiting for transfers between devices, send(): lax.ppermute(value, self.name, [(r, r ^ self.flip(m)) for r in range(self...  102 us
    pallas_call x3, Pallas kernels, attend_back(): pl.pallas_call(functools.partial(attend_back_kernel, kb=kb), grid=(pairs,...  76.8 us
    pallas_call x2, Pallas kernels, attend(): pl.pallas_call(functools.partial(attend_kernel, heads=step), grid=(heads...  46.3 us
    ppermute x24, starting transfers between devices, send(): lax.ppermute(value, self.name, [(r, r ^ self.flip(m)) for r in range(self...  37.3 us
    dot_general x6, matrix products, product(): return jnp.dot(a, b, preferred_element_type=F32)  35.9 us
    dot_general x7, matrix products, product_t(): lax.dot_general(a, b, (((1,), (1,)), ((), ())), preferred_element_type=F32)  31.6 us
    ppermute x6, starting transfers between devices, start(): lax.ppermute(above.astype(BF), 'seq', [(r, r + 1) for r in range(k)])  31.5 us
    pallas_call x2, Pallas kernels, weight_grads(): pl.pallas_call(functools.partial(grads_kernel, spans=tuple(spans), source...  26.3 us
  transfers between devices with their start and end apart: 58, of which 18 were waited for; matrix products, arithmetic and copies ran while one was open for 25% of the time, Pallas kernels for 30%

profile of v5, /device:TPU:0, one launch (start us, length us, event | category | flops | bytes accessed | tf_op | source)
XLA Modules:
  0.0 652.2 jit_solution(934964239202559067)
XLA Ops:
  8.5 5.6 collective-permute-start
  25.9 14.3 %collective-permute-done.4 = bf16[32,896]{1,0:T(8,128)(2,1)S(1)} collective-permute-done((bf16[32,896]{1,0:T(8,128)(2,1)S(1)}, bf16[32,896]{1,0:T(8,128)(2,1)S(1)}, u32[]{:S(2)}, u32[]{:S(2)}) %collective-permute-start.4) | collective-permute-done | bytes 57376 | tf_op jit(solution)/shard_map/ppermute | solution.py:425
  55.5 30.5 %collective-permute-done.7 = bf16[32,5120]{1,0:T(8,128)(2,1)S(1)} collective-permute-done((bf16[32,5120]{1,0:T(8,128)(2,1)S(1)}, bf16[32,5120]{1,0:T(8,128)(2,1)S(1)}, u32[]{:S(2)}, u32[]{:S(2)}) %collective-permute-start.7) | collective-permute-done | bytes 327712 | tf_op jit(solution)/shard_map/ppermute | solution.py:425
  91.5 30.4 %collective-permute-done.10 = bf16[32,5120]{1,0:T(8,128)(2,1)S(1)} collective-permute-done((bf16[32,5120]{1,0:T(8,128)(2,1)S(1)}, bf16[32,5120]{1,0:T(8,128)(2,1)S(1)}, u32[]{:S(2)}, u32[]{:S(2)}) %collective-permute-start.10) | collective-permute-done | bytes 327712 | tf_op jit(solution)/shard_map/ppermute | solution.py:425
  137.8 11.3 %modulate.1 = (bf16[2048,1024]{1,0:T(8,128)(2,1)}, bf16[2048,1024]{1,0:T(8,128)(2,1)}) custom-call(s32[1]{0:T(128)} %bitcast.me_ref, bf16[512,1024]{1,0:T(8,128)(2,1)} %refs_0_.1, bf16[512,1024]{1,0:T(8,128)(2,1)} %copy-done.24, bf16[512,1024]{1,0:T(8,128)(2,1)} %copy-done.25, bf16[512,1024]{1,0:T(8,128)(2,1)} %copy-done.26, bf16[512,1024]{1,0:T(8,128)(2,1)} %copy-done.23, ...), custom_call_target="tpu_custom_call" | custom-call | flops 1 | bytes 1 | tf_op jit(solution)/shard_map/modulate/pallas_call | solution.py:300
  157.7 7.6 %convolution_convert_fusion.2.q_ref.k_ref.v_ref = bf16[2048,768]{1,0:T(8,128)(2,1)} fusion(bf16[2048,1024]{1,0:T(8,128)(2,1)} %get-tuple-element.202.refs_0_, bf16[1024,896]{1,0:T(8,128)(2,1)S(1)} %copy-done.21), kind=kOutput, calls=%fused_computation.6 | convolution fusion | flops 3222798336 | bytes 8912896 | tf_op jit(solution)/shard_map/dot_general | solution.py:24
  182.7 29.2 %attend.2 = (bf16[2048,256]{1,0:T(8,128)(2,1)}, f32[2,2,2048]{2,1,0:T(2,128)}) custom-call(bf16[2048,768]{1,0:T(8,128)(2,1)} %convolution_convert_fusion.2.q_ref.k_ref.v_ref, bf16[2048,768]{1,0:T(8,128)(2,1)} %convolution_convert_fusion.2.q_ref.k_ref.v_ref, bf16[2048,768]{1,0:T(8,128)(2,1)} %convolution_convert_fusion.2.q_ref.k_ref.v_ref, ...), custom_call_target="tpu_custom_call" | custom-call | flops 1 | bytes 1 | tf_op jit(solution)/shard_map/attend/pallas_call | solution.py:94
  223.9 8.3 %fusion.2.k_ref.v_ref = bf16[1024,2048]{1,0:T(8,128)(2,1)} fusion(bf16[1024,1024]{1,0:T(8,128)(2,1)S(1)} %constant_dynamic-slice_fusion.4.refs_2_, bf16[1024,5120]{1,0:T(8,128)(2,1)} %all-gather.7.cloned.1.call-done), kind=kOutput, calls=%fused_computation.5 | convolution fusion | flops 4297064448 | bytes 10485760 | tf_op jit(solution)/shard_map/dot_general | solution.py:24
  247.7 17.1 %attend.3 = (bf16[512,1024]{1,0:T(8,128)(2,1)}, f32[8,2,512]{2,1,0:T(2,128)}) custom-call(bf16[512,1024]{1,0:T(8,128)(2,1)} %fusion.40.q_ref, bf16[1024,2048]{1,0:T(8,128)(2,1)} %fusion.2.k_ref.v_ref, bf16[1024,2048]{1,0:T(8,128)(2,1)} %fusion.2.k_ref.v_ref, bf16[512,128]{1,0:T(8,128)(2,1)} %select_convert_fusion.3.qtag_ref, ...), custom_call_target="tpu_custom_call" | custom-call | flops 1 | bytes 1 | tf_op jit(solution)/shard_map/attend/pallas_call | solution.py:94
  269.9 12.8 %mlp_up.1 = (bf16[512,4096]{1,0:T(8,128)(2,1)}, bf16[512,4096]{1,0:T(8,128)(2,1)}) custom-call(bf16[512,1024]{1,0:T(8,128)(2,1)} %add_convert_fusion.6.a_ref, bf16[1024,4096]{1,0:T(8,128)(2,1)} %all-gather.9.cloned.1.call-done.w_ref, f32[1,4096]{1,0:T(1,128)} %bitcast.122), custom_call_target="tpu_custom_call" | custom-call | flops 1 | bytes 1 | tf_op jit(solution)/shard_map/mlp_up/pallas_call | solution.py:213
  282.7 9.2 %convolution_convert_fusion.1 = bf16[4096,1024]{1,0:T(8,128)(2,1)} fusion(bf16[512,4096]{1,0:T(8,128)(2,1)} %get-tuple-element.327, bf16[512,1024]{1,0:T(8,128)(2,1)S(1)} %copy-done.6), kind=kOutput, calls=%fused_computation.1 | convolution fusion | flops 4299161600 | bytes 13631488 | tf_op jit(solution)/shard_map/dot_general | solution.py:32
  291.9 10.0 %all-gather.11.cloned.1.call-done.w_ref = bf16[4096,1024]{1,0:T(8,128)(2,1)} async-done(((bf16[512,1024]{1,0:T(8,128)(2,1)}), bf16[4096,1024]{1,0:T(8,128)(2,1)}) %all-gather.11.cloned.1.call-update) | async-done | bytes 8388624 | tf_op jit(solution)/shard_map/all_gather | solution.py:529
  302.2 10.5 %mlp_back.1 = (bf16[512,4096]{1,0:T(8,128)(2,1)}, f32[1,4096]{1,0:T(1,128)}) custom-call(bf16[512,1024]{1,0:T(8,128)(2,1)} %g_ref.1, bf16[4096,1024]{1,0:T(8,128)(2,1)} %all-gather.11.cloned.1.call-done.w_ref, bf16[512,4096]{1,0:T(8,128)(2,1)} %get-tuple-element.244.slope_ref), custom_call_target="tpu_custom_call" | custom-call | flops 1 | bytes 1 | tf_op jit(solution)/shard_map/mlp_back/pallas_call | solution.py:240
  312.7 9.8 %convolution_convert_fusion = bf16[1024,4096]{1,0:T(8,128)(2,1)} fusion(bf16[512,1024]{1,0:T(8,128)(2,1)S(1)} %copy-done.18, bf16[512,4096]{1,0:T(8,128)(2,1)} %get-tuple-element.246), kind=kOutput, calls=%fused_computation | convolution fusion | flops 4299161600 | bytes 13631488 | tf_op jit(solution)/shard_map/dot_general | solution.py:32
  322.5 8.9 %multiply_reduce_fusion = (bf16[1024]{0:T(1024)(128)(2,1)S(1)}, f32[512]{0:T(512)S(1)}, f32[512]{0:T(512)S(1)}, bf16[1024]{0:T(1024)(128)(2,1)S(1)}, f32[512,1024]{1,0:T(8,128)S(1)}) fusion(f32[512,1024]{1,0:T(8,128)S(1)} %get-tuple-element.490, f32[512]{0:T(512)S(1)} %add_rsqrt_fusion.1, f32[512]{0:T(512)S(1)} %broadcast_multiply_fusion.7, ...), kind=kOutput, calls=%fused_computation.27 | convolution fusion | flops 4299682816 | bytes 16793600 | tf_op jit(solution)/shard_map/dot_general | solution.py:28
  336.5 25.3 %attend_back.3 = (bf16[512,1024]{1,0:T(8,128)(2,1)}, bf16[1024,1024]{1,0:T(8,128)(2,1)}, bf16[1024,1024]{1,0:T(8,128)(2,1)}) custom-call(bf16[512,1024]{1,0:T(8,128)(2,1)} %fusion.40.q_ref, bf16[1024,2048]{1,0:T(8,128)(2,1)} %fusion.2.k_ref.v_ref, bf16[1024,2048]{1,0:T(8,128)(2,1)} %fusion.2.k_ref.v_ref, bf16[512,1024]{1,0:T(8,128)(2,1)} %fusion.43.do_ref, ...), custom_call_target="tpu_custom_call" | custom-call | flops 1 | bytes 1 | tf_op jit(solution)/shard_map/attend_back/pallas_call | solution.py:166
  372.0 4.8 all-to-all-start.1
  376.8 16.9 %weight_grads.2 = bf16[1024,5120]{1,0:T(8,128)(2,1)} custom-call(bf16[512,1024]{1,0:T(8,128)(2,1)} %bitcast.111, bf16[512,1024]{1,0:T(8,128)(2,1)} %copy-done.17, bf16[1024,1024]{1,0:T(8,128)(2,1)} %copy-done.9, bf16[512,1024]{1,0:T(8,128)(2,1)} %get-tuple-element.230.o_ref.refs_3_, bf16[512,1024]{1,0:T(8,128)(2,1)} %copy-done.15, ...), custom_call_target="tpu_custom_call" | custom-call | flops 1 | bytes 1 | tf_op jit(solution)/shard_map/weight_grads/pallas_call | solution.py:403
  393.7 5.3 fusion.14
  399.0 5.2 add_convert_fusion
  410.1 4.7 collective-permute-start.24
  420.6 25.2 %attend_back.4 = (bf16[2048,128]{1,0:T(8,128)(2,1)}, bf16[2048,128]{1,0:T(8,128)(2,1)}, bf16[2048,128]{1,0:T(8,128)(2,1)}) custom-call(bf16[2048,768]{1,0:T(8,128)(2,1)} %convolution_convert_fusion.2.q_ref.k_ref.v_ref, bf16[2048,768]{1,0:T(8,128)(2,1)} %convolution_convert_fusion.2.q_ref.k_ref.v_ref, ...), custom_call_target="tpu_custom_call" | custom-call | flops 1 | bytes 1 | tf_op jit(solution)/shard_map/attend_back/pallas_call | solution.py:166
  445.8 5.8 reduce-scatter.7.cloned.1.call-done
  467.2 26.3 %attend_back.5 = (bf16[2048,128]{1,0:T(8,128)(2,1)}, bf16[2048,128]{1,0:T(8,128)(2,1)}, bf16[2048,128]{1,0:T(8,128)(2,1)}) custom-call(bf16[2048,768]{1,0:T(8,128)(2,1)} %convolution_convert_fusion.2.q_ref.k_ref.v_ref, bf16[2048,768]{1,0:T(8,128)(2,1)} %convolution_convert_fusion.2.q_ref.k_ref.v_ref, ...), custom_call_target="tpu_custom_call" | custom-call | flops 1 | bytes 1 | tf_op jit(solution)/shard_map/attend_back/pallas_call | solution.py:166
  498.1 5.5 collective-permute-start.34
  506.0 13.4 %modulate_back.1 = (bf16[2048,1024]{1,0:T(8,128)(2,1)}, f32[4,2048]{1,0:T(4,128)}) custom-call(bf16[2048,256]{1,0:T(8,128)(2,1)} %copy-done.12, bf16[2048,256]{1,0:T(8,128)(2,1)} %copy-done.11, bf16[2048,256]{1,0:T(8,128)(2,1)} %copy-done.10, bf16[1024,768]{1,0:T(8,128)(2,1)} %slice.106.w_ref, bf16[2048,1024]{1,0:T(8,128)(2,1)} %get-tuple-element.276.x_ref, ...), custom_call_target="tpu_custom_call" | custom-call | flops 1 | bytes 1 | tf_op jit(solution)/shard_map/modulate_back/pallas_call | solution.py:352
  528.5 9.4 %weight_grads.3 = bf16[1024,768]{1,0:T(8,128)(2,1)} custom-call(bf16[2048,1024]{1,0:T(8,128)(2,1)} %get-tuple-element.202.refs_0_, bf16[2048,256]{1,0:T(8,128)(2,1)} %copy-done.12, bf16[2048,256]{1,0:T(8,128)(2,1)} %copy-done.11, bf16[2048,256]{1,0:T(8,128)(2,1)} %copy-done.10), custom_call_target="tpu_custom_call" | custom-call | flops 1 | bytes 1 | tf_op jit(solution)/shard_map/weight_grads/pallas_call | solution.py:403
  552.5 11.5 %collective-permute-done.38 = bf16[32,5120]{1,0:T(8,128)(2,1)} collective-permute-done((bf16[32,5120]{1,0:T(8,128)(2,1)}, bf16[32,5120]{1,0:T(8,128)(2,1)}, u32[]{:S(2)}, u32[]{:S(2)}) %collective-permute-start.38) | collective-permute-done | bytes 327712 | tf_op jit(solution)/shard_map/ppermute | solution.py:425
  564.0 6.8 %collective-permute-done.41 = bf16[32,5120]{1,0:T(8,128)(2,1)} collective-permute-done((bf16[32,5120]{1,0:T(8,128)(2,1)}, bf16[32,5120]{1,0:T(8,128)(2,1)}, u32[]{:S(2)}, u32[]{:S(2)}) %collective-permute-start.41) | collective-permute-done | bytes 327712 | tf_op jit(solution)/shard_map/ppermute | solution.py:425
  576.4 9.2 %add_convert_fusion.3 = bf16[512,1024]{1,0:T(8,128)(2,1)} fusion(f32[512,1024]{1,0:T(8,128)S(1)} %get-tuple-element.490, bf16[512,4096]{1,0:T(8,128)(2,1)S(1)} %copy-done.57, bf16[4096,1024]{1,0:T(8,128)(2,1)} %all-gather.11.cloned.1.call-done.w_ref, f32[1024]{0:T(1024)S(1)} %reshape.282), kind=kOutput, calls=%fused_computation.24 | convolution fusion | flops 4296540160 | bytes 15732736 | tf_op jit(solution)/shard_map/dot_general | solution.py:24
  594.7 11.5 %collective-permute-start.43 = (bf16[512,1024]{1,0:T(8,128)(2,1)S(1)}, bf16[512,1024]{1,0:T(8,128)(2,1)}, u32[]{:S(2)}, u32[]{:S(2)}) collective-permute-start(bf16[512,1024]{1,0:T(8,128)(2,1)S(1)} %get-tuple-element.416), channel_id=1, source_target_pairs={{0,1},{1,2},{2,3},{4,5},{5,6},{6,7},{8,9},{9,10},{10,11},{12,13},{... | collective-permute-start | bytes 3145736 | tf_op jit(solution)/shard_map/ppermute | solution.py:486
  607.6 17.6 %collective-permute-done.44 = bf16[512,1024]{1,0:T(8,128)(2,1)S(1)} collective-permute-done((bf16[512,1024]{1,0:T(8,128)(2,1)S(1)}, bf16[512,1024]{1,0:T(8,128)(2,1)S(1)}, u32[]{:S(2)}, u32[]{:S(2)}) %collective-permute-start.44) | collective-permute-done | bytes 1048608 | tf_op jit(solution)/shard_map/ppermute | solution.py:487
  (355 shorter events, 216.7 us)
Async XLA Ops:
  7.2 120.6 %all-gather.5.cloned.1.call-start = ((), (), s32[]{:S(2)}) async-start(), calls=%async_computation.6 | async-start | bytes 2064384 | tf_op jit(solution)/shard_map/all_gather | solution.py:551
  7.2 34.4 %collective-permute-start.1 = (bf16[512,1024]{1,0:T(8,128)(2,1)}, bf16[512,1024]{1,0:T(8,128)(2,1)S(1)}, u32[]{:S(2)}, u32[]{:S(2)}) collective-permute-start(bf16[512,1024]{1,0:T(8,128)(2,1)} %refs_0_.1), channel_id=1, source_target_pairs={{1,0},{2,1},{3,2},{5,4},{6,5},{7,6},{9,8},{10,9},{11,10},{13,12},{... | collective-permute-start | bytes 3145736 | tf_op jit(solution)/shard_map/ppermute | solution.py:497
  8.5 33.1 %collective-permute-start = (bf16[512,1024]{1,0:T(8,128)(2,1)}, bf16[512,1024]{1,0:T(8,128)(2,1)S(1)}, u32[]{:S(2)}, u32[]{:S(2)}) collective-permute-start(bf16[512,1024]{1,0:T(8,128)(2,1)} %refs_0_.1), channel_id=1, source_target_pairs={{0,1},{1,2},{2,3},{4,5},{5,6},{6,7},{8,9},{9,10},{10,11},{12,13},{... | collective-permute-start | bytes 3145736 | tf_op jit(solution)/shard_map/ppermute | solution.py:496
  42.3 43.8 %collective-permute-start.5 = (bf16[512,1024]{1,0:T(8,128)(2,1)S(1)}, bf16[512,1024]{1,0:T(8,128)(2,1)S(1)}, u32[]{:S(2)}, u32[]{:S(2)}) collective-permute-start(bf16[512,1024]{1,0:T(8,128)(2,1)S(1)} %collective-permute-done.refs_1_), channel_id=1, source_target_pairs={{0,1},{1,2},{2,3},{4,5},{5,6},{6,7},{8,9},{9,10},{10,11},{12,13},{... | collective-permute-start | bytes 3145736 | tf_op jit(solution)/shard_map/ppermute | solution.py:496
  46.0 40.1 %collective-permute-start.6 = (bf16[512,1024]{1,0:T(8,128)(2,1)S(1)}, bf16[512,1024]{1,0:T(8,128)(2,1)}, u32[]{:S(2)}, u32[]{:S(2)}) collective-permute-start(bf16[512,1024]{1,0:T(8,128)(2,1)S(1)} %collective-permute-done.1.refs_4_), channel_id=1, source_target_pairs={{1,0},{2,1},{3,2},{5,4},{6,5},{7,6},{9,8},{10,9},{11,10},{13,12},{... | collective-permute-start | bytes 3145736 | tf_op jit(solution)/shard_map/ppermute | solution.py:497
  50.7 161.3 %all-gather.7.cloned.1.call-start = ((), (), s32[]{:S(2)}) async-start(), calls=%async_computation.7 | async-start | bytes 11796480 | tf_op jit(solution)/shard_map/all_gather | solution.py:529
  51.6 34.4 %collective-permute-start.7 = (bf16[32,5120]{1,0:T(8,128)(2,1)S(1)}, bf16[32,5120]{1,0:T(8,128)(2,1)S(1)}, u32[]{:S(2)}, u32[]{:S(2)}) collective-permute-start(bf16[32,5120]{1,0:T(8,128)(2,1)S(1)} %constant_dynamic-update-slice_fusion), channel_id=1, source_target_pairs={{0,2},{1,3},{2,0},{3,1},{4,6},{5,7},{6,4},{7,5},{8,10},{9,11},{10,... | collective-permute-start | bytes 983048 | tf_op jit(solution)/shard_map/ppermute | solution.py:425
  86.0 39.4 %collective-permute-start.8 = (bf16[512,1024]{1,0:T(8,128)(2,1)S(1)}, bf16[512,1024]{1,0:T(8,128)(2,1)S(1)}, u32[]{:S(2)}, u32[]{:S(2)}) collective-permute-start(bf16[512,1024]{1,0:T(8,128)(2,1)S(1)} %collective-permute-done.5.refs_2_), channel_id=1, source_target_pairs={{0,1},{1,2},{2,3},{4,5},{5,6},{6,7},{8,9},{9,10},{10,11},{12,13},{... | collective-permute-start | bytes 3145736 | tf_op jit(solution)/shard_map/ppermute | solution.py:496
  87.4 39.0 %collective-permute-start.9 = (bf16[512,1024]{1,0:T(8,128)(2,1)}, bf16[512,1024]{1,0:T(8,128)(2,1)}, u32[]{:S(2)}, u32[]{:S(2)}) collective-permute-start(bf16[512,1024]{1,0:T(8,128)(2,1)} %collective-permute-done.6.refs_5_), channel_id=1, source_target_pairs={{1,0},{2,1},{3,2},{5,4},{6,5},{7,6},{9,8},{10,9},{11,10},{13,12},{... | collective-permute-start | bytes 3145736 | tf_op jit(solution)/shard_map/ppermute | solution.py:497
  88.7 33.2 %collective-permute-start.10 = (bf16[32,5120]{1,0:T(8,128)(2,1)S(1)}, bf16[32,5120]{1,0:T(8,128)(2,1)S(1)}, u32[]{:S(2)}, u32[]{:S(2)}) collective-permute-start(bf16[32,5120]{1,0:T(8,128)(2,1)S(1)} %constant_dynamic-update-slice_fusion), channel_id=1, source_target_pairs={{0,1},{1,0},{2,3},{3,2},{4,5},{5,4},{6,7},{7,6},{8,9},{9,8},{10,11... | collective-permute-start | bytes 983048 | tf_op jit(solution)/shard_map/ppermute | solution.py:425
  91.4 34.0 %collective-permute-start.11 = (bf16[32,5120]{1,0:T(8,128)(2,1)S(1)}, bf16[32,5120]{1,0:T(8,128)(2,1)S(1)}, u32[]{:S(2)}, u32[]{:S(2)}) collective-permute-start(bf16[32,5120]{1,0:T(8,128)(2,1)S(1)} %collective-permute-done.7), channel_id=1, source_target_pairs={{0,1},{1,0},{2,3},{3,2},{4,5},{5,4},{6,7},{7,6},{8,9},{9,8},{10,11... | collective-permute-start | bytes 983048 | tf_op jit(solution)/shard_map/ppermute | solution.py:425
  127.8 142.1 %all-gather.9.cloned.1.call-start = ((), (), s32[]{:S(2)}) async-start(), calls=%async_computation.8 | async-start | bytes 9437184 | tf_op jit(solution)/shard_map/all_gather | solution.py:529
  173.5 38.4 %collective-permute-start.21 = (bf16[128,1024]{1,0:T(8,128)(2,1)S(1)}, bf16[128,1024]{1,0:T(8,128)(2,1)S(1)}, u32[]{:S(2)}, u32[]{:S(2)}) collective-permute-start(bf16[128,1024]{1,0:T(8,128)(2,1)S(1)} %copy-done.44), channel_id=1, source_target_pairs={{0,2},{1,3},{2,0},{3,1},{4,6},{5,7},{6,4},{7,5},{8,10},{9,11},{10,... | collective-permute-start | bytes 786440 | tf_op jit(solution)/shard_map/ppermute | solution.py:425
  175.0 36.9 %collective-permute-start.19 = (bf16[256,1024]{1,0:T(8,128)(2,1)S(1)}, bf16[256,1024]{1,0:T(8,128)(2,1)S(1)}, u32[]{:S(2)}, u32[]{:S(2)}) collective-permute-start(bf16[256,1024]{1,0:T(8,128)(2,1)S(1)} %collective-permute-done.17), channel_id=1, source_target_pairs={{0,1},{1,2},{2,3},{4,5},{5,6},{6,7},{8,9},{9,10},{10,11},{12,13},{... | collective-permute-start | bytes 1572872 | tf_op jit(solution)/shard_map/ppermute | solution.py:496
  179.4 32.5 %collective-permute-start.20 = (bf16[256,1024]{1,0:T(8,128)(2,1)}, bf16[256,1024]{1,0:T(8,128)(2,1)S(1)}, u32[]{:S(2)}, u32[]{:S(2)}) collective-permute-start(bf16[256,1024]{1,0:T(8,128)(2,1)} %collective-permute-done.18), channel_id=1, source_target_pairs={{1,0},{2,1},{3,2},{5,4},{6,5},{7,6},{9,8},{10,9},{11,10},{13,12},{... | collective-permute-start | bytes 1572872 | tf_op jit(solution)/shard_map/ppermute | solution.py:497
  216.5 85.4 %all-gather.11.cloned.1.call-start = ((), (), s32[]{:S(2)}) async-start(), calls=%async_computation.9 | async-start | bytes 9437184 | tf_op jit(solution)/shard_map/all_gather | solution.py:529
  244.9 159.4 %reduce-scatter.5.cloned.1.call-start = ((), (), s32[]{:S(2)}) async-start(), calls=%async_computation.10 | async-start | bytes 9437184 | tf_op jit(solution)/shard_map/reduce_scatter | solution.py:516
  301.9 149.6 %reduce-scatter.7.cloned.1.call-start = ((), (), s32[]{:S(2)}) async-start(), calls=%async_computation.11 | async-start | bytes 9437184 | tf_op jit(solution)/shard_map/reduce_scatter | solution.py:516
  372.0 32.2 %all-to-all-start.1 = ((bf16[512,4,256]{2,0,1:T(8,128)(2,1)}), bf16[512,4,256]{2,0,1:T(8,128)(2,1)}, u32[]{:S(2)}, u32[]{:S(2)}) async-start(bf16[512,4,256]{2,0,1:T(8,128)(2,1)} %bitcast.113), calls=%async_computation.1 | async-start | bytes 2097152 | tf_op jit(solution)/shard_map/all_to_all | solution.py:664
  376.8 168.9 %reduce-scatter.9.cloned.1.call-start = ((), (), s32[]{:S(2)}) async-start(), calls=%async_computation.12 | async-start | bytes 11796480 | tf_op jit(solution)/shard_map/reduce_scatter | solution.py:516
  404.3 222.0 %reduce-scatter.11.cloned.1.call-start = ((), (), s32[]{:S(2)}) async-start(), calls=%async_computation.13 | async-start | bytes 2064384 | tf_op jit(solution)/shard_map/reduce_scatter | solution.py:516
  408.7 42.9 %collective-permute-start.25 = (bf16[256,1024]{1,0:T(8,128)(2,1)}, bf16[256,1024]{1,0:T(8,128)(2,1)}, u32[]{:S(2)}, u32[]{:S(2)}) collective-permute-start(bf16[256,1024]{1,0:T(8,128)(2,1)} %get-tuple-element.425), channel_id=1, source_target_pairs={{3,2},{7,6},{11,10},{15,14},{19,18},{23,22},{27,26},{31,30}} | collective-permute-start | bytes 1572872 | tf_op jit(solution)/shard_map/ppermute | solution.py:487
  410.1 41.4 %collective-permute-start.24 = (bf16[256,1024]{1,0:T(8,128)(2,1)}, bf16[256,1024]{1,0:T(8,128)(2,1)}, u32[]{:S(2)}, u32[]{:S(2)}) collective-permute-start(bf16[256,1024]{1,0:T(8,128)(2,1)} %get-tuple-element.426), channel_id=1, source_target_pairs={{0,1},{4,5},{8,9},{12,13},{16,17},{20,21},{24,25},{28,29}} | collective-permute-start | bytes 1572872 | tf_op jit(solution)/shard_map/ppermute | solution.py:486
  416.2 45.0 %collective-permute-start.30 = (bf16[128,1024]{1,0:T(8,128)(2,1)}, bf16[128,1024]{1,0:T(8,128)(2,1)}, u32[]{:S(2)}, u32[]{:S(2)}) collective-permute-start(bf16[128,1024]{1,0:T(8,128)(2,1)} %get-tuple-element.439), channel_id=1, source_target_pairs={{0,3},{1,2},{2,1},{3,0},{4,7},{5,6},{6,5},{7,4},{8,11},{9,10},{10,... | collective-permute-start | bytes 786440 | tf_op jit(solution)/shard_map/ppermute | solution.py:425
  418.5 45.2 %collective-permute-start.29 = (bf16[128,1024]{1,0:T(8,128)(2,1)}, bf16[128,1024]{1,0:T(8,128)(2,1)}, u32[]{:S(2)}, u32[]{:S(2)}) collective-permute-start(bf16[128,1024]{1,0:T(8,128)(2,1)} %get-tuple-element.440), channel_id=1, source_target_pairs={{0,2},{1,3},{2,0},{3,1},{4,6},{5,7},{6,4},{7,5},{8,10},{9,11},{10,... | collective-permute-start | bytes 786440 | tf_op jit(solution)/shard_map/ppermute | solution.py:425
  418.5 46.0 %collective-permute-start.28 = (bf16[128,1024]{1,0:T(8,128)(2,1)S(1)}, bf16[128,1024]{1,0:T(8,128)(2,1)}, u32[]{:S(2)}, u32[]{:S(2)}) collective-permute-start(bf16[128,1024]{1,0:T(8,128)(2,1)S(1)} %get-tuple-element.441), channel_id=1, source_target_pairs={{0,1},{1,0},{2,3},{3,2},{4,5},{5,4},{6,7},{7,6},{8,9},{9,8},{10,11... | collective-permute-start | bytes 786440 | tf_op jit(solution)/shard_map/ppermute | solution.py:425
  454.7 39.3 %collective-permute-start.27 = (bf16[256,1024]{1,0:T(8,128)(2,1)}, bf16[256,1024]{1,0:T(8,128)(2,1)}, u32[]{:S(2)}, u32[]{:S(2)}) collective-permute-start(bf16[256,1024]{1,0:T(8,128)(2,1)} %get-tuple-element.423), channel_id=1, source_target_pairs={{3,2},{2,1},{7,6},{6,5},{11,10},{10,9},{15,14},{14,13},{19,18},{18... | collective-permute-start | bytes 1572872 | tf_op jit(solution)/shard_map/ppermute | solution.py:487
  456.1 37.8 %collective-permute-start.26 = (bf16[256,1024]{1,0:T(8,128)(2,1)}, bf16[256,1024]{1,0:T(8,128)(2,1)}, u32[]{:S(2)}, u32[]{:S(2)}) collective-permute-start(bf16[256,1024]{1,0:T(8,128)(2,1)} %get-tuple-element.424), channel_id=1, source_target_pairs={{0,1},{1,2},{4,5},{5,6},{8,9},{9,10},{12,13},{13,14},{16,17},{17,1... | collective-permute-start | bytes 1572872 | tf_op jit(solution)/shard_map/ppermute | solution.py:486
  461.2 32.3 %collective-permute-start.33 = (bf16[32,4096]{1,0:T(8,128)(2,1)}, bf16[32,4096]{1,0:T(8,128)(2,1)}, u32[]{:S(2)}, u32[]{:S(2)}) collective-permute-start(bf16[32,4096]{1,0:T(8,128)(2,1)} %get-tuple-element.435), channel_id=1, source_target_pairs={{0,3},{1,2},{2,1},{3,0},{4,7},{5,6},{6,5},{7,4},{8,11},{9,10},{10,... | collective-permute-start | bytes 786440 | tf_op jit(solution)/shard_map/ppermute | solution.py:425
  551.4 40.9 %collective-permute-start.42 = (bf16[32,5120]{1,0:T(8,128)(2,1)}, bf16[32,5120]{1,0:T(8,128)(2,1)}, u32[]{:S(2)}, u32[]{:S(2)}) collective-permute-start(bf16[32,5120]{1,0:T(8,128)(2,1)} %get-tuple-element.427), channel_id=1, source_target_pairs={{0,3},{1,2},{2,1},{3,0},{4,7},{5,6},{6,5},{7,4},{8,11},{9,10},{10,... | collective-permute-start | bytes 983048 | tf_op jit(solution)/shard_map/ppermute | solution.py:425
  593.4 31.8 %collective-permute-start.44 = (bf16[512,1024]{1,0:T(8,128)(2,1)S(1)}, bf16[512,1024]{1,0:T(8,128)(2,1)S(1)}, u32[]{:S(2)}, u32[]{:S(2)}) collective-permute-start(bf16[512,1024]{1,0:T(8,128)(2,1)S(1)} %get-tuple-element.415), channel_id=1, source_target_pairs={{3,2},{2,1},{1,0},{7,6},{6,5},{5,4},{11,10},{10,9},{9,8},{15,14},{... | collective-permute-start | bytes 3145736 | tf_op jit(solution)/shard_map/ppermute | solution.py:487
  594.7 31.6 %collective-permute-start.43 = (bf16[512,1024]{1,0:T(8,128)(2,1)S(1)}, bf16[512,1024]{1,0:T(8,128)(2,1)}, u32[]{:S(2)}, u32[]{:S(2)}) collective-permute-start(bf16[512,1024]{1,0:T(8,128)(2,1)S(1)} %get-tuple-element.416), channel_id=1, source_target_pairs={{0,1},{1,2},{2,3},{4,5},{5,6},{6,7},{8,9},{9,10},{10,11},{12,13},{... | collective-permute-start | bytes 3145736 | tf_op jit(solution)/shard_map/ppermute | solution.py:486
  (84 other events, 1224.5 us)
Sparse Core Ops, SparseCore 0:
  50.8 30.8 all-gather.4
  127.9 61.4 all-gather.6
  191.3 54.4 all-gather.8
  247.5 54.3 all-gather.10
  305.2 71.2 reduce-scatter.4
  380.2 71.2 reduce-scatter.6
  455.1 81.5 reduce-scatter.8
  570.9 39.2 reduce-scatter.10
